TPU v7x, 512 devices: a whole 4x8x8 slice. The times are simulated.
512 devices in a mesh: spec: 8 (over y_hi, core), frow: 8 (over y_lo, x), fcol: 8 (over z).
Axes of the slice: x: 4, y: 8 (y_hi: 4, y_lo: 2; y = y_hi * 2 + y_lo), z: 8, core: 2. Of those that a mesh axis runs over, the one named last changes fastest.
Arguments:
- primal_slab: float32 [96, 16, 8, 8, 1024], P('spec', None, 'frow', 'fcol'), may hold values from -8 to 8
- wave_dual: float32 [96, 1024, 1024], P('spec', 'frow', 'fcol'), may hold values from -3 to 3
- nuc_dual: float32 [96, 1024, 1024], P('spec', 'frow', 'fcol'), may hold values from -3 to 3
- l21_weights: float32 [2, 1024, 1024], P(None, 'frow', 'fcol'), may hold values from 2.078461 to 20.784609
- nuc_thresh: float32 [8, 8, 8], P('frow', 'fcol'), may hold values from 32 to 320
- basis: float32 [8, 8, 96, 8], P('frow', 'fcol', 'spec'), may hold values from -0.625 to 0.625
- band_of: int32 [8, 8, 96], P('frow', 'fcol', 'spec'), may hold values from 0 to 1
- margin_width: int32 [8, 8, 2], P('frow', 'fcol'), may hold values from 10 to 21
Outputs:
- wave_new: float32 [96, 1024, 1024], P('spec', 'frow', 'fcol')
- nuc_new: float32 [96, 1024, 1024], P('spec', 'frow', 'fcol')
All inputs are finite; a program needn't handle non-finite values.
Results may differ from a plain program's by a relative error of at most 0.0003.
Values sent between devices are 32-bit elements; how exact they have to be, the bound alone decides.
No kernel may reach another device: no remote copies, remote signals or barrier semaphores. Data moves between devices by JAX's collectives and lax.ppermute only.
A program may use at most 128 MiB of HBM per device.

v0:
```python
import jax
import jax.numpy as jnp
from jax import lax
from jax.sharding import PartitionSpec as P

HALO = 21


low_taps = [
    -0.00011747678400228192,
    0.0006754494059985568,
    -0.0003917403729959771,
    -0.00487035299301066,
    0.008746094047015655,
    0.013981027917015516,
    -0.04408825393106472,
    -0.01736930100202211,
    0.128747426620186,
    0.00047248457399797254,
    -0.2840155429624281,
    -0.015829105256023893,
    0.5853546836548691,
    0.6756307362980128,
    0.3128715909144659,
    0.05441584224308161,
]
tap_lag = 7
highest = lax.Precision.HIGHEST


def with_halo(shard, sides, width):
    for axis, dim in sides:
        count, length = (lax.axis_size(axis), shard.shape[dim])
        up = [(i, (i + 1) % count) for i in range(count - 1)]
        down = [(j, i) for i, j in up]
        last = lax.slice_in_dim(shard, length - width, length, axis=dim)
        initial = lax.slice_in_dim(shard, 0, width, axis=dim)
        before = lax.ppermute(last, axis, up)
        after = lax.ppermute(initial, axis, down)
        shard = jnp.concatenate([before, shard, after], axis=dim)
    return shard


def high_taps():
    return [(-1.0) ** place * low_taps[15 - place] for place in range(16)]


def filter_matrix(in_length, filter_taps, out_first, out_count):
    outputs = jnp.arange(out_count, dtype=jnp.int32)[:, None]
    inputs = jnp.arange(in_length, dtype=jnp.int32)[None, :]
    offset = inputs - 2 * (outputs + out_first)
    matches = (offset[:, :, None] == jnp.arange(16, dtype=jnp.int32)[None, None, :]).astype(
        jnp.float32
    )
    return jnp.einsum(
        "jnt,t->jn", matches, jnp.asarray(filter_taps, jnp.float32), precision=highest
    )


def paired_matrix(in_length, low_count, high_first, high_count):
    low_part = filter_matrix(in_length, low_taps, 0, low_count)
    high_part = filter_matrix(in_length, high_taps(), high_first, high_count)
    return jnp.concatenate([low_part, high_part], axis=0)


def analyse(extended, facet_rows, facet_cols):
    low_rows = facet_rows // 2 + 14
    low_cols = facet_cols // 2 + 14
    vertical = paired_matrix(extended.shape[1], low_rows, tap_lag, facet_rows // 2)
    across = paired_matrix(extended.shape[2], low_cols, tap_lag, facet_cols // 2)
    level_one = jnp.einsum("jn,cnk->cjk", vertical, extended, precision=highest)
    level_one = jnp.einsum("cjk,mk->cjm", level_one, across, precision=highest)
    coarse_in = level_one[:, :low_rows, :low_cols]
    upper_right = level_one[:, tap_lag : tap_lag + facet_rows // 2, low_cols:]
    lower_left = level_one[:, low_rows:, tap_lag : tap_lag + facet_cols // 2]
    lower_right = level_one[:, low_rows:, low_cols:]
    vertical_two = paired_matrix(low_rows, facet_rows // 4, 0, facet_rows // 4)
    across_two = paired_matrix(low_cols, facet_cols // 4, 0, facet_cols // 4)
    coarse = jnp.einsum("jn,cnk->cjk", vertical_two, coarse_in, precision=highest)
    coarse = jnp.einsum("cjk,mk->cjm", coarse, across_two, precision=highest)
    upper_half = jnp.concatenate([coarse, upper_right], axis=2)
    lower_half = jnp.concatenate([lower_left, lower_right], axis=2)
    return jnp.concatenate([upper_half, lower_half], axis=1)


def window_mask(widths, facet_rows, facet_cols):
    row_pos = jnp.arange(facet_rows + 2 * HALO, dtype=jnp.int32)
    col_pos = jnp.arange(facet_cols + 2 * HALO, dtype=jnp.int32)
    row_in = (row_pos >= HALO - widths[0]) & (row_pos < HALO + facet_rows + widths[0])
    col_in = (col_pos >= HALO - widths[1]) & (col_pos < HALO + facet_cols + widths[1])
    return row_in[:, None] & col_in[None, :]


def shrink_spectrum(combined, spectrum, local_basis, thresholds):
    singular = jnp.sqrt(jnp.sum(spectrum * spectrum, axis=(1, 2)))
    retained = thresholds / jnp.maximum(singular, thresholds)
    scaled = spectrum * (1.0 - retained)[:, None, None]
    return combined - jnp.einsum("cr,rij->cij", local_basis, scaled, precision=highest)


def shards(primal_slab, wave_dual, nuc_dual, l21_weights, nuc_thresh, basis, band_of, margin_width):
    channels = wave_dual.shape[0]
    facet_rows = wave_dual.shape[1]
    facet_cols = wave_dual.shape[2]
    arrived = lax.all_to_all(
        lax.all_to_all(primal_slab, "frow", split_axis=1, concat_axis=2, tiled=True),
        "fcol",
        split_axis=4,
        concat_axis=3,
        tiled=True,
    )
    facet_block = arrived.reshape(channels, facet_rows, facet_cols)
    margin_ready = with_halo(facet_block, (("frow", 1), ("fcol", 2)), HALO)
    local_basis = basis[0, 0]
    thresholds = nuc_thresh[0, 0]
    combined = nuc_dual + facet_block
    spectrum_part = jnp.einsum("cr,cij->rij", local_basis, combined, precision=highest)
    spectrum = lax.psum(spectrum_part, "spec")
    nuc_new = shrink_spectrum(combined, spectrum, local_basis, thresholds)
    inside = window_mask(margin_width[0, 0], facet_rows, facet_cols)
    extended = jnp.where(inside[None], margin_ready, 0.0)
    dual_sum = wave_dual + analyse(extended, facet_rows, facet_cols)
    bands = l21_weights.shape[0]
    onehot = (band_of[0, 0][None, :] == jnp.arange(bands, dtype=jnp.int32)[:, None]).astype(
        jnp.float32
    )
    band_part = jnp.einsum("bc,cij->bij", onehot, dual_sum * dual_sum, precision=highest)
    band_sq = lax.psum(band_part, "spec")
    shrink_ratio = l21_weights / jnp.maximum(jnp.sqrt(band_sq), l21_weights)
    wave_new = dual_sum * jnp.einsum("bc,bij->cij", onehot, shrink_ratio, precision=highest)
    return (wave_new, nuc_new)


def solution(mesh):
    return jax.shard_map(
        shards,
        mesh=mesh,
        in_specs=(
            P("spec", None, "frow", "fcol", None),
            P("spec", "frow", "fcol"),
            P("spec", "frow", "fcol"),
            P(None, "frow", "fcol"),
            P("frow", "fcol", None),
            P("frow", "fcol", "spec", None),
            P("frow", "fcol", "spec"),
            P("frow", "fcol", None),
        ),
        out_specs=(P("spec", "frow", "fcol"), P("spec", "frow", "fcol")),
        check_vma=False,
    )
```

profile of v0, /device:TPU:1, one launch (start us, length us, event | category | flops | bytes accessed | tf_op | source)
XLA Modules:
  0.0 233.8 jit_solution(15922698853513053076)
XLA Ops:
  7.2 2.8 %copy.102 = f32[12,16,1,1,1024]{4,3,2,0,1:T(1,128)} copy(f32[12,16,1,1,1024]{4,3,2,1,0:T(1,128)} %param.16) | data formatting | bytes 1572864 | tf_op args[0]
  10.1 5.9 %all-to-all-start = ((f32[12,16,1,1,1024]{4,3,2,0,1:T(1,128)}), f32[12,16,1,1,1024]{4,3,2,0,1:T(1,128)S(1)}, u32[]{:S(2)}, u32[]{:S(2)}) async-start(f32[12,16,1,1,1024]{4,3,2,0,1:T(1,128)} %copy.102), calls=%async_computation | async-start | bytes 1572864 | tf_op jit(solution)/shard_map/all_to_all | solution.py:106
  17.1 7.2 %all-to-all-done = f32[12,16,1,1,1024]{4,3,2,0,1:T(1,128)S(1)} async-done(((f32[12,16,1,1,1024]{4,3,2,0,1:T(1,128)}), f32[12,16,1,1,1024]{4,3,2,0,1:T(1,128)S(1)}, u32[]{:S(2)}, u32[]{:S(2)}) %all-to-all-start) | async-done | bytes 786464 | tf_op jit(solution)/shard_map/all_to_all | solution.py:106
  25.0 5.8 %copy.121 = f32[12,2,8,1,1,1024]{0,2,1,5,4,3:T(8,128)} copy(f32[12,2,8,1,1,1024]{5,4,1,2,0,3:T(1,128)S(1)} %bitcast.72) | data formatting | bytes 1572864 | tf_op jit(solution)/shard_map/all_to_all | solution.py:106
  30.8 7.2 %bitcast_bitcast_fusion = f32[1024,2,1,8,12]{4,3,2,1,0:T(8,128)} fusion(f32[12,2,8,1,1,1024]{0,2,1,5,4,3:T(8,128)} %copy.121), kind=kLoop, calls=%fused_computation.75 | loop fusion | bytes 1572864
  37.9 10.6 %reshape.168 = f32[8,1,24576]{2,1,0:T(1,128)} reshape(f32[1024,2,1,8,12]{4,3,2,1,0:T(8,128)} %bitcast_bitcast_fusion) | data formatting | bytes 1572864
  48.5 13.2 %all-to-all-start.1 = ((f32[8,1,24576]{2,1,0:T(1,128)}), f32[8,1,24576]{2,1,0:T(1,128)S(1)}, u32[]{:S(2)}, u32[]{:S(2)}) async-start(f32[8,1,24576]{2,1,0:T(1,128)} %reshape.168), calls=%async_computation.1 | async-start | bytes 1572864 | tf_op jit(solution)/shard_map/all_to_all | solution.py:105
  65.2 2.3 fusion.12
  68.2 15.9 %all-to-all-done.1 = f32[8,1,24576]{2,1,0:T(1,128)S(1)} async-done(((f32[8,1,24576]{2,1,0:T(1,128)}), f32[8,1,24576]{2,1,0:T(1,128)S(1)}, u32[]{:S(2)}, u32[]{:S(2)}) %all-to-all-start.1) | async-done | bytes 786464 | tf_op jit(solution)/shard_map/all_to_all | solution.py:105
  84.6 2.6 %reduce = f32[8,24576]{1,0:T(8,128)S(1)} reduce(f32[8,1,24576]{2,1,0:T(1,128)S(1)} %all-to-all-done.1, f32[]{:T(128)} %broadcast.122), dimensions={1}, to_apply=%all_to_all.24.reduce_sub_computation | reduce | bytes 1572868 | tf_op jit(solution)/shard_map/all_to_all | solution.py:105
  87.2 12.5 %reshape.169 = f32[1024,2,1,8,12]{4,3,2,1,0:T(8,128)} reshape(f32[8,24576]{1,0:T(8,128)S(1)} %reduce) | data formatting | bytes 1572864
  99.7 5.3 %copy.105 = f32[12,2,8,1,1024]{4,2,1,0,3:T(8,128)S(1)} copy(f32[12,2,8,1,1024]{0,2,3,1,4:T(8,128)} %bitcast.71) | data formatting | bytes 1572864 | tf_op jit(solution)/shard_map/all_to_all | solution.py:105
  106.4 4.0 %collective-permute-start = (f32[12,21,128]{2,1,0:T(8,128)S(1)}, f32[12,21,128]{2,1,0:T(8,128)S(1)}, u32[]{:S(2)}, u32[]{:S(2)}) collective-permute-start(f32[12,21,128]{2,1,0:T(8,128)S(1)} %get-tuple-element.25), channel_id=1, source_target_pairs={{0,8},{8,16},{16,24},{24,32},{32,40},{40,48},{48,56},{1,9},{9,17},... | collective-permute-start | bytes 387080 | tf_op jit(solution)/shard_map/ppermute | solution.py:38
  110.5 2.3 fusion.13
  112.9 1.4 fusion.44
  114.2 1.8 copy.107
  118.5 4.7 %collective-permute-start.2 = (f32[12,170,21]{1,2,0:T(8,128)}, f32[12,170,21]{1,2,0:T(8,128)}, u32[]{:S(2)}, u32[]{:S(2)}) collective-permute-start(f32[12,170,21]{1,2,0:T(8,128)} %copy.106), channel_id=1, source_target_pairs={{0,1},{1,2},{2,3},{3,4},{4,5},{5,6},{6,7},{8,9},{9,10},{10,11},{11... | collective-permute-start | bytes 514088 | tf_op jit(solution)/shard_map/ppermute | solution.py:38
  123.2 2.6 %convolution_bitcast_fusion.1 = f32[8,128,128]{2,0,1:T(8,128)} fusion(f32[12,128,128]{2,1,0:T(8,128)S(1)} %reshape.155, f32[12,128,128]{2,1,0:T(8,128)S(1)} %copy-done.1, f32[1,1,12,8]{2,3,1,0:T(8,128)S(1)} %copy-done), kind=kOutput, calls=%fused_computation.19 | convolution fusion | flops 19070976 | bytes 2097536 | tf_op jit(solution)/shard_map/cr,cij->rij/dot_general | solution.py:117
  126.5 2.4 %copy.108 = f32[12,170,21]{2,1,0:T(8,128)} copy(f32[12,170,21]{1,2,0:T(8,128)} %collective-permute-done.2) | data formatting | bytes 342720 | tf_op jit(solution)/shard_map/ppermute | solution.py:38
  128.8 3.8 %fusion = f32[12,170,142]{1,2,0:T(8,128)S(1)} fusion(f32[12,170,21]{2,1,0:T(8,128)S(1)} %copy.109, f32[12,21,128]{2,1,0:T(8,128)S(1)} %collective-permute-done.1, f32[12,128,128]{2,1,0:T(8,128)S(1)} %reshape.155, f32[12,21,128]{2,1,0:T(8,128)S(1)} %copy-done.6, f32[12,170,21]{2,1,0:T(8,128)} %copy.108, pred[170,170]{1,0:T(8,128)(4,1)S(1)} %copy-done.10, ...), kind=kOutput, calls=%fused_computation.1 | convolution fusion | flops 592705344 | bytes 2671380 | tf_op jit(solution)/shard_map/jn,cnk->cjk/dot_general | solution.py:71
  132.6 1.6 fusion.9
  138.1 82.5 %all-reduce.3.cloned.1.call-done = (f32[2,128,128]{2,1,0:T(8,128)}, f32[8,128,128]{2,0,1:T(8,128)}) async-done(((f32[2,128,128]{2,1,0:T(8,128)}, f32[8,128,128]{2,0,1:T(8,128)}), (f32[2,128,128]{2,1,0:T(8,128)}, f32[8,128,128]{2,0,1:T(8,128)})) %all-reduce.3.cloned.1.call-update) | async-done | bytes 655376 | tf_op jit(solution)/shard_map/psum | solution.py:128
  222.4 1.3 copy_multiply_fusion
  224.0 1.8 fusion.11
  (71 shorter events, 15.6 us)
Async XLA Ops:
  7.2 116.0 %copy-start = (f32[1,1,12,8]{2,3,1,0:T(8,128)S(1)}, f32[1,1,12,8]{2,3,1,0:T(8,128)}, u32[]{:S(2)}) copy-start(f32[1,1,12,8]{2,3,1,0:T(8,128)} %param.21) | copy-start | bytes 1156
  7.2 9.5 %copy-start.15 = (f32[16,1,1]{0,1,2:T(1,128)S(1)}, f32[16,1,1]{0,1,2:T(1,128)}, u32[]{:S(2)}) copy-start(f32[16,1,1]{0,1,2:T(1,128)} %constant.32) | copy-start | bytes 196
  7.2 8.7 %copy-start.12 = (s32[1,1,2]{2,1,0:T(1,128)S(1)}, s32[1,1,2]{2,1,0:T(1,128)}, u32[]{:S(2)}) copy-start(s32[1,1,2]{2,1,0:T(1,128)} %param.23) | copy-start | bytes 28
  10.1 14.2 %all-to-all-start = ((f32[12,16,1,1,1024]{4,3,2,0,1:T(1,128)}), f32[12,16,1,1,1024]{4,3,2,0,1:T(1,128)S(1)}, u32[]{:S(2)}, u32[]{:S(2)}) async-start(f32[12,16,1,1,1024]{4,3,2,0,1:T(1,128)} %copy.102), calls=%async_computation | async-start | bytes 1572864 | tf_op jit(solution)/shard_map/all_to_all | solution.py:106
  48.5 16.1 %copy-start.14 = (f32[16,1,1]{0,1,2:T(1,128)S(1)}, f32[16,1,1]{0,1,2:T(1,128)}, u32[]{:S(2)}) copy-start(f32[16,1,1]{0,1,2:T(1,128)} %constant.31) | copy-start | bytes 196
  48.5 35.6 %all-to-all-start.1 = ((f32[8,1,24576]{2,1,0:T(1,128)}), f32[8,1,24576]{2,1,0:T(1,128)S(1)}, u32[]{:S(2)}, u32[]{:S(2)}) async-start(f32[8,1,24576]{2,1,0:T(1,128)} %reshape.168), calls=%async_computation.1 | async-start | bytes 1572864 | tf_op jit(solution)/shard_map/all_to_all | solution.py:105
  61.7 159.0 %all-reduce.3.cloned.1.call-start = ((), (), s32[]{:S(2)}) async-start(), calls=%async_computation.2 | async-start | bytes 1310720 | tf_op jit(solution)/shard_map/psum | solution.py:128
  105.1 7.6 %collective-permute-start.1 = (f32[12,21,128]{2,1,0:T(8,128)S(1)}, f32[12,21,128]{2,1,0:T(8,128)S(1)}, u32[]{:S(2)}, u32[]{:S(2)}) collective-permute-start(f32[12,21,128]{2,1,0:T(8,128)S(1)} %get-tuple-element.26), channel_id=1, source_target_pairs={{8,0},{16,8},{24,16},{32,24},{40,32},{48,40},{56,48},{9,1},{17,9},... | collective-permute-start | bytes 387080 | tf_op jit(solution)/shard_map/ppermute | solution.py:39
  106.4 6.3 %collective-permute-start = (f32[12,21,128]{2,1,0:T(8,128)S(1)}, f32[12,21,128]{2,1,0:T(8,128)S(1)}, u32[]{:S(2)}, u32[]{:S(2)}) collective-permute-start(f32[12,21,128]{2,1,0:T(8,128)S(1)} %get-tuple-element.25), channel_id=1, source_target_pairs={{0,8},{8,16},{16,24},{24,32},{32,40},{40,48},{48,56},{1,9},{9,17},... | collective-permute-start | bytes 387080 | tf_op jit(solution)/shard_map/ppermute | solution.py:38
  112.8 1.5 copy-start.5
  114.2 9.0 %copy-start.1 = (f32[12,128,128]{2,1,0:T(8,128)S(1)}, f32[12,128,128]{2,1,0:T(8,128)}, u32[]{:S(2)}) copy-start(f32[12,128,128]{2,1,0:T(8,128)} %param.18) | copy-start | bytes 2359300
  116.0 9.8 %collective-permute-start.3 = (f32[12,170,21]{1,2,0:T(8,128)S(1)}, f32[12,170,21]{1,2,0:T(8,128)S(1)}, u32[]{:S(2)}, u32[]{:S(2)}) collective-permute-start(f32[12,170,21]{1,2,0:T(8,128)S(1)} %copy.107), channel_id=1, source_target_pairs={{1,0},{2,1},{3,2},{4,3},{5,4},{6,5},{7,6},{9,8},{10,9},{11,10},{12... | collective-permute-start | bytes 514088 | tf_op jit(solution)/shard_map/ppermute | solution.py:39
  118.5 7.9 %collective-permute-start.2 = (f32[12,170,21]{1,2,0:T(8,128)}, f32[12,170,21]{1,2,0:T(8,128)}, u32[]{:S(2)}, u32[]{:S(2)}) collective-permute-start(f32[12,170,21]{1,2,0:T(8,128)} %copy.106), channel_id=1, source_target_pairs={{0,1},{1,2},{2,3},{3,4},{4,5},{5,6},{6,7},{8,9},{9,10},{10,11},{11... | collective-permute-start | bytes 514088 | tf_op jit(solution)/shard_map/ppermute | solution.py:38
  125.8 3.0 %copy-start.6 = (f32[12,21,128]{2,1,0:T(8,128)S(1)}, f32[12,21,128]{2,1,0:T(8,128)}, u32[]{:S(2)}) copy-start(f32[12,21,128]{2,1,0:T(8,128)} %copy-done.5) | copy-start | bytes 387076
  125.8 3.0 %copy-start.10 = (pred[170,170]{1,0:T(8,128)(4,1)S(1)}, pred[170,170]{1,0:T(8,128)(4,1)}, u32[]{:S(2)}) copy-start(pred[170,170]{1,0:T(8,128)(4,1)} %broadcast_and_fusion) | copy-start | bytes 86704
  134.1 0.7 copy-start.8
  134.2 0.7 copy-start.9
  134.2 1.7 copy-start.2
  135.9 0.7 copy-start.11
  136.2 84.5 %copy-start.7 = (f32[2,128,128]{2,1,0:T(8,128)S(1)}, f32[2,128,128]{2,1,0:T(8,128)}, u32[]{:S(2)}) copy-start(f32[2,128,128]{2,1,0:T(8,128)} %param.19) | copy-start | bytes 393220
  220.7 1.7 copy-start.3
  222.4 1.3 copy-start.4
  222.4 1.6 copy-start.13
Sparse Core Ops, SparseCore 0:
  138.3 82.3 all-reduce.2
where the time goes:
time: 235 us; the launch traced here: 234 us
  waiting for transfers between devices  106 us (45%)
  local copies, waits for them, and re-layouts  56.2 us (24%)
  starting transfers between devices  30.6 us (13%)
  matrix products  17.8 us (8%)
  between operations  16.9 us (7%)
  other arithmetic  6.49 us (3%)
    psum x1, waiting for transfers between devices, shards(): band_sq = lax.psum(band_part, 'spec')  82.5 us
    unnamed x37, local copies, waits for them, and re-layouts  35 us
    all_to_all x1, waiting for transfers between devices, shards(): lax.all_to_all(lax.all_to_all(primal_slab, 'frow', split_axis=1, concat_a...  15.9 us
    all_to_all x1, starting transfers between devices, shards(): lax.all_to_all(lax.all_to_all(primal_slab, 'frow', split_axis=1, concat_a...  13.2 us
    ppermute x2, starting transfers between devices, with_halo(): before = lax.ppermute(last, axis, up)  8.69 us
    all_to_all x1, waiting for transfers between devices, shards(): lax.all_to_all(primal_slab, 'frow', split_axis=1, concat_axis=2, tiled=True)  7.17 us
    all_to_all x2, local copies, waits for them, and re-layouts, shards(): lax.all_to_all(primal_slab, 'frow', split_axis=1, concat_axis=2, tiled=True)  6.51 us
    all_to_all x1, starting transfers between devices, shards(): lax.all_to_all(primal_slab, 'frow', split_axis=1, concat_axis=2, tiled=True)  5.86 us
  transfers between devices with their start and end apart: 7, of which 4 were waited for; matrix products, arithmetic and copies ran while one was open for 5% of the time, Pallas kernels for 0%

commit v1 on v0

v1 whole, which is shorter than its diff:
```python
import functools

import jax
import jax.numpy as jnp
import numpy as np
from jax import lax
from jax.experimental import pallas as pl
from jax.experimental.pallas import tpu as pltpu
from jax.sharding import PartitionSpec as P

HALO = 21
EDGE = 24
SLOTS = 3
LANES = 128
FACET = 128
EXT = FACET + 2 * EDGE
VMEM = pl.BlockSpec(memory_space=pltpu.VMEM)
SMEM = pl.BlockSpec(memory_space=pltpu.SMEM)

low_taps = [
    -0.00011747678400228192,
    0.0006754494059985568,
    -0.0003917403729959771,
    -0.00487035299301066,
    0.008746094047015655,
    0.013981027917015516,
    -0.04408825393106472,
    -0.01736930100202211,
    0.128747426620186,
    0.00047248457399797254,
    -0.2840155429624281,
    -0.015829105256023893,
    0.5853546836548691,
    0.6756307362980128,
    0.3128715909144659,
    0.05441584224308161,
]
tap_lag = 7
high_taps = [(-1.0) ** place * low_taps[15 - place] for place in range(16)]


def filter_matrix(in_length, taps, first, count):
    matrix = np.zeros((count, in_length))
    for out in range(count):
        matrix[out, 2 * (out + first) : 2 * (out + first) + 16] = taps
    return matrix


@functools.cache
def operators():
    length = FACET + 2 * HALO
    half, quarter = FACET // 2, FACET // 4
    low_all = filter_matrix(length, low_taps, 0, half + 14)
    high = filter_matrix(length, high_taps, tap_lag, half)
    low = low_all[tap_lag : tap_lag + half]
    coarse = np.concatenate(
        [
            filter_matrix(half + 14, low_taps, 0, quarter) @ low_all,
            filter_matrix(half + 14, high_taps, 0, quarter) @ low_all,
        ]
    )
    return coarse, low, high


def row_operator():
    whole = np.concatenate(operators())
    placed = np.zeros((whole.shape[0], 2 * LANES), np.float32)
    placed[:, :FACET] = whole[:, HALO : HALO + FACET]
    placed[:, FACET + EDGE - HALO : FACET + EDGE] = whole[:, :HALO]
    placed[:, FACET + EDGE : FACET + EDGE + HALO] = whole[:, HALO + FACET :]
    return placed


def column_operators():
    coarse, low, high = operators()
    whole = np.concatenate([coarse, high, low, high]).T.astype(np.float32)
    sides = np.zeros((2, EDGE, 2 * LANES), np.float32)
    sides[0, :HALO] = whole[:HALO]
    sides[1, :HALO] = whole[HALO + FACET :]
    return whole[HALO : HALO + FACET], sides


def split(values):
    head = values.astype(jnp.bfloat16)
    return head, (values - head.astype(jnp.float32)).astype(jnp.bfloat16)


def pack_kernel(rows_ref, out_ref, *, chans, facet_rows, facet_cols, deal):
    block = deal * (chans + chans // SLOTS)
    per_chan = deal * facet_rows * facet_cols
    for i in range(facet_rows):
        for q in range(deal):
            for j in range(facet_cols):
                first = (deal * i + q) * facet_cols + j
                out_ref[pl.ds((i * facet_cols + j) * block + q * chans, chans), :] = rows_ref[
                    pl.ds(first, chans, stride=per_chan), :
                ]
    lane = lax.broadcasted_iota(jnp.int32, (per_chan, LANES), 1)
    column = lax.broadcasted_iota(jnp.int32, (per_chan, LANES), 0) % facet_cols
    for group in range(chans // SLOTS):
        left = jnp.zeros((per_chan, LANES), jnp.float32)
        right = jnp.zeros((per_chan, LANES), jnp.float32)
        on_left = lane < 0
        for slot in range(SLOTS):
            rows = rows_ref[pl.ds((group * SLOTS + slot) * per_chan, per_chan), :]
            start = 2 * HALO * slot
            here = (lane >= start) & (lane < start + HALO)
            on_left = on_left | here
            left = jnp.where(here, pltpu.roll(rows, (start + HALO) % LANES, 1), left)
            here = (lane >= start + HALO) & (lane < start + 2 * HALO)
            right = jnp.where(here, pltpu.roll(rows, start + HALO, 1), right)
        left = jnp.where(column > 0, pltpu.roll(left, 1, 0), 0.0)
        right = jnp.where(column < facet_cols - 1, pltpu.roll(right, per_chan - 1, 0), 0.0)
        sides = jnp.where(on_left, left, right)
        for i in range(facet_rows):
            for q in range(deal):
                first = (deal * i + q) * facet_cols
                place = i * facet_cols * block + deal * chans + q * (chans // SLOTS) + group
                out_ref[pl.ds(place, facet_cols, stride=block), :] = sides[first : first + facet_cols]


def prepare_kernel(width_ref, rows_ref, centre_ref, sides_ref, v_ref, w_ref, pad):
    lane = lax.broadcasted_iota(jnp.int32, rows_ref.shape, 1)
    up = (lane < FACET) | ((lane >= FACET + EDGE - width_ref[0]) & (lane < FACET + EDGE + width_ref[0]))
    head, tail = split(jnp.where(up, rows_ref[...], 0.0))
    v_ref[:, : 2 * LANES] = head
    v_ref[:, 2 * LANES : 4 * LANES] = tail
    v_ref[:, 4 * LANES :] = head
    place = lax.broadcasted_iota(jnp.int32, sides_ref.shape[1:], 0)
    before = jnp.where(place >= HALO - width_ref[1], sides_ref[0], 0.0)[:HALO]
    after = jnp.where(place < width_ref[1], sides_ref[1], 0.0)[:HALO]
    centre_head, centre_tail = split(centre_ref[...])
    for slot in range(SLOTS):
        pad[...] = jnp.zeros_like(pad)
        pad[2 * HALO * slot : 2 * HALO * slot + HALO, :] = before
        pad[2 * HALO * slot + HALO : 2 * HALO * (slot + 1), :] = after
        head, tail = split(pad[...])
        w_ref[slot] = jnp.concatenate(
            [centre_head, head, centre_head, head, centre_tail, tail], axis=0
        )


def unpack_kernel(in_ref, facet_ref, side_ref, top_ref, bottom_ref, *, chans, deal, senders):
    groups = chans // SLOTS
    block = deal * (chans + groups)
    for at in range(chans + groups):
        if at < chans:
            starts = [q * chans + at for q in range(deal)]
        else:
            starts = [deal * chans + q * groups + at - chans for q in range(deal)]
        rows = jnp.concatenate([in_ref[pl.ds(s, senders, stride=block), :] for s in starts], axis=0)
        if at < chans:
            facet_ref[at] = rows
        else:
            side_ref[at - chans] = rows
        top_ref[at] = rows[:EDGE]
        bottom_ref[at] = rows[FACET - EDGE :]


def project_kernel(facet_ref, nuc_ref, basis_ref, combined_ref, out_ref, *, chans, rank):
    for part in range(0, FACET, 32):
        rows = pl.ds(part, 32)
        total = [None] * rank
        for ch in range(chans):
            block = nuc_ref[ch, rows, :] + facet_ref[ch, rows, :]
            combined_ref[ch, rows, :] = block
            for k in range(rank):
                term = basis_ref[ch, k] * block
                total[k] = term if total[k] is None else total[k] + term
        for k in range(rank):
            out_ref[k, rows, :] = total[k]


def wavelet_kernel(
    band_ref, facet_ref, side_ref, above_ref, below_ref, v_ref, w_ref, wave_ref, out_ref, sq_ref, *, chans
):
    groups = chans // SLOTS
    half = FACET // 2
    lane = lax.broadcasted_iota(jnp.int32, (half, LANES), 1)
    nothing = jnp.zeros((2 * LANES - EXT, 2 * LANES), jnp.bfloat16)
    sides = [
        split(jnp.concatenate([side_ref[g], above_ref[chans + g], below_ref[chans + g]], axis=0))
        for g in range(groups)
    ]
    sq_ref[...] = jnp.zeros_like(sq_ref)
    for slot in range(SLOTS):
        for group in range(groups):
            ch = group * SLOTS + slot
            rows = jnp.concatenate([facet_ref[ch], above_ref[ch], below_ref[ch]], axis=0)
            head, tail = split(rows)
            side_head, side_tail = sides[group]
            taken = jnp.concatenate([head, side_head, tail, side_tail, head, side_head], axis=1)
            across = jnp.dot(taken, w_ref[slot], preferred_element_type=jnp.float32)
            head, tail = split(across)
            stacked = jnp.concatenate([head, nothing, head, nothing, tail, nothing], axis=0)
            both = jnp.dot(v_ref[...], stacked, preferred_element_type=jnp.float32)
            upper = jnp.where(lane < half, both[:half, :LANES], both[half:FACET, :LANES])
            coeffs = jnp.concatenate([upper, both[FACET:, LANES:]], axis=0)
            dual = wave_ref[ch] + coeffs
            out_ref[ch] = dual
            band = band_ref[ch]
            sq_ref[band] = sq_ref[band] + dual * dual


def gate_kernel(first_ref, held_ref, out_ref):
    pass


def weigh_kernel(me_ref, thresh_ref, weight_ref, parts_ref, squares_ref, out_ref, *, per, copies):
    for k in range(per):
        total = parts_ref[0, k]
        for source in range(1, copies):
            total = total + parts_ref[source, k]
        threshold = thresh_ref[me_ref[0] * per + k]
        singular = jnp.sqrt(jnp.sum(total * total, keepdims=True))
        scaled = total * (1.0 - threshold / jnp.maximum(singular, threshold))
        for target in range(copies):
            out_ref[target, k * FACET : (k + 1) * FACET] = scaled
    total = squares_ref[0]
    for source in range(1, copies):
        total = total + squares_ref[source]
    weight = weight_ref[me_ref[0]]
    ratio = weight / jnp.maximum(jnp.sqrt(total), weight)
    for target in range(copies):
        out_ref[target, per * FACET :] = ratio


def finish_kernel(
    band_ref, basis_ref, combined_ref, dual_ref, all_ref, wave_ref, nuc_ref, *, chans, rank, bands, per
):
    share = all_ref.shape[1] - per * FACET
    pieces = FACET // share if share <= FACET else 1
    size = min(share, 32)
    for part in range(0, FACET, size):
        rows = pl.ds(part, size)
        scaled = [all_ref[k // per, pl.ds(k % per * FACET + part, size), :] for k in range(rank)]
        for ch in range(chans):
            total = basis_ref[ch, 0] * scaled[0]
            for k in range(1, rank):
                total = total + basis_ref[ch, k] * scaled[k]
            nuc_ref[ch, rows, :] = combined_ref[ch, rows, :] - total
            source = band_ref[ch] * pieces + part // share
            ratio = all_ref[source, pl.ds(per * FACET + part % share, size), :]
            wave_ref[ch, rows, :] = dual_ref[ch, rows, :] * ratio


def call(kernel, name, ins, outs, operands, scratch=(), flops=0, limit=24):
    size = sum(4 * int(np.prod(o.shape)) for o in outs) + sum(4 * int(np.prod(o.shape)) for o in operands)
    return pl.pallas_call(
        kernel,
        name=name,
        in_specs=ins,
        out_specs=[VMEM] * len(outs),
        out_shape=outs,
        scratch_shapes=list(scratch),
        compiler_params=pltpu.CompilerParams(vmem_limit_bytes=limit * 1024 * 1024),
        cost_estimate=pl.CostEstimate(flops=flops, bytes_accessed=size, transcendentals=0),
    )(*operands)


def f32(*shape):
    return jax.ShapeDtypeStruct(shape, jnp.float32)


def bf16(*shape):
    return jax.ShapeDtypeStruct(shape, jnp.bfloat16)


def shards(primal_slab, wave_dual, nuc_dual, l21_weights, nuc_thresh, basis, band_of, margin_width):
    chans = wave_dual.shape[0]
    spec, rows, cols = (lax.axis_size(a) for a in ("spec", "frow", "fcol"))
    senders = rows * cols
    deal = primal_slab.shape[1] // rows
    rank = basis.shape[3]
    bands = l21_weights.shape[0]
    plane = ("frow", "fcol")
    me = lax.axis_index("spec").astype(jnp.int32).reshape(1)
    local_basis = basis.reshape(chans, rank)
    bands_here = band_of.reshape(chans)
    widths = margin_width.reshape(2)

    groups = chans // SLOTS
    block = deal * (chans + groups)
    (packed,) = call(
        functools.partial(pack_kernel, chans=chans, facet_rows=rows, facet_cols=cols, deal=deal),
        "pack", [VMEM], [f32(senders * block, LANES)],
        [primal_slab.reshape(-1, LANES)],
    )
    arrived = lax.all_to_all(
        packed.reshape(senders, block, LANES), plane, split_axis=0, concat_axis=0, tiled=True
    )
    centre, sides = column_operators()
    vertical, across = call(
        prepare_kernel, "prepare", [SMEM, VMEM, VMEM, VMEM],
        [bf16(3 * FACET // 2, 6 * LANES), bf16(SLOTS, 6 * LANES, 2 * LANES)],
        [widths, jnp.asarray(row_operator()), jnp.asarray(centre), jnp.asarray(sides)],
        scratch=[pltpu.VMEM((LANES, 2 * LANES), jnp.float32)],
    )
    strip = f32(chans + groups, EDGE, LANES)
    facet, side, top, bottom = call(
        functools.partial(unpack_kernel, chans=chans, deal=deal, senders=senders),
        "unpack", [VMEM],
        [f32(chans, FACET, LANES), f32(groups, FACET, LANES), strip, strip],
        [arrived.reshape(-1, LANES)],
    )
    above = lax.ppermute(bottom, "frow", [(i, i + 1) for i in range(rows - 1)])
    below = lax.ppermute(top, "frow", [(i + 1, i) for i in range(rows - 1)])
    combined, partial = call(
        functools.partial(project_kernel, chans=chans, rank=rank),
        "project", [VMEM, VMEM, SMEM],
        [f32(chans, FACET, LANES), f32(rank, FACET, LANES)],
        [facet, nuc_dual, local_basis],
        flops=2 * chans * rank * FACET * LANES,
    )
    per = rank // spec
    share = bands * FACET // spec
    parts = lax.all_to_all(
        partial.reshape(spec, per * FACET, LANES), "spec", split_axis=0, concat_axis=0, tiled=True
    )
    dual_sum, band_part = call(
        functools.partial(wavelet_kernel, chans=chans),
        "wavelet", [SMEM] + [VMEM] * 7,
        [f32(chans, FACET, LANES), f32(bands, FACET, LANES)],
        [bands_here, facet, side, above, below, vertical, across, wave_dual],
        flops=2 * chans * 3 * 192 * 256 * 600,
    )
    band_part = pl.pallas_call(
        gate_kernel,
        name="gate",
        in_specs=[pl.BlockSpec(memory_space=pl.ANY)] * 2,
        out_specs=pl.BlockSpec(memory_space=pl.ANY),
        out_shape=f32(bands, FACET, LANES),
        input_output_aliases={1: 0},
    )(parts, band_part)
    squares = lax.all_to_all(
        band_part.reshape(spec, share, LANES), "spec", split_axis=0, concat_axis=0, tiled=True
    )
    (weighed,) = call(
        functools.partial(weigh_kernel, per=per, copies=spec),
        "weigh", [SMEM, SMEM, VMEM, VMEM, VMEM], [f32(spec, per * FACET + share, LANES)],
        [me, nuc_thresh.reshape(rank), l21_weights.reshape(spec, share, LANES),
         parts.reshape(spec, per, FACET, LANES), squares],
    )
    everyone = lax.all_to_all(weighed, "spec", split_axis=0, concat_axis=0, tiled=True)
    wave_new, nuc_new = call(
        functools.partial(finish_kernel, chans=chans, rank=rank, bands=bands, per=per),
        "finish", [SMEM, SMEM, VMEM, VMEM, VMEM],
        [f32(chans, FACET, LANES), f32(chans, FACET, LANES)],
        [bands_here, local_basis, combined, dual_sum, everyone],
        flops=2 * chans * rank * FACET * LANES,
    )
    return (wave_new, nuc_new)


def solution(mesh):
    return jax.shard_map(
        shards,
        mesh=mesh,
        in_specs=(
            P("spec", None, "frow", "fcol", None),
            P("spec", "frow", "fcol"),
            P("spec", "frow", "fcol"),
            P(None, "frow", "fcol"),
            P("frow", "fcol", None),
            P("frow", "fcol", "spec", None),
            P("frow", "fcol", "spec"),
            P("frow", "fcol", None),
        ),
        out_specs=(P("spec", "frow", "fcol"), P("spec", "frow", "fcol")),
        check_vma=False,
    )
```

time: 235 us -> 124 us (0.53)
  the two profiles are of different devices: /device:TPU:1 before, /device:TPU:6 now
where the time goes in v1:
time: 124 us; the launch traced here: 123 us
  waiting for transfers between devices  48.8 us (39%)
  starting transfers between devices  35.3 us (28%)
  blocking collectives  20.1 us (16%)
  Pallas kernels  11.2 us (9%)
  local copies, waits for them, and re-layouts  7.21 us (6%)
    all_to_all x1, waiting for transfers between devices, shards(): lax.all_to_all(packed.reshape(senders, block, LANES), plane, split_axis=0...  27.1 us
    all_to_all x1, blocking collectives, shards(): lax.all_to_all(weighed, 'spec', split_axis=0, concat_axis=0, tiled=True)  20.1 us
    all_to_all x1, starting transfers between devices, shards(): lax.all_to_all(packed.reshape(senders, block, LANES), plane, split_axis=0...  15 us
    pallas_call x7, Pallas kernels, call(): pl.pallas_call(kernel, name=name, in_specs=ins, out_specs=[VMEM] * len(ou...  11.2 us
    all_to_all x1, waiting for transfers between devices, shards(): lax.all_to_all(band_part.reshape(spec, share, LANES), 'spec', split_axis=...  9.24 us
    ppermute x1, waiting for transfers between devices, shards(): above = lax.ppermute(bottom, 'frow', [(i, i + 1) for i in range(rows - 1)])  8.49 us
    unnamed x34, local copies, waits for them, and re-layouts  7.13 us
    all_to_all x1, starting transfers between devices, shards(): lax.all_to_all(band_part.reshape(spec, share, LANES), 'spec', split_axis=...  6.67 us
  transfers between devices with their start and end apart: 5, of which 4 were waited for; matrix products, arithmetic and copies ran while one was open for 0% of the time, Pallas kernels for 3%

profile of v1, /device:TPU:6, one launch (start us, length us, event | category | flops | bytes accessed | tf_op | source)
XLA Modules:
  0.0 123.4 jit_solution(14474196154799071513)
XLA Ops:
  0.6 1.1 copy-done.2
  1.8 1.8 %pack.1 = f32[2048,128]{1,0:T(8,128)} custom-call(f32[1536,128]{1,0:T(8,128)S(1)} %bitcast.13), custom_call_target="tpu_custom_call" | custom-call | bytes 1835008 | tf_op jit(solution)/shard_map/pack/pallas_call | solution.py:249
  3.6 15.0 %all-to-all-start = ((f32[64,32,128]{2,1,0:T(8,128)}), f32[64,32,128]{2,1,0:T(8,128)S(1)}, u32[]{:S(2)}, u32[]{:S(2)}) async-start(f32[64,32,128]{2,1,0:T(8,128)} %bitcast.3), calls=%async_computation | async-start | bytes 2097152 | tf_op jit(solution)/shard_map/all_to_all | solution.py:289
  18.7 27.1 %all-to-all-done = f32[64,32,128]{2,1,0:T(8,128)S(1)} async-done(((f32[64,32,128]{2,1,0:T(8,128)}), f32[64,32,128]{2,1,0:T(8,128)S(1)}, u32[]{:S(2)}, u32[]{:S(2)}) %all-to-all-start) | async-done | bytes 1048608 | tf_op jit(solution)/shard_map/all_to_all | solution.py:289
  46.4 0.7 copy-done.13
  47.1 0.7 copy-done.15
  47.9 2.0 %project.1 = (f32[12,128,128]{2,1,0:T(8,128)S(1)}, f32[8,128,128]{2,1,0:T(8,128)}) custom-call(f32[12,128,128]{2,1,0:T(8,128)S(1)} %get-tuple-element.12.facet_ref, f32[12,128,128]{2,1,0:T(8,128)S(1)} %copy-done.3, f32[12,8]{1,0:T(8,128)S(1)} %copy.15.basis_ref), custom_call_target="tpu_custom_call" | custom-call | flops 3145728 | bytes 2883968 | tf_op jit(solution)/shard_map/project/pallas_call | solution.py:249
  49.8 6.2 %all-to-all-start.1 = ((f32[8,128,128]{2,1,0:T(8,128)}), f32[8,128,128]{2,1,0:T(8,128)S(1)}, u32[]{:S(2)}, u32[]{:S(2)}) async-start(f32[8,128,128]{2,1,0:T(8,128)} %get-tuple-element.20), calls=%async_computation.1 | async-start | bytes 1048576 | tf_op jit(solution)/shard_map/all_to_all | solution.py:317
  56.0 5.5 %collective-permute-start = (f32[16,24,128]{2,1,0:T(8,128)}, f32[16,24,128]{2,1,0:T(8,128)S(1)}, u32[]{:S(2)}, u32[]{:S(2)}) collective-permute-start(f32[16,24,128]{2,1,0:T(8,128)} %copy-done.15), channel_id=1, source_target_pairs={{0,8},{8,16},{16,24},{24,32},{32,40},{40,48},{48,56},{1,9},{9,17},... | collective-permute-start | bytes 589832 | tf_op jit(solution)/shard_map/ppermute | solution.py:306
  61.6 1.9 %collective-permute-start.1 = (f32[16,24,128]{2,1,0:T(8,128)S(1)}, f32[16,24,128]{2,1,0:T(8,128)S(1)}, u32[]{:S(2)}, u32[]{:S(2)}) collective-permute-start(f32[16,24,128]{2,1,0:T(8,128)S(1)} %get-tuple-element.16), channel_id=1, source_target_pairs={{8,0},{16,8},{24,16},{32,24},{40,32},{48,40},{56,48},{9,1},{17,9},... | collective-permute-start | bytes 589832 | tf_op jit(solution)/shard_map/ppermute | solution.py:307
  63.5 0.7 prepare.1
  64.3 8.5 %collective-permute-done.above_ref = f32[16,24,128]{2,1,0:T(8,128)S(1)} collective-permute-done((f32[16,24,128]{2,1,0:T(8,128)}, f32[16,24,128]{2,1,0:T(8,128)S(1)}, u32[]{:S(2)}, u32[]{:S(2)}) %collective-permute-start) | collective-permute-done | bytes 196640 | tf_op jit(solution)/shard_map/ppermute | solution.py:306
  72.7 4.0 %collective-permute-done.1.below_ref = f32[16,24,128]{2,1,0:T(8,128)S(1)} collective-permute-done((f32[16,24,128]{2,1,0:T(8,128)S(1)}, f32[16,24,128]{2,1,0:T(8,128)S(1)}, u32[]{:S(2)}, u32[]{:S(2)}) %collective-permute-start.1) | collective-permute-done | bytes 196640 | tf_op jit(solution)/shard_map/ppermute | solution.py:307
  76.7 1.1 copy-done.12
  77.9 0.9 copy-done.14
  78.8 3.0 %wavelet.1 = (f32[12,128,128]{2,1,0:T(8,128)S(1)}, f32[2,128,128]{2,1,0:T(8,128)S(1)}) custom-call(s32[12]{0:T(128)S(1)} %bitcast.18, f32[12,128,128]{2,1,0:T(8,128)S(1)} %get-tuple-element.12.facet_ref, f32[4,128,128]{2,1,0:T(8,128)S(1)} %copy-done.14, f32[16,24,128]{2,1,0:T(8,128)S(1)} %collective-permute-done.above_ref, ...), custom_call_target="tpu_custom_call" | custom-call | flops 2123366400 | bytes 6094896 | tf_op jit(solution)/shard_map/wavelet/pallas_call | solution.py:249
  81.8 0.6 copy-done.4
  82.4 0.8 copy-done
  83.2 6.7 %all-to-all-start.2 = ((f32[8,32,128]{2,1,0:T(8,128)}), f32[8,32,128]{2,1,0:T(8,128)S(1)}, u32[]{:S(2)}, u32[]{:S(2)}) async-start(f32[8,32,128]{2,1,0:T(8,128)} %bitcast.14), calls=%async_computation.2 | async-start | bytes 262144 | tf_op jit(solution)/shard_map/all_to_all | solution.py:335
  89.9 9.2 %all-to-all-done.2.squares_ref = f32[8,32,128]{2,1,0:T(8,128)S(1)} async-done(((f32[8,32,128]{2,1,0:T(8,128)}), f32[8,32,128]{2,1,0:T(8,128)S(1)}, u32[]{:S(2)}, u32[]{:S(2)}) %all-to-all-start.2) | async-done | bytes 131104 | tf_op jit(solution)/shard_map/all_to_all | solution.py:335
  99.2 1.0 copy-done.1
  100.2 0.7 weigh.1
  100.9 20.1 %all_to_all.20.all_ref = f32[8,160,128]{2,1,0:T(8,128)S(1)} all-to-all(f32[8,160,128]{2,1,0:T(8,128)S(1)} %weigh.1), channel_id=1, replica_groups=mesh['spec'=8,'frow'=8,'fcol'=8] {'spec'}, dimensions={0} | all-to-all | bytes 1310720 | tf_op jit(solution)/shard_map/all_to_all | solution.py:344
  121.0 2.3 %finish.1 = (f32[12,128,128]{2,1,0:T(8,128)}, f32[12,128,128]{2,1,0:T(8,128)}) custom-call(s32[12]{0:T(128)S(1)} %bitcast.19, f32[12,8]{1,0:T(8,128)S(1)} %copy.15.basis_ref, f32[12,128,128]{2,1,0:T(8,128)S(1)} %get-tuple-element.13.combined_ref, f32[12,128,128]{2,1,0:T(8,128)S(1)} %get-tuple-element.19.dual_ref, f32[8,160,128]{2,1,0:T(8,128)S(1)} %all_to_all.20.all_ref), custom_call_target="tpu_custom_call" | custom-call | flops 3145728 | bytes 3801520 | tf_op jit(solution)/shard_map/finish/pallas_call | solution.py:249
  (30 shorter events, 0.8 us)
Async XLA Ops:
  0.6 1.1 copy-start.2
  3.6 15.0 %copy-start.16 = (f32[1,1,12,8]{2,3,1,0:T(8,128)S(1)}, f32[1,1,12,8]{2,3,1,0:T(8,128)}, u32[]{:S(2)}) copy-start(f32[1,1,12,8]{2,3,1,0:T(8,128)} %param.16) | copy-start | bytes 1156
  3.6 44.2 %copy-start.3 = (f32[12,128,128]{2,1,0:T(8,128)S(1)}, f32[12,128,128]{2,1,0:T(8,128)}, u32[]{:S(2)}) copy-start(f32[12,128,128]{2,1,0:T(8,128)} %nuc_ref.1) | copy-start | bytes 2359300
  3.6 42.2 %all-to-all-start = ((f32[64,32,128]{2,1,0:T(8,128)}), f32[64,32,128]{2,1,0:T(8,128)S(1)}, u32[]{:S(2)}, u32[]{:S(2)}) async-start(f32[64,32,128]{2,1,0:T(8,128)} %bitcast.3), calls=%async_computation | async-start | bytes 2097152 | tf_op jit(solution)/shard_map/all_to_all | solution.py:289
  46.4 0.7 copy-start.13
  47.1 0.7 copy-start.15
  47.8 15.7 %copy-start.5 = (f32[192,256]{1,0:T(8,128)S(1)}, f32[192,256]{1,0:T(8,128)}, u32[]{:S(2)}) copy-start(f32[192,256]{1,0:T(8,128)} %constant.12.clone.rows_ref) | copy-start | bytes 589828
  47.8 15.7 %copy-start.7 = (f32[128,256]{1,0:T(8,128)S(1)}, f32[128,256]{1,0:T(8,128)}, u32[]{:S(2)}) copy-start(f32[128,256]{1,0:T(8,128)} %constant.13.clone.centre_ref) | copy-start | bytes 393220
  47.8 15.7 %copy-start.8 = (f32[2,24,256]{2,1,0:T(8,128)S(1)}, f32[2,24,256]{2,1,0:T(8,128)}, u32[]{:S(2)}) copy-start(f32[2,24,256]{2,1,0:T(8,128)} %constant.14.clone.sides_ref) | copy-start | bytes 147460
  47.8 15.7 %copy-start.10 = (s32[1,1,2]{2,1,0:T(1,128)S(1)}, s32[1,1,2]{2,1,0:T(1,128)}, u32[]{:S(2)}) copy-start(s32[1,1,2]{2,1,0:T(1,128)} %param.18) | copy-start | bytes 28
  47.8 28.9 %copy-start.11 = (s32[1,1,12]{2,1,0:T(1,128)S(1)}, s32[1,1,12]{2,1,0:T(1,128)}, u32[]{:S(2)}) copy-start(s32[1,1,12]{2,1,0:T(1,128)} %param.17) | copy-start | bytes 148
  49.8 32.6 %all-to-all-start.1 = ((f32[8,128,128]{2,1,0:T(8,128)}), f32[8,128,128]{2,1,0:T(8,128)S(1)}, u32[]{:S(2)}, u32[]{:S(2)}) async-start(f32[8,128,128]{2,1,0:T(8,128)} %get-tuple-element.20), calls=%async_computation.1 | async-start | bytes 1048576 | tf_op jit(solution)/shard_map/all_to_all | solution.py:317
  56.0 16.7 %collective-permute-start = (f32[16,24,128]{2,1,0:T(8,128)}, f32[16,24,128]{2,1,0:T(8,128)S(1)}, u32[]{:S(2)}, u32[]{:S(2)}) collective-permute-start(f32[16,24,128]{2,1,0:T(8,128)} %copy-done.15), channel_id=1, source_target_pairs={{0,8},{8,16},{16,24},{24,32},{32,40},{40,48},{48,56},{1,9},{9,17},... | collective-permute-start | bytes 589832 | tf_op jit(solution)/shard_map/ppermute | solution.py:306
  61.6 15.2 %collective-permute-start.1 = (f32[16,24,128]{2,1,0:T(8,128)S(1)}, f32[16,24,128]{2,1,0:T(8,128)S(1)}, u32[]{:S(2)}, u32[]{:S(2)}) collective-permute-start(f32[16,24,128]{2,1,0:T(8,128)S(1)} %get-tuple-element.16), channel_id=1, source_target_pairs={{8,0},{16,8},{24,16},{32,24},{40,32},{48,40},{56,48},{9,1},{17,9},... | collective-permute-start | bytes 589832 | tf_op jit(solution)/shard_map/ppermute | solution.py:307
  76.7 1.1 copy-start.12
  77.9 0.9 copy-start.14
  78.8 20.3 %copy-start.6 = (f32[2,128,128]{2,1,0:T(8,128)S(1)}, f32[2,128,128]{2,1,0:T(8,128)}, u32[]{:S(2)}) copy-start(f32[2,128,128]{2,1,0:T(8,128)} %param.14) | copy-start | bytes 393220
  78.8 20.3 %copy-start.9 = (f32[1,1,8]{2,1,0:T(1,128)S(1)}, f32[1,1,8]{2,1,0:T(1,128)}, u32[]{:S(2)}) copy-start(f32[1,1,8]{2,1,0:T(1,128)} %param.15) | copy-start | bytes 100
  81.8 0.7 copy-start.4
  82.4 0.8 copy-start
  83.2 15.9 %all-to-all-start.2 = ((f32[8,32,128]{2,1,0:T(8,128)}), f32[8,32,128]{2,1,0:T(8,128)S(1)}, u32[]{:S(2)}, u32[]{:S(2)}) async-start(f32[8,32,128]{2,1,0:T(8,128)} %bitcast.14), calls=%async_computation.2 | async-start | bytes 262144 | tf_op jit(solution)/shard_map/all_to_all | solution.py:335
  99.2 1.0 copy-start.1

commit v2 on v1

--- a/solution.py
+++ b/solution.py
@@ -16,6 +16,7 @@
 EXT = FACET + 2 * EDGE
 VMEM = pl.BlockSpec(memory_space=pltpu.VMEM)
 SMEM = pl.BlockSpec(memory_space=pltpu.SMEM)
+ANY = pl.BlockSpec(memory_space=pl.ANY)
 
 low_taps = [
     -0.00011747678400228192,
@@ -165,15 +166,23 @@
             block = nuc_ref[ch, rows, :] + facet_ref[ch, rows, :]
             combined_ref[ch, rows, :] = block
             for k in range(rank):
-                term = basis_ref[ch, k] * block
+                term = basis_ref[k, ch] * block
                 total[k] = term if total[k] is None else total[k] + term
         for k in range(rank):
             out_ref[k, rows, :] = total[k]
 
 
 def wavelet_kernel(
-    band_ref, facet_ref, side_ref, above_ref, below_ref, v_ref, w_ref, wave_ref, out_ref, sq_ref, *, chans
+    band_ref, facet_ref, side_ref, above_ref, below_ref, v_ref, w_ref, partial_ref, wave_ref,
+    out_ref, sums_ref, wave, squares, sems, *, chans,
 ):
+    fetches = [pltpu.make_async_copy(wave_ref.at[ch], wave.at[ch], sems.at[ch]) for ch in range(chans)]
+    for fetch in fetches:
+        fetch.start()
+    copies, height = sums_ref.shape[0], sums_ref.shape[1]
+    taken_rows = partial_ref.shape[1]
+    sums_ref[:, :taken_rows, :] = partial_ref[...]
+    squares[...] = jnp.zeros_like(squares)
     groups = chans // SLOTS
     half = FACET // 2
     lane = lax.broadcasted_iota(jnp.int32, (half, LANES), 1)
@@ -182,7 +191,6 @@
         split(jnp.concatenate([side_ref[g], above_ref[chans + g], below_ref[chans + g]], axis=0))
         for g in range(groups)
     ]
-    sq_ref[...] = jnp.zeros_like(sq_ref)
     for slot in range(SLOTS):
         for group in range(groups):
             ch = group * SLOTS + slot
@@ -196,29 +204,31 @@
             both = jnp.dot(v_ref[...], stacked, preferred_element_type=jnp.float32)
             upper = jnp.where(lane < half, both[:half, :LANES], both[half:FACET, :LANES])
             coeffs = jnp.concatenate([upper, both[FACET:, LANES:]], axis=0)
-            dual = wave_ref[ch] + coeffs
+            fetches[ch].wait()
+            dual = wave[ch] + coeffs
             out_ref[ch] = dual
             band = band_ref[ch]
-            sq_ref[band] = sq_ref[band] + dual * dual
-
-
-def gate_kernel(first_ref, held_ref, out_ref):
-    pass
-
-
-def weigh_kernel(me_ref, thresh_ref, weight_ref, parts_ref, squares_ref, out_ref, *, per, copies):
+            squares[band] = squares[band] + dual * dual
+    share = height - taken_rows
+    for source in range(copies):
+        band, first = divmod(source * share, FACET)
+        sums_ref[source, taken_rows:, :] = squares[band, first : first + share, :]
+
+
+def weigh_kernel(me_ref, thresh_ref, weight_ref, parts_ref, out_ref, *, per, copies):
     for k in range(per):
-        total = parts_ref[0, k]
+        rows = pl.ds(k * FACET, FACET)
+        total = parts_ref[0, rows]
         for source in range(1, copies):
-            total = total + parts_ref[source, k]
+            total = total + parts_ref[source, rows]
         threshold = thresh_ref[me_ref[0] * per + k]
         singular = jnp.sqrt(jnp.sum(total * total, keepdims=True))
         scaled = total * (1.0 - threshold / jnp.maximum(singular, threshold))
         for target in range(copies):
-            out_ref[target, k * FACET : (k + 1) * FACET] = scaled
-    total = squares_ref[0]
+            out_ref[target, rows] = scaled
+    total = parts_ref[0, per * FACET :]
     for source in range(1, copies):
-        total = total + squares_ref[source]
+        total = total + parts_ref[source, per * FACET :]
     weight = weight_ref[me_ref[0]]
     ratio = weight / jnp.maximum(jnp.sqrt(total), weight)
     for target in range(copies):
@@ -226,31 +236,39 @@
 
 
 def finish_kernel(
-    band_ref, basis_ref, combined_ref, dual_ref, all_ref, wave_ref, nuc_ref, *, chans, rank, bands, per
+    band_ref, basis_ref, combined_ref, dual_ref, all_ref, wave_ref, nuc_ref, wave, nuc, sems,
+    *, chans, rank, per,
 ):
     share = all_ref.shape[1] - per * FACET
-    pieces = FACET // share if share <= FACET else 1
+    pieces = FACET // share
     size = min(share, 32)
-    for part in range(0, FACET, size):
+    copies = []
+    for step, part in enumerate(range(0, FACET, size)):
         rows = pl.ds(part, size)
         scaled = [all_ref[k // per, pl.ds(k % per * FACET + part, size), :] for k in range(rank)]
         for ch in range(chans):
-            total = basis_ref[ch, 0] * scaled[0]
+            total = basis_ref[0, ch] * scaled[0]
             for k in range(1, rank):
-                total = total + basis_ref[ch, k] * scaled[k]
-            nuc_ref[ch, rows, :] = combined_ref[ch, rows, :] - total
+                total = total + basis_ref[k, ch] * scaled[k]
+            nuc[ch, rows, :] = combined_ref[ch, rows, :] - total
             source = band_ref[ch] * pieces + part // share
             ratio = all_ref[source, pl.ds(per * FACET + part % share, size), :]
-            wave_ref[ch, rows, :] = dual_ref[ch, rows, :] * ratio
-
-
-def call(kernel, name, ins, outs, operands, scratch=(), flops=0, limit=24):
+            wave[ch, rows, :] = dual_ref[ch, rows, :] * ratio
+        for place, (held, out) in enumerate(((nuc, nuc_ref), (wave, wave_ref))):
+            copy = pltpu.make_async_copy(held.at[:, rows, :], out.at[:, rows, :], sems.at[place, step])
+            copy.start()
+            copies.append(copy)
+    for copy in copies:
+        copy.wait()
+
+
+def call(kernel, name, ins, outs, operands, scratch=(), flops=0, limit=24, places=None):
     size = sum(4 * int(np.prod(o.shape)) for o in outs) + sum(4 * int(np.prod(o.shape)) for o in operands)
     return pl.pallas_call(
         kernel,
         name=name,
         in_specs=ins,
-        out_specs=[VMEM] * len(outs),
+        out_specs=places or [VMEM] * len(outs),
         out_shape=outs,
         scratch_shapes=list(scratch),
         compiler_params=pltpu.CompilerParams(vmem_limit_bytes=limit * 1024 * 1024),
@@ -275,7 +293,7 @@
     bands = l21_weights.shape[0]
     plane = ("frow", "fcol")
     me = lax.axis_index("spec").astype(jnp.int32).reshape(1)
-    local_basis = basis.reshape(chans, rank)
+    local_basis = basis.reshape(chans, rank).T
     bands_here = band_of.reshape(chans)
     widths = margin_width.reshape(2)
 
@@ -314,40 +332,38 @@
     )
     per = rank // spec
     share = bands * FACET // spec
-    parts = lax.all_to_all(
-        partial.reshape(spec, per * FACET, LANES), "spec", split_axis=0, concat_axis=0, tiled=True
-    )
-    dual_sum, band_part = call(
+    dual_sum, sums = call(
         functools.partial(wavelet_kernel, chans=chans),
-        "wavelet", [SMEM] + [VMEM] * 7,
-        [f32(chans, FACET, LANES), f32(bands, FACET, LANES)],
-        [bands_here, facet, side, above, below, vertical, across, wave_dual],
+        "wavelet", [SMEM] + [VMEM] * 7 + [ANY],
+        [f32(chans, FACET, LANES), f32(spec, per * FACET + share, LANES)],
+        [bands_here, facet, side, above, below, vertical, across,
+         partial.reshape(spec, per * FACET, LANES), wave_dual],
+        scratch=[
+            pltpu.VMEM((chans, FACET, LANES), jnp.float32),
+            pltpu.VMEM((bands, FACET, LANES), jnp.float32),
+            pltpu.SemaphoreType.DMA((chans,)),
+        ],
         flops=2 * chans * 3 * 192 * 256 * 600,
     )
-    band_part = pl.pallas_call(
-        gate_kernel,
-        name="gate",
-        in_specs=[pl.BlockSpec(memory_space=pl.ANY)] * 2,
-        out_specs=pl.BlockSpec(memory_space=pl.ANY),
-        out_shape=f32(bands, FACET, LANES),
-        input_output_aliases={1: 0},
-    )(parts, band_part)
-    squares = lax.all_to_all(
-        band_part.reshape(spec, share, LANES), "spec", split_axis=0, concat_axis=0, tiled=True
-    )
+    parts = lax.all_to_all(sums, "spec", split_axis=0, concat_axis=0, tiled=True)
     (weighed,) = call(
         functools.partial(weigh_kernel, per=per, copies=spec),
-        "weigh", [SMEM, SMEM, VMEM, VMEM, VMEM], [f32(spec, per * FACET + share, LANES)],
-        [me, nuc_thresh.reshape(rank), l21_weights.reshape(spec, share, LANES),
-         parts.reshape(spec, per, FACET, LANES), squares],
+        "weigh", [SMEM, SMEM, VMEM, VMEM], [f32(spec, per * FACET + share, LANES)],
+        [me, nuc_thresh.reshape(rank), l21_weights.reshape(spec, share, LANES), parts],
     )
     everyone = lax.all_to_all(weighed, "spec", split_axis=0, concat_axis=0, tiled=True)
     wave_new, nuc_new = call(
-        functools.partial(finish_kernel, chans=chans, rank=rank, bands=bands, per=per),
+        functools.partial(finish_kernel, chans=chans, rank=rank, per=per),
         "finish", [SMEM, SMEM, VMEM, VMEM, VMEM],
         [f32(chans, FACET, LANES), f32(chans, FACET, LANES)],
         [bands_here, local_basis, combined, dual_sum, everyone],
+        scratch=[
+            pltpu.VMEM((chans, FACET, LANES), jnp.float32),
+            pltpu.VMEM((chans, FACET, LANES), jnp.float32),
+            pltpu.SemaphoreType.DMA((2, FACET // min(share, 32))),
+        ],
         flops=2 * chans * rank * FACET * LANES,
+        places=[ANY, ANY],
     )
     return (wave_new, nuc_new)
 

time: 124 us -> 121 us (0.976)
  the two profiles are of different devices: /device:TPU:6 before, /device:TPU:1 now
where the time goes in v2:
time: 121 us; the launch traced here: 120 us
  blocking collectives  69.3 us (57%)
  waiting for transfers between devices  18.8 us (16%)
  Pallas kernels  15.3 us (13%)
  starting transfers between devices  14.1 us (12%)
    all_to_all x1, blocking collectives, shards(): lax.all_to_all(packed.reshape(senders, block, LANES), plane, split_axis=0...  43.7 us
    all_to_all x1, blocking collectives, shards(): lax.all_to_all(weighed, 'spec', split_axis=0, concat_axis=0, tiled=True)  25.6 us
    all_to_all x1, waiting for transfers between devices, shards(): lax.all_to_all(sums, 'spec', split_axis=0, concat_axis=0, tiled=True)  15.6 us
    pallas_call x7, Pallas kernels, call(): pl.pallas_call(kernel, name=name, in_specs=ins, out_specs=places or [VMEM...  15.3 us
    all_to_all x1, starting transfers between devices, shards(): lax.all_to_all(sums, 'spec', split_axis=0, concat_axis=0, tiled=True)  10.7 us
    ppermute x1, waiting for transfers between devices, shards(): below = lax.ppermute(top, 'frow', [(i + 1, i) for i in range(rows - 1)])  3.18 us
  transfers between devices with their start and end apart: 3, of which 2 were waited for; matrix products, arithmetic and copies ran while one was open for 0% of the time, Pallas kernels for 2%

profile of v2, /device:TPU:1, one launch (start us, length us, event | category | flops | bytes accessed | tf_op | source)
XLA Modules:
  0.0 119.6 jit_solution(9601892265176793585)
XLA Ops:
  0.6 1.1 copy-done
  1.8 0.8 pack.1
  2.6 0.0 copy-start.2
  2.6 0.0 copy-start.4
  2.6 0.0 copy-start.5
  2.6 0.0 copy-start.8
  2.7 43.7 %all_to_all.15 = f32[64,32,128]{2,1,0:T(8,128)S(1)} all-to-all(f32[64,32,128]{2,1,0:T(8,128)S(1)} %bitcast.11), channel_id=1, replica_groups=mesh['spec'=8,'frow'=8,'fcol'=8] {'frow','fcol'}, dimensions={0} | all-to-all | bytes 2097152 | tf_op jit(solution)/shard_map/all_to_all | solution.py:307
  46.3 0.6 unpack.1
  47.0 0.0 copy-start.9
  47.0 0.0 copy-start.10
  47.0 2.2 %collective-permute-start = (f32[16,24,128]{2,1,0:T(8,128)S(1)}, f32[16,24,128]{2,1,0:T(8,128)S(1)}, u32[]{:S(2)}, u32[]{:S(2)}) collective-permute-start(f32[16,24,128]{2,1,0:T(8,128)S(1)} %get-tuple-element.15), channel_id=1, source_target_pairs={{0,8},{8,16},{16,24},{24,32},{32,40},{40,48},{48,56},{1,9},{9,17},... | collective-permute-start | bytes 589832 | tf_op jit(solution)/shard_map/ppermute | solution.py:324
  49.2 1.3 %collective-permute-start.1 = (f32[16,24,128]{2,1,0:T(8,128)S(1)}, f32[16,24,128]{2,1,0:T(8,128)S(1)}, u32[]{:S(2)}, u32[]{:S(2)}) collective-permute-start(f32[16,24,128]{2,1,0:T(8,128)S(1)} %get-tuple-element.16), channel_id=1, source_target_pairs={{8,0},{16,8},{24,16},{32,24},{40,32},{48,40},{56,48},{9,1},{17,9},... | collective-permute-start | bytes 589832 | tf_op jit(solution)/shard_map/ppermute | solution.py:325
  50.5 0.7 prepare.1
  51.2 1.2 project.1
  52.4 0.0 collective-permute-done.above_ref
  52.4 3.2 %collective-permute-done.1.below_ref = f32[16,24,128]{2,1,0:T(8,128)S(1)} collective-permute-done((f32[16,24,128]{2,1,0:T(8,128)S(1)}, f32[16,24,128]{2,1,0:T(8,128)S(1)}, u32[]{:S(2)}, u32[]{:S(2)}) %collective-permute-start.1) | collective-permute-done | bytes 196640 | tf_op jit(solution)/shard_map/ppermute | solution.py:325
  55.6 9.3 %wavelet.1 = (f32[12,128,128]{2,1,0:T(8,128)S(1)}, f32[8,160,128]{2,1,0:T(8,128)}) custom-call(s32[12]{0:T(128)S(1)} %bitcast.19, f32[12,128,128]{2,1,0:T(8,128)S(1)} %get-tuple-element.12.facet_ref, f32[4,128,128]{2,1,0:T(8,128)S(1)} %get-tuple-element.14.side_ref, f32[16,24,128]{2,1,0:T(8,128)S(1)} %collective-permute-done.above_ref, ...), custom_call_target="tpu_custom_call" | custom-call | flops 2123366400 | bytes 7143472 | tf_op jit(solution)/shard_map/wavelet/pallas_call | solution.py:267
  64.9 0.0 copy-start.3
  64.9 0.0 copy-start.7
  65.0 10.7 %all-to-all-start.1 = ((f32[8,160,128]{2,1,0:T(8,128)}), f32[8,160,128]{2,1,0:T(8,128)S(1)}, u32[]{:S(2)}, u32[]{:S(2)}) async-start(f32[8,160,128]{2,1,0:T(8,128)} %get-tuple-element.21), calls=%async_computation.1 | async-start | bytes 1310720 | tf_op jit(solution)/shard_map/all_to_all | solution.py:348
  75.6 15.6 %all-to-all-done.1.parts_ref = f32[8,160,128]{2,1,0:T(8,128)S(1)} async-done(((f32[8,160,128]{2,1,0:T(8,128)}), f32[8,160,128]{2,1,0:T(8,128)S(1)}, u32[]{:S(2)}, u32[]{:S(2)}) %all-to-all-start.1) | async-done | bytes 655392 | tf_op jit(solution)/shard_map/all_to_all | solution.py:348
  91.2 0.7 weigh.1
  92.0 25.6 %all_to_all.16.all_ref = f32[8,160,128]{2,1,0:T(8,128)S(1)} all-to-all(f32[8,160,128]{2,1,0:T(8,128)S(1)} %weigh.1), channel_id=1, replica_groups=mesh['spec'=8,'frow'=8,'fcol'=8] {'spec'}, dimensions={0} | all-to-all | bytes 1310720 | tf_op jit(solution)/shard_map/all_to_all | solution.py:354
  117.6 2.0 %finish.1 = (f32[12,128,128]{2,1,0:T(8,128)}, f32[12,128,128]{2,1,0:T(8,128)}) custom-call(s32[12]{0:T(128)S(1)} %bitcast.20, f32[8,12]{1,0:T(8,128)S(1)} %bitcast.16, f32[12,128,128]{2,1,0:T(8,128)S(1)} %get-tuple-element.13.combined_ref, f32[12,128,128]{2,1,0:T(8,128)S(1)} %get-tuple-element.20.dual_ref, f32[8,160,128]{2,1,0:T(8,128)S(1)} %all_to_all.16.all_ref), custom_call_target="tpu_custom_call" | custom-call | flops 3145728 | bytes 3801520 | tf_op jit(solution)/shard_map/finish/pallas_call | solution.py:267
  (13 shorter events, 0.0 us)
Async XLA Ops:
  0.6 1.1 copy-start
  2.6 47.9 %copy-start.2 = (f32[192,256]{1,0:T(8,128)S(1)}, f32[192,256]{1,0:T(8,128)}, u32[]{:S(2)}) copy-start(f32[192,256]{1,0:T(8,128)} %constant.12.clone.rows_ref) | copy-start | bytes 589828
  2.6 47.9 %copy-start.4 = (f32[128,256]{1,0:T(8,128)S(1)}, f32[128,256]{1,0:T(8,128)}, u32[]{:S(2)}) copy-start(f32[128,256]{1,0:T(8,128)} %constant.13.clone.centre_ref) | copy-start | bytes 393220
  2.6 47.9 %copy-start.5 = (f32[2,24,256]{2,1,0:T(8,128)S(1)}, f32[2,24,256]{2,1,0:T(8,128)}, u32[]{:S(2)}) copy-start(f32[2,24,256]{2,1,0:T(8,128)} %constant.14.clone.sides_ref) | copy-start | bytes 147460
  2.6 47.9 %copy-start.8 = (s32[1,1,2]{2,1,0:T(1,128)S(1)}, s32[1,1,2]{2,1,0:T(1,128)}, u32[]{:S(2)}) copy-start(s32[1,1,2]{2,1,0:T(1,128)} %param.18) | copy-start | bytes 28
  46.3 4.9 %copy-start.1 = (f32[12,128,128]{2,1,0:T(8,128)S(1)}, f32[12,128,128]{2,1,0:T(8,128)}, u32[]{:S(2)}) copy-start(f32[12,128,128]{2,1,0:T(8,128)} %nuc_ref.1) | copy-start | bytes 2359300
  46.3 4.9 %copy-start.6 = (f32[1,1,12,8]{2,3,1,0:T(8,128)S(1)}, f32[1,1,12,8]{2,3,1,0:T(8,128)}, u32[]{:S(2)}) copy-start(f32[1,1,12,8]{2,3,1,0:T(8,128)} %param.16) | copy-start | bytes 1156
  47.0 8.6 %copy-start.9 = (s32[1,1,12]{2,1,0:T(1,128)S(1)}, s32[1,1,12]{2,1,0:T(1,128)}, u32[]{:S(2)}) copy-start(s32[1,1,12]{2,1,0:T(1,128)} %param.17) | copy-start | bytes 148
  47.0 8.6 %copy-start.10 = (f32[12,128,128]{2,1,0:T(8,128)S(1)}, f32[12,128,128]{2,1,0:T(8,128)}, u32[]{:S(2)}) copy-start(f32[12,128,128]{2,1,0:T(8,128)} %wave_ref.1) | copy-start | bytes 2359300
  47.0 5.4 %collective-permute-start = (f32[16,24,128]{2,1,0:T(8,128)S(1)}, f32[16,24,128]{2,1,0:T(8,128)S(1)}, u32[]{:S(2)}, u32[]{:S(2)}) collective-permute-start(f32[16,24,128]{2,1,0:T(8,128)S(1)} %get-tuple-element.15), channel_id=1, source_target_pairs={{0,8},{8,16},{16,24},{24,32},{32,40},{40,48},{48,56},{1,9},{9,17},... | collective-permute-start | bytes 589832 | tf_op jit(solution)/shard_map/ppermute | solution.py:324
  49.2 6.4 %collective-permute-start.1 = (f32[16,24,128]{2,1,0:T(8,128)S(1)}, f32[16,24,128]{2,1,0:T(8,128)S(1)}, u32[]{:S(2)}, u32[]{:S(2)}) collective-permute-start(f32[16,24,128]{2,1,0:T(8,128)S(1)} %get-tuple-element.16), channel_id=1, source_target_pairs={{8,0},{16,8},{24,16},{32,24},{40,32},{48,40},{56,48},{9,1},{17,9},... | collective-permute-start | bytes 589832 | tf_op jit(solution)/shard_map/ppermute | solution.py:325
  64.9 26.3 %copy-start.3 = (f32[2,128,128]{2,1,0:T(8,128)S(1)}, f32[2,128,128]{2,1,0:T(8,128)}, u32[]{:S(2)}) copy-start(f32[2,128,128]{2,1,0:T(8,128)} %param.14) | copy-start | bytes 393220
  64.9 26.3 %copy-start.7 = (f32[1,1,8]{2,1,0:T(1,128)S(1)}, f32[1,1,8]{2,1,0:T(1,128)}, u32[]{:S(2)}) copy-start(f32[1,1,8]{2,1,0:T(1,128)} %param.15) | copy-start | bytes 100
  65.0 26.3 %all-to-all-start.1 = ((f32[8,160,128]{2,1,0:T(8,128)}), f32[8,160,128]{2,1,0:T(8,128)S(1)}, u32[]{:S(2)}, u32[]{:S(2)}) async-start(f32[8,160,128]{2,1,0:T(8,128)} %get-tuple-element.21), calls=%async_computation.1 | async-start | bytes 1310720 | tf_op jit(solution)/shard_map/all_to_all | solution.py:348

commit v3 on v2

--- a/solution.py
+++ b/solution.py
@@ -16,7 +16,7 @@
 EXT = FACET + 2 * EDGE
 VMEM = pl.BlockSpec(memory_space=pltpu.VMEM)
 SMEM = pl.BlockSpec(memory_space=pltpu.SMEM)
-ANY = pl.BlockSpec(memory_space=pl.ANY)
+HBM = pl.BlockSpec(memory_space=pltpu.HBM)
 
 low_taps = [
     -0.00011747678400228192,
@@ -173,15 +173,18 @@
 
 
 def wavelet_kernel(
-    band_ref, facet_ref, side_ref, above_ref, below_ref, v_ref, w_ref, partial_ref, wave_ref,
-    out_ref, sums_ref, wave, squares, sems, *, chans,
+    me_ref, band_ref, facet_ref, side_ref, above_ref, below_ref, v_ref, w_ref, partial_ref, wave_ref,
+    out_ref, own_ref, other_ref, wave, squares, sems, *, chans,
 ):
     fetches = [pltpu.make_async_copy(wave_ref.at[ch], wave.at[ch], sems.at[ch]) for ch in range(chans)]
     for fetch in fetches:
         fetch.start()
-    copies, height = sums_ref.shape[0], sums_ref.shape[1]
-    taken_rows = partial_ref.shape[1]
-    sums_ref[:, :taken_rows, :] = partial_ref[...]
+    core = me_ref[0] % 2
+    chips = own_ref.shape[0]
+    share = own_ref.shape[1] - FACET
+    for chip in range(chips):
+        own_ref[chip, :FACET, :] = partial_ref[2 * chip + core]
+        other_ref[chip, :FACET, :] = partial_ref[2 * chip + 1 - core]
     squares[...] = jnp.zeros_like(squares)
     groups = chans // SLOTS
     half = FACET // 2
@@ -207,55 +210,64 @@
             fetches[ch].wait()
             dual = wave[ch] + coeffs
             out_ref[ch] = dual
-            band = band_ref[ch]
-            squares[band] = squares[band] + dual * dual
-    share = height - taken_rows
-    for source in range(copies):
-        band, first = divmod(source * share, FACET)
-        sums_ref[source, taken_rows:, :] = squares[band, first : first + share, :]
-
-
-def weigh_kernel(me_ref, thresh_ref, weight_ref, parts_ref, out_ref, *, per, copies):
-    for k in range(per):
-        rows = pl.ds(k * FACET, FACET)
-        total = parts_ref[0, rows]
-        for source in range(1, copies):
-            total = total + parts_ref[source, rows]
-        threshold = thresh_ref[me_ref[0] * per + k]
-        singular = jnp.sqrt(jnp.sum(total * total, keepdims=True))
-        scaled = total * (1.0 - threshold / jnp.maximum(singular, threshold))
-        for target in range(copies):
-            out_ref[target, rows] = scaled
-    total = parts_ref[0, per * FACET :]
-    for source in range(1, copies):
-        total = total + parts_ref[source, per * FACET :]
+            rows = pl.ds(pl.multiple_of(band_ref[ch] * FACET, FACET), FACET)
+            squares[rows, :] = squares[rows, :] + dual * dual
+    for chip in range(chips):
+        first = pl.multiple_of((2 * chip + core) * share, share)
+        own_ref[chip, FACET:, :] = squares[pl.ds(first, share), :]
+        first = pl.multiple_of((2 * chip + 1 - core) * share, share)
+        other_ref[chip, FACET:, :] = squares[pl.ds(first, share), :]
+
+
+def pair_kernel(me_ref, own_ref, came_ref, *outs):
+    chips = own_ref.shape[0]
+    for step, out_ref in enumerate(outs):
+        chip = (me_ref[0] // 2 + step) % chips
+        out_ref[...] = own_ref[chip] + came_ref[chip]
+
+
+def weigh_kernel(me_ref, thresh_ref, weight_ref, *refs):
+    parts, out_ref = refs[:-1], refs[-1]
+    total = parts[0][...]
+    for part in parts[1:]:
+        total = total + part[...]
+    spectrum, squares = total[:FACET], total[FACET:]
+    threshold = thresh_ref[me_ref[0]]
+    singular = jnp.sqrt(jnp.sum(spectrum * spectrum, keepdims=True))
+    out_ref[:FACET] = spectrum * (1.0 - threshold / jnp.maximum(singular, threshold))
     weight = weight_ref[me_ref[0]]
-    ratio = weight / jnp.maximum(jnp.sqrt(total), weight)
-    for target in range(copies):
-        out_ref[target, per * FACET :] = ratio
+    out_ref[FACET:] = weight / jnp.maximum(jnp.sqrt(squares), weight)
+
+
+def stack_kernel(*refs):
+    for place, ref in enumerate(refs[:-1]):
+        refs[-1][place] = ref[...]
 
 
 def finish_kernel(
-    band_ref, basis_ref, combined_ref, dual_ref, all_ref, wave_ref, nuc_ref, wave, nuc, sems,
-    *, chans, rank, per,
+    me_ref, band_ref, basis_ref, combined_ref, dual_ref, own_ref, other_ref, wave_ref, nuc_ref,
+    ordered, wave, nuc, sems, *, chans, rank,
 ):
-    share = all_ref.shape[1] - per * FACET
+    core, chips = me_ref[0] % 2, own_ref.shape[0]
+    for step in range(chips):
+        chip = (me_ref[0] // 2 + chips - step) % chips
+        ordered[2 * chip + core] = own_ref[step]
+        ordered[2 * chip + 1 - core] = other_ref[step]
+    share = ordered.shape[1] - FACET
     pieces = FACET // share
-    size = min(share, 32)
     copies = []
-    for step, part in enumerate(range(0, FACET, size)):
-        rows = pl.ds(part, size)
-        scaled = [all_ref[k // per, pl.ds(k % per * FACET + part, size), :] for k in range(rank)]
+    for part in range(pieces):
+        rows = pl.ds(part * share, share)
+        scaled = [ordered[k, rows, :] for k in range(rank)]
         for ch in range(chans):
             total = basis_ref[0, ch] * scaled[0]
             for k in range(1, rank):
                 total = total + basis_ref[k, ch] * scaled[k]
             nuc[ch, rows, :] = combined_ref[ch, rows, :] - total
-            source = band_ref[ch] * pieces + part // share
-            ratio = all_ref[source, pl.ds(per * FACET + part % share, size), :]
+            ratio = ordered[band_ref[ch] * pieces + part, FACET:, :]
             wave[ch, rows, :] = dual_ref[ch, rows, :] * ratio
         for place, (held, out) in enumerate(((nuc, nuc_ref), (wave, wave_ref))):
-            copy = pltpu.make_async_copy(held.at[:, rows, :], out.at[:, rows, :], sems.at[place, step])
+            copy = pltpu.make_async_copy(held.at[:, rows, :], out.at[:, rows, :], sems.at[place, part])
             copy.start()
             copies.append(copy)
     for copy in copies:
@@ -330,40 +342,50 @@
         [facet, nuc_dual, local_basis],
         flops=2 * chans * rank * FACET * LANES,
     )
-    per = rank // spec
     share = bands * FACET // spec
-    dual_sum, sums = call(
+    chips = spec // 2
+    chunk, chunks = f32(FACET + share, LANES), f32(chips, FACET + share, LANES)
+    dual_sum, own, other = call(
         functools.partial(wavelet_kernel, chans=chans),
-        "wavelet", [SMEM] + [VMEM] * 7 + [ANY],
-        [f32(chans, FACET, LANES), f32(spec, per * FACET + share, LANES)],
-        [bands_here, facet, side, above, below, vertical, across,
-         partial.reshape(spec, per * FACET, LANES), wave_dual],
+        "wavelet", [SMEM, SMEM] + [VMEM] * 7 + [HBM],
+        [f32(chans, FACET, LANES), chunks, chunks],
+        [me, bands_here, facet, side, above, below, vertical, across, partial, wave_dual],
         scratch=[
             pltpu.VMEM((chans, FACET, LANES), jnp.float32),
-            pltpu.VMEM((bands, FACET, LANES), jnp.float32),
+            pltpu.VMEM((bands * FACET, LANES), jnp.float32),
             pltpu.SemaphoreType.DMA((chans,)),
         ],
         flops=2 * chans * 3 * 192 * 256 * 600,
     )
-    parts = lax.all_to_all(sums, "spec", split_axis=0, concat_axis=0, tiled=True)
+
+    def swap(values):
+        return lax.ppermute(values, "spec", [(i, i ^ 1) for i in range(spec)])
+
+    def onward(values, step):
+        return lax.ppermute(values, "spec", [(i, (i + 2 * step) % spec) for i in range(spec)])
+
+    steps = range(1, chips)
+    mine = call(pair_kernel, "pair", [SMEM, VMEM, VMEM], [chunk] * chips, [me, own, swap(other)])
+    came = [onward(mine[step], step) for step in steps]
     (weighed,) = call(
-        functools.partial(weigh_kernel, per=per, copies=spec),
-        "weigh", [SMEM, SMEM, VMEM, VMEM], [f32(spec, per * FACET + share, LANES)],
-        [me, nuc_thresh.reshape(rank), l21_weights.reshape(spec, share, LANES), parts],
-    )
-    everyone = lax.all_to_all(weighed, "spec", split_axis=0, concat_axis=0, tiled=True)
+        weigh_kernel, "weigh", [SMEM, SMEM, VMEM] + [VMEM] * chips, [chunk],
+        [me, nuc_thresh.reshape(rank), l21_weights.reshape(spec, share, LANES), mine[0], *came],
+    )
+    gathered = [weighed] + [onward(weighed, step) for step in steps]
+    (stacked,) = call(stack_kernel, "stack", [VMEM] * chips, [chunks], gathered)
     wave_new, nuc_new = call(
-        functools.partial(finish_kernel, chans=chans, rank=rank, per=per),
-        "finish", [SMEM, SMEM, VMEM, VMEM, VMEM],
+        functools.partial(finish_kernel, chans=chans, rank=rank),
+        "finish", [SMEM, SMEM, SMEM] + [VMEM] * 4,
         [f32(chans, FACET, LANES), f32(chans, FACET, LANES)],
-        [bands_here, local_basis, combined, dual_sum, everyone],
+        [me, bands_here, local_basis, combined, dual_sum, stacked, swap(stacked)],
         scratch=[
+            pltpu.VMEM((spec, FACET + share, LANES), jnp.float32),
             pltpu.VMEM((chans, FACET, LANES), jnp.float32),
             pltpu.VMEM((chans, FACET, LANES), jnp.float32),
-            pltpu.SemaphoreType.DMA((2, FACET // min(share, 32))),
+            pltpu.SemaphoreType.DMA((2, FACET // share)),
         ],
         flops=2 * chans * rank * FACET * LANES,
-        places=[ANY, ANY],
+        places=[HBM, HBM],
     )
     return (wave_new, nuc_new)
 

time: 121 us -> 119 us (0.983); the launches traced: 120 us -> 119 us
  starting transfers between devices: 14.1 us -> 40.5 us
  blocking collectives: 69.3 us -> 43.7 us
  waiting for transfers between devices: 18.8 us -> 17.3 us
    ppermute x0 -> x8, starting transfers between devices: none -> 37.1 us  [the longest x6 24.9 us: onward(): lax.ppermute(values, 'spec', [(i, (i + 2 * step) % spec) for i in range(s...]
    all_to_all x1 -> x0, blocking collectives: 25.6 us -> none  [shards(): lax.all_to_all(weighed, 'spec', split_axis=0, concat_axis=0, tiled=True)]
    all_to_all x1 -> x0, waiting for transfers between devices: 15.6 us -> none  [shards(): lax.all_to_all(sums, 'spec', split_axis=0, concat_axis=0, tiled=True)]
    ppermute x0 -> x8, waiting for transfers between devices: none -> 13.9 us  [the longest x6 11.4 us: onward(): lax.ppermute(values, 'spec', [(i, (i + 2 * step) % spec) for i in range(s...]
    all_to_all x1 -> x0, starting transfers between devices: 10.7 us -> none  [shards(): lax.all_to_all(sums, 'spec', split_axis=0, concat_axis=0, tiled=True)]
    pallas_call x7 -> x9, Pallas kernels: 15.3 us -> 15.3 us  [call(): pl.pallas_call(kernel, name=name, in_specs=ins, out_specs=places or [VMEM...]
  transfers between devices with their start and end apart: 3 -> 10, of which waited for: 2 -> 7; matrix products, arithmetic and copies ran while one was open for 0% -> 0% of each run, Pallas kernels for 2% -> 2%
where the time goes in v3:
time: 119 us
  blocking collectives  43.7 us (37%)
  starting transfers between devices  40.5 us (34%)
  waiting for transfers between devices  17.3 us (15%)
  Pallas kernels  15.3 us (13%)
    all_to_all x1, blocking collectives, shards(): lax.all_to_all(packed.reshape(senders, block, LANES), plane, split_axis=0...  43.7 us
    ppermute x6, starting transfers between devices, onward(): lax.ppermute(values, 'spec', [(i, (i + 2 * step) % spec) for i in range(s...  24.9 us
    pallas_call x9, Pallas kernels, call(): pl.pallas_call(kernel, name=name, in_specs=ins, out_specs=places or [VMEM...  15.3 us
    ppermute x2, starting transfers between devices, swap(): return lax.ppermute(values, 'spec', [(i, i ^ 1) for i in range(spec)])  12.2 us
    ppermute x6, waiting for transfers between devices, onward(): lax.ppermute(values, 'spec', [(i, (i + 2 * step) % spec) for i in range(s...  11.4 us
    ppermute x1, waiting for transfers between devices, shards(): below = lax.ppermute(top, 'frow', [(i + 1, i) for i in range(rows - 1)])  3.42 us
    ppermute x2, waiting for transfers between devices, swap(): return lax.ppermute(values, 'spec', [(i, i ^ 1) for i in range(spec)])  2.47 us
  transfers between devices with their start and end apart: 10, of which 7 were waited for; matrix products, arithmetic and copies ran while one was open for 0% of the time, Pallas kernels for 2%

profile of v3, /device:TPU:1, one launch (start us, length us, event | category | flops | bytes accessed | tf_op | source)
XLA Modules:
  0.0 118.9 jit_solution(10059495848039104710)
XLA Ops:
  0.6 1.1 copy-done
  1.8 0.8 pack.1
  2.7 43.7 %all_to_all.5 = f32[64,32,128]{2,1,0:T(8,128)S(1)} all-to-all(f32[64,32,128]{2,1,0:T(8,128)S(1)} %bitcast.11), channel_id=1, replica_groups=mesh['spec'=8,'frow'=8,'fcol'=8] {'frow','fcol'}, dimensions={0} | all-to-all | bytes 2097152 | tf_op jit(solution)/shard_map/all_to_all | solution.py:319
  46.3 1.3 %unpack.1 = (f32[12,128,128]{2,1,0:T(8,128)S(1)}, f32[4,128,128]{2,1,0:T(8,128)S(1)}, f32[16,24,128]{2,1,0:T(8,128)}, f32[16,24,128]{2,1,0:T(8,128)}) custom-call(f32[2048,128]{1,0:T(8,128)S(1)} %bitcast.12), custom_call_target="tpu_custom_call" | custom-call | bytes 2490368 | tf_op jit(solution)/shard_map/unpack/pallas_call | solution.py:279
  47.7 2.2 %collective-permute-start = (f32[16,24,128]{2,1,0:T(8,128)}, f32[16,24,128]{2,1,0:T(8,128)S(1)}, u32[]{:S(2)}, u32[]{:S(2)}) collective-permute-start(f32[16,24,128]{2,1,0:T(8,128)} %get-tuple-element.20), channel_id=1, source_target_pairs={{0,8},{8,16},{16,24},{24,32},{32,40},{40,48},{48,56},{1,9},{9,17},... | collective-permute-start | bytes 589832 | tf_op jit(solution)/shard_map/ppermute | solution.py:336
  49.9 1.3 %collective-permute-start.1 = (f32[16,24,128]{2,1,0:T(8,128)}, f32[16,24,128]{2,1,0:T(8,128)S(1)}, u32[]{:S(2)}, u32[]{:S(2)}) collective-permute-start(f32[16,24,128]{2,1,0:T(8,128)} %get-tuple-element.21), channel_id=1, source_target_pairs={{8,0},{16,8},{24,16},{32,24},{40,32},{48,40},{56,48},{9,1},{17,9},... | collective-permute-start | bytes 589832 | tf_op jit(solution)/shard_map/ppermute | solution.py:337
  51.9 1.1 project.1
  53.1 3.4 %collective-permute-done.1.below_ref = f32[16,24,128]{2,1,0:T(8,128)S(1)} collective-permute-done((f32[16,24,128]{2,1,0:T(8,128)}, f32[16,24,128]{2,1,0:T(8,128)S(1)}, u32[]{:S(2)}, u32[]{:S(2)}) %collective-permute-start.1) | collective-permute-done | bytes 196640 | tf_op jit(solution)/shard_map/ppermute | solution.py:337
  56.5 8.6 %wavelet.1 = (f32[12,128,128]{2,1,0:T(8,128)S(1)}, f32[4,160,128]{2,1,0:T(8,128)S(1)}, f32[4,160,128]{2,1,0:T(8,128)S(1)}) custom-call(s32[1]{0:T(128)} %bitcast.me_ref, s32[12]{0:T(128)S(1)} %bitcast.19, f32[12,128,128]{2,1,0:T(8,128)S(1)} %get-tuple-element.17.facet_ref, f32[4,128,128]{2,1,0:T(8,128)S(1)} %get-tuple-element.19.side_ref, ...), custom_call_target="tpu_custom_call" | custom-call | flops 2123366400 | bytes 7143476 | tf_op jit(solution)/shard_map/wavelet/pallas_call | solution.py:279
  65.1 6.3 %collective-permute-start.2 = (f32[4,160,128]{2,1,0:T(8,128)S(1)}, f32[4,160,128]{2,1,0:T(8,128)S(1)}, u32[]{:S(2)}, u32[]{:S(2)}) collective-permute-start(f32[4,160,128]{2,1,0:T(8,128)S(1)} %get-tuple-element.27), channel_id=1, source_target_pairs={{0,64},{64,0},{128,192},{192,128},{256,320},{320,256},{384,448},{4... | collective-permute-start | bytes 983048 | tf_op jit(solution)/shard_map/ppermute | solution.py:362
  71.4 1.2 %collective-permute-done.2.came_ref = f32[4,160,128]{2,1,0:T(8,128)S(1)} collective-permute-done((f32[4,160,128]{2,1,0:T(8,128)S(1)}, f32[4,160,128]{2,1,0:T(8,128)S(1)}, u32[]{:S(2)}, u32[]{:S(2)}) %collective-permute-start.2) | collective-permute-done | bytes 327712 | tf_op jit(solution)/shard_map/ppermute | solution.py:362
  72.6 4.2 %collective-permute-start.3 = (f32[160,128]{1,0:T(8,128)S(1)}, f32[160,128]{1,0:T(8,128)S(1)}, u32[]{:S(2)}, u32[]{:S(2)}) collective-permute-start(f32[160,128]{1,0:T(8,128)S(1)} %get-tuple-element.29), channel_id=1, source_target_pairs={{0,128},{64,192},{128,256},{192,320},{256,384},{320,448},{384,0},{... | collective-permute-start | bytes 245768 | tf_op jit(solution)/shard_map/ppermute | solution.py:365
  76.9 4.8 %collective-permute-start.4 = (f32[160,128]{1,0:T(8,128)S(1)}, f32[160,128]{1,0:T(8,128)S(1)}, u32[]{:S(2)}, u32[]{:S(2)}) collective-permute-start(f32[160,128]{1,0:T(8,128)S(1)} %get-tuple-element.30), channel_id=1, source_target_pairs={{0,256},{64,320},{128,384},{192,448},{256,0},{320,64},{384,128},{4... | collective-permute-start | bytes 245768 | tf_op jit(solution)/shard_map/ppermute | solution.py:365
  81.6 5.0 %collective-permute-start.5 = (f32[160,128]{1,0:T(8,128)S(1)}, f32[160,128]{1,0:T(8,128)S(1)}, u32[]{:S(2)}, u32[]{:S(2)}) collective-permute-start(f32[160,128]{1,0:T(8,128)S(1)} %get-tuple-element.31), channel_id=1, source_target_pairs={{0,384},{64,448},{128,0},{192,64},{256,128},{320,192},{384,256},{4... | collective-permute-start | bytes 245768 | tf_op jit(solution)/shard_map/ppermute | solution.py:365
  86.6 2.8 %collective-permute-done.4.refs_2_ = f32[160,128]{1,0:T(8,128)S(1)} collective-permute-done((f32[160,128]{1,0:T(8,128)S(1)}, f32[160,128]{1,0:T(8,128)S(1)}, u32[]{:S(2)}, u32[]{:S(2)}) %collective-permute-start.4) | collective-permute-done | bytes 81952 | tf_op jit(solution)/shard_map/ppermute | solution.py:365
  89.5 3.1 %collective-permute-done.5.refs_3_ = f32[160,128]{1,0:T(8,128)S(1)} collective-permute-done((f32[160,128]{1,0:T(8,128)S(1)}, f32[160,128]{1,0:T(8,128)S(1)}, u32[]{:S(2)}, u32[]{:S(2)}) %collective-permute-start.5) | collective-permute-done | bytes 81952 | tf_op jit(solution)/shard_map/ppermute | solution.py:365
  93.2 2.6 %collective-permute-start.8 = (f32[160,128]{1,0:T(8,128)S(1)}, f32[160,128]{1,0:T(8,128)S(1)}, u32[]{:S(2)}, u32[]{:S(2)}) collective-permute-start(f32[160,128]{1,0:T(8,128)S(1)} %weigh.1.refs_0_), channel_id=1, source_target_pairs={{0,384},{64,448},{128,0},{192,64},{256,128},{320,192},{384,256},{4... | collective-permute-start | bytes 245768 | tf_op jit(solution)/shard_map/ppermute | solution.py:365
  95.8 6.4 %collective-permute-start.7 = (f32[160,128]{1,0:T(8,128)S(1)}, f32[160,128]{1,0:T(8,128)S(1)}, u32[]{:S(2)}, u32[]{:S(2)}) collective-permute-start(f32[160,128]{1,0:T(8,128)S(1)} %weigh.1.refs_0_), channel_id=1, source_target_pairs={{0,256},{64,320},{128,384},{192,448},{256,0},{320,64},{384,128},{4... | collective-permute-start | bytes 245768 | tf_op jit(solution)/shard_map/ppermute | solution.py:365
  102.3 1.9 %collective-permute-start.6 = (f32[160,128]{1,0:T(8,128)S(1)}, f32[160,128]{1,0:T(8,128)S(1)}, u32[]{:S(2)}, u32[]{:S(2)}) collective-permute-start(f32[160,128]{1,0:T(8,128)S(1)} %weigh.1.refs_0_), channel_id=1, source_target_pairs={{0,128},{64,192},{128,256},{192,320},{256,384},{320,448},{384,0},{... | collective-permute-start | bytes 245768 | tf_op jit(solution)/shard_map/ppermute | solution.py:365
  104.2 0.8 collective-permute-done.7.refs_2_
  105.0 4.7 %collective-permute-done.6.refs_1_ = f32[160,128]{1,0:T(8,128)S(1)} collective-permute-done((f32[160,128]{1,0:T(8,128)S(1)}, f32[160,128]{1,0:T(8,128)S(1)}, u32[]{:S(2)}, u32[]{:S(2)}) %collective-permute-start.6) | collective-permute-done | bytes 81952 | tf_op jit(solution)/shard_map/ppermute | solution.py:365
  109.8 5.9 %collective-permute-start.9 = (f32[4,160,128]{2,1,0:T(8,128)S(1)}, f32[4,160,128]{2,1,0:T(8,128)S(1)}, u32[]{:S(2)}, u32[]{:S(2)}) collective-permute-start(f32[4,160,128]{2,1,0:T(8,128)S(1)} %stack.1.own_ref), channel_id=1, source_target_pairs={{0,64},{64,0},{128,192},{192,128},{256,320},{320,256},{384,448},{4... | collective-permute-start | bytes 983048 | tf_op jit(solution)/shard_map/ppermute | solution.py:362
  115.7 1.2 %collective-permute-done.9.other_ref = f32[4,160,128]{2,1,0:T(8,128)S(1)} collective-permute-done((f32[4,160,128]{2,1,0:T(8,128)S(1)}, f32[4,160,128]{2,1,0:T(8,128)S(1)}, u32[]{:S(2)}, u32[]{:S(2)}) %collective-permute-start.9) | collective-permute-done | bytes 327712 | tf_op jit(solution)/shard_map/ppermute | solution.py:362
  116.9 2.0 %finish.1 = (f32[12,128,128]{2,1,0:T(8,128)}, f32[12,128,128]{2,1,0:T(8,128)}) custom-call(s32[1]{0:T(128)} %bitcast.me_ref, s32[12]{0:T(128)S(1)} %bitcast.20, f32[8,12]{1,0:T(8,128)S(1)} %bitcast.16, f32[12,128,128]{2,1,0:T(8,128)S(1)} %get-tuple-element.18.combined_ref, f32[12,128,128]{2,1,0:T(8,128)S(1)} %get-tuple-element.25.dual_ref, ...), custom_call_target="tpu_custom_call" | custom-call | flops 3145728 | bytes 3801524 | tf_op jit(solution)/shard_map/finish/pallas_call | solution.py:279
  (28 shorter events, 1.5 us)
Async XLA Ops:
  0.6 1.1 copy-start
  2.6 48.6 %copy-start.2 = (f32[192,256]{1,0:T(8,128)S(1)}, f32[192,256]{1,0:T(8,128)}, u32[]{:S(2)}) copy-start(f32[192,256]{1,0:T(8,128)} %constant.12.clone.rows_ref) | copy-start | bytes 589828
  2.6 48.6 %copy-start.3 = (f32[128,256]{1,0:T(8,128)S(1)}, f32[128,256]{1,0:T(8,128)}, u32[]{:S(2)}) copy-start(f32[128,256]{1,0:T(8,128)} %constant.13.clone.centre_ref) | copy-start | bytes 393220
  2.6 48.6 %copy-start.5 = (f32[2,24,256]{2,1,0:T(8,128)S(1)}, f32[2,24,256]{2,1,0:T(8,128)}, u32[]{:S(2)}) copy-start(f32[2,24,256]{2,1,0:T(8,128)} %constant.14.clone.sides_ref) | copy-start | bytes 147460
  2.6 48.6 %copy-start.7 = (s32[1,1,2]{2,1,0:T(1,128)S(1)}, s32[1,1,2]{2,1,0:T(1,128)}, u32[]{:S(2)}) copy-start(s32[1,1,2]{2,1,0:T(1,128)} %param.18) | copy-start | bytes 28
  46.3 5.6 %copy-start.1 = (f32[12,128,128]{2,1,0:T(8,128)S(1)}, f32[12,128,128]{2,1,0:T(8,128)}, u32[]{:S(2)}) copy-start(f32[12,128,128]{2,1,0:T(8,128)} %nuc_ref.1) | copy-start | bytes 2359300
  46.3 5.6 %copy-start.6 = (f32[1,1,12,8]{2,3,1,0:T(8,128)S(1)}, f32[1,1,12,8]{2,3,1,0:T(8,128)}, u32[]{:S(2)}) copy-start(f32[1,1,12,8]{2,3,1,0:T(8,128)} %param.16) | copy-start | bytes 1156
  47.7 8.8 %copy-start.9 = (s32[1,1,12]{2,1,0:T(1,128)S(1)}, s32[1,1,12]{2,1,0:T(1,128)}, u32[]{:S(2)}) copy-start(s32[1,1,12]{2,1,0:T(1,128)} %param.17) | copy-start | bytes 148
  47.7 8.8 %copy-start.10 = (f32[12,128,128]{2,1,0:T(8,128)S(1)}, f32[12,128,128]{2,1,0:T(8,128)}, u32[]{:S(2)}) copy-start(f32[12,128,128]{2,1,0:T(8,128)} %wave_ref.1) | copy-start | bytes 2359300
  47.7 5.4 %collective-permute-start = (f32[16,24,128]{2,1,0:T(8,128)}, f32[16,24,128]{2,1,0:T(8,128)S(1)}, u32[]{:S(2)}, u32[]{:S(2)}) collective-permute-start(f32[16,24,128]{2,1,0:T(8,128)} %get-tuple-element.20), channel_id=1, source_target_pairs={{0,8},{8,16},{16,24},{24,32},{32,40},{40,48},{48,56},{1,9},{9,17},... | collective-permute-start | bytes 589832 | tf_op jit(solution)/shard_map/ppermute | solution.py:336
  49.9 6.6 %collective-permute-start.1 = (f32[16,24,128]{2,1,0:T(8,128)}, f32[16,24,128]{2,1,0:T(8,128)S(1)}, u32[]{:S(2)}, u32[]{:S(2)}) collective-permute-start(f32[16,24,128]{2,1,0:T(8,128)} %get-tuple-element.21), channel_id=1, source_target_pairs={{8,0},{16,8},{24,16},{32,24},{40,32},{48,40},{56,48},{9,1},{17,9},... | collective-permute-start | bytes 589832 | tf_op jit(solution)/shard_map/ppermute | solution.py:337
  56.5 36.0 %copy-start.4 = (f32[2,128,128]{2,1,0:T(8,128)S(1)}, f32[2,128,128]{2,1,0:T(8,128)}, u32[]{:S(2)}) copy-start(f32[2,128,128]{2,1,0:T(8,128)} %param.14) | copy-start | bytes 393220
  56.5 36.0 %copy-start.8 = (f32[1,1,8]{2,1,0:T(1,128)S(1)}, f32[1,1,8]{2,1,0:T(1,128)}, u32[]{:S(2)}) copy-start(f32[1,1,8]{2,1,0:T(1,128)} %param.15) | copy-start | bytes 100
  65.1 7.5 %collective-permute-start.2 = (f32[4,160,128]{2,1,0:T(8,128)S(1)}, f32[4,160,128]{2,1,0:T(8,128)S(1)}, u32[]{:S(2)}, u32[]{:S(2)}) collective-permute-start(f32[4,160,128]{2,1,0:T(8,128)S(1)} %get-tuple-element.27), channel_id=1, source_target_pairs={{0,64},{64,0},{128,192},{192,128},{256,320},{320,256},{384,448},{4... | collective-permute-start | bytes 983048 | tf_op jit(solution)/shard_map/ppermute | solution.py:362
  72.6 14.0 %collective-permute-start.3 = (f32[160,128]{1,0:T(8,128)S(1)}, f32[160,128]{1,0:T(8,128)S(1)}, u32[]{:S(2)}, u32[]{:S(2)}) collective-permute-start(f32[160,128]{1,0:T(8,128)S(1)} %get-tuple-element.29), channel_id=1, source_target_pairs={{0,128},{64,192},{128,256},{192,320},{256,384},{320,448},{384,0},{... | collective-permute-start | bytes 245768 | tf_op jit(solution)/shard_map/ppermute | solution.py:365
  76.9 12.6 %collective-permute-start.4 = (f32[160,128]{1,0:T(8,128)S(1)}, f32[160,128]{1,0:T(8,128)S(1)}, u32[]{:S(2)}, u32[]{:S(2)}) collective-permute-start(f32[160,128]{1,0:T(8,128)S(1)} %get-tuple-element.30), channel_id=1, source_target_pairs={{0,256},{64,320},{128,384},{192,448},{256,0},{320,64},{384,128},{4... | collective-permute-start | bytes 245768 | tf_op jit(solution)/shard_map/ppermute | solution.py:365
  81.6 10.9 %collective-permute-start.5 = (f32[160,128]{1,0:T(8,128)S(1)}, f32[160,128]{1,0:T(8,128)S(1)}, u32[]{:S(2)}, u32[]{:S(2)}) collective-permute-start(f32[160,128]{1,0:T(8,128)S(1)} %get-tuple-element.31), channel_id=1, source_target_pairs={{0,384},{64,448},{128,0},{192,64},{256,128},{320,192},{384,256},{4... | collective-permute-start | bytes 245768 | tf_op jit(solution)/shard_map/ppermute | solution.py:365
  93.2 11.0 %collective-permute-start.8 = (f32[160,128]{1,0:T(8,128)S(1)}, f32[160,128]{1,0:T(8,128)S(1)}, u32[]{:S(2)}, u32[]{:S(2)}) collective-permute-start(f32[160,128]{1,0:T(8,128)S(1)} %weigh.1.refs_0_), channel_id=1, source_target_pairs={{0,384},{64,448},{128,0},{192,64},{256,128},{320,192},{384,256},{4... | collective-permute-start | bytes 245768 | tf_op jit(solution)/shard_map/ppermute | solution.py:365
  95.8 9.2 %collective-permute-start.7 = (f32[160,128]{1,0:T(8,128)S(1)}, f32[160,128]{1,0:T(8,128)S(1)}, u32[]{:S(2)}, u32[]{:S(2)}) collective-permute-start(f32[160,128]{1,0:T(8,128)S(1)} %weigh.1.refs_0_), channel_id=1, source_target_pairs={{0,256},{64,320},{128,384},{192,448},{256,0},{320,64},{384,128},{4... | collective-permute-start | bytes 245768 | tf_op jit(solution)/shard_map/ppermute | solution.py:365
  102.3 7.5 %collective-permute-start.6 = (f32[160,128]{1,0:T(8,128)S(1)}, f32[160,128]{1,0:T(8,128)S(1)}, u32[]{:S(2)}, u32[]{:S(2)}) collective-permute-start(f32[160,128]{1,0:T(8,128)S(1)} %weigh.1.refs_0_), channel_id=1, source_target_pairs={{0,128},{64,192},{128,256},{192,320},{256,384},{320,448},{384,0},{... | collective-permute-start | bytes 245768 | tf_op jit(solution)/shard_map/ppermute | solution.py:365
  109.8 7.2 %collective-permute-start.9 = (f32[4,160,128]{2,1,0:T(8,128)S(1)}, f32[4,160,128]{2,1,0:T(8,128)S(1)}, u32[]{:S(2)}, u32[]{:S(2)}) collective-permute-start(f32[4,160,128]{2,1,0:T(8,128)S(1)} %stack.1.own_ref), channel_id=1, source_target_pairs={{0,64},{64,0},{128,192},{192,128},{256,320},{320,256},{384,448},{4... | collective-permute-start | bytes 983048 | tf_op jit(solution)/shard_map/ppermute | solution.py:362

commit v4 on v3

--- a/solution.py
+++ b/solution.py
@@ -65,10 +65,13 @@
 
 def row_operator():
     whole = np.concatenate(operators())
-    placed = np.zeros((whole.shape[0], 2 * LANES), np.float32)
-    placed[:, :FACET] = whole[:, HALO : HALO + FACET]
-    placed[:, FACET + EDGE - HALO : FACET + EDGE] = whole[:, :HALO]
-    placed[:, FACET + EDGE : FACET + EDGE + HALO] = whole[:, HALO + FACET :]
+    placed = np.zeros((2, whole.shape[0], 2 * LANES), np.float32)
+    placed[:, :, :FACET] = whole[:, HALO : HALO + FACET]
+    above, below = whole[:, :HALO], whole[:, HALO + FACET :]
+    placed[0, :, FACET : FACET + HALO] = below
+    placed[0, :, EXT - HALO : EXT] = above
+    placed[1, :, FACET + EDGE - HALO : FACET + EDGE] = above
+    placed[1, :, FACET + EDGE : FACET + EDGE + HALO] = below
     return placed
 
 
@@ -120,10 +123,14 @@
                 out_ref[pl.ds(place, facet_cols, stride=block), :] = sides[first : first + facet_cols]
 
 
-def prepare_kernel(width_ref, rows_ref, centre_ref, sides_ref, v_ref, w_ref, pad):
-    lane = lax.broadcasted_iota(jnp.int32, rows_ref.shape, 1)
-    up = (lane < FACET) | ((lane >= FACET + EDGE - width_ref[0]) & (lane < FACET + EDGE + width_ref[0]))
-    head, tail = split(jnp.where(up, rows_ref[...], 0.0))
+def prepare_kernel(me_ref, width_ref, rows_ref, centre_ref, sides_ref, v_ref, w_ref, pad):
+    odd = me_ref[1] % 2
+    lane = lax.broadcasted_iota(jnp.int32, rows_ref.shape[1:], 1)
+    first = jnp.where(odd == 1, FACET + EDGE - width_ref[0], EXT - width_ref[0])
+    last = jnp.where(odd == 1, FACET + EDGE, FACET) + width_ref[0]
+    above = (lane >= first) & (lane < first + width_ref[0])
+    below = (lane >= last - width_ref[0]) & (lane < last)
+    head, tail = split(jnp.where((lane < FACET) | above | below, rows_ref[odd], 0.0))
     v_ref[:, : 2 * LANES] = head
     v_ref[:, 2 * LANES : 4 * LANES] = tail
     v_ref[:, 4 * LANES :] = head
@@ -141,21 +148,22 @@
         )
 
 
-def unpack_kernel(in_ref, facet_ref, side_ref, top_ref, bottom_ref, *, chans, deal, senders):
+def unpack_kernel(me_ref, in_ref, facet_ref, side_ref, first_ref, second_ref, *, chans, deal, senders):
     groups = chans // SLOTS
     block = deal * (chans + groups)
+    odd = me_ref[1] % 2
+    first = pl.ds(pl.multiple_of((FACET - EDGE) * (1 - odd), 8), EDGE)
+    second = pl.ds(pl.multiple_of((FACET - EDGE) * odd, 8), EDGE)
     for at in range(chans + groups):
         if at < chans:
             starts = [q * chans + at for q in range(deal)]
         else:
             starts = [deal * chans + q * groups + at - chans for q in range(deal)]
         rows = jnp.concatenate([in_ref[pl.ds(s, senders, stride=block), :] for s in starts], axis=0)
-        if at < chans:
-            facet_ref[at] = rows
-        else:
-            side_ref[at - chans] = rows
-        top_ref[at] = rows[:EDGE]
-        bottom_ref[at] = rows[FACET - EDGE :]
+        held, place = (facet_ref, at) if at < chans else (side_ref, at - chans)
+        held[place] = rows
+        first_ref[at] = held[place, first, :]
+        second_ref[at] = held[place, second, :]
 
 
 def project_kernel(facet_ref, nuc_ref, basis_ref, combined_ref, out_ref, *, chans, rank):
@@ -173,12 +181,9 @@
 
 
 def wavelet_kernel(
-    me_ref, band_ref, facet_ref, side_ref, above_ref, below_ref, v_ref, w_ref, partial_ref, wave_ref,
-    out_ref, own_ref, other_ref, wave, squares, sems, *, chans,
+    me_ref, band_ref, facet_ref, side_ref, first_ref, second_ref, v_ref, w_ref, partial_ref, wave_ref,
+    out_ref, own_ref, other_ref, squares, *, chans,
 ):
-    fetches = [pltpu.make_async_copy(wave_ref.at[ch], wave.at[ch], sems.at[ch]) for ch in range(chans)]
-    for fetch in fetches:
-        fetch.start()
     core = me_ref[0] % 2
     chips = own_ref.shape[0]
     share = own_ref.shape[1] - FACET
@@ -191,13 +196,13 @@
     lane = lax.broadcasted_iota(jnp.int32, (half, LANES), 1)
     nothing = jnp.zeros((2 * LANES - EXT, 2 * LANES), jnp.bfloat16)
     sides = [
-        split(jnp.concatenate([side_ref[g], above_ref[chans + g], below_ref[chans + g]], axis=0))
+        split(jnp.concatenate([side_ref[g], first_ref[chans + g], second_ref[chans + g]], axis=0))
         for g in range(groups)
     ]
     for slot in range(SLOTS):
         for group in range(groups):
             ch = group * SLOTS + slot
-            rows = jnp.concatenate([facet_ref[ch], above_ref[ch], below_ref[ch]], axis=0)
+            rows = jnp.concatenate([facet_ref[ch], first_ref[ch], second_ref[ch]], axis=0)
             head, tail = split(rows)
             side_head, side_tail = sides[group]
             taken = jnp.concatenate([head, side_head, tail, side_tail, head, side_head], axis=1)
@@ -207,8 +212,7 @@
             both = jnp.dot(v_ref[...], stacked, preferred_element_type=jnp.float32)
             upper = jnp.where(lane < half, both[:half, :LANES], both[half:FACET, :LANES])
             coeffs = jnp.concatenate([upper, both[FACET:, LANES:]], axis=0)
-            fetches[ch].wait()
-            dual = wave[ch] + coeffs
+            dual = wave_ref[ch] + coeffs
             out_ref[ch] = dual
             rows = pl.ds(pl.multiple_of(band_ref[ch] * FACET, FACET), FACET)
             squares[rows, :] = squares[rows, :] + dual * dual
@@ -219,29 +223,24 @@
         other_ref[chip, FACET:, :] = squares[pl.ds(first, share), :]
 
 
-def pair_kernel(me_ref, own_ref, came_ref, *outs):
-    chips = own_ref.shape[0]
-    for step, out_ref in enumerate(outs):
-        chip = (me_ref[0] // 2 + step) % chips
-        out_ref[...] = own_ref[chip] + came_ref[chip]
-
-
-def weigh_kernel(me_ref, thresh_ref, weight_ref, *refs):
-    parts, out_ref = refs[:-1], refs[-1]
-    total = parts[0][...]
-    for part in parts[1:]:
-        total = total + part[...]
+def pair_kernel(own_ref, came_ref, out_ref):
+    out_ref[...] = own_ref[...] + came_ref[...]
+
+
+def weigh_kernel(me_ref, thresh_ref, weight_ref, parts_ref, out_ref):
+    chips = parts_ref.shape[0]
+    total = parts_ref[0]
+    for chip in range(1, chips):
+        total = total + parts_ref[chip]
     spectrum, squares = total[:FACET], total[FACET:]
     threshold = thresh_ref[me_ref[0]]
     singular = jnp.sqrt(jnp.sum(spectrum * spectrum, keepdims=True))
-    out_ref[:FACET] = spectrum * (1.0 - threshold / jnp.maximum(singular, threshold))
+    scaled = spectrum * (1.0 - threshold / jnp.maximum(singular, threshold))
     weight = weight_ref[me_ref[0]]
-    out_ref[FACET:] = weight / jnp.maximum(jnp.sqrt(squares), weight)
-
-
-def stack_kernel(*refs):
-    for place, ref in enumerate(refs[:-1]):
-        refs[-1][place] = ref[...]
+    ratio = weight / jnp.maximum(jnp.sqrt(squares), weight)
+    for chip in range(chips):
+        out_ref[chip, :FACET] = scaled
+        out_ref[chip, FACET:] = ratio
 
 
 def finish_kernel(
@@ -249,10 +248,9 @@
     ordered, wave, nuc, sems, *, chans, rank,
 ):
     core, chips = me_ref[0] % 2, own_ref.shape[0]
-    for step in range(chips):
-        chip = (me_ref[0] // 2 + chips - step) % chips
-        ordered[2 * chip + core] = own_ref[step]
-        ordered[2 * chip + 1 - core] = other_ref[step]
+    for chip in range(chips):
+        ordered[2 * chip + core] = own_ref[chip]
+        ordered[2 * chip + 1 - core] = other_ref[chip]
     share = ordered.shape[1] - FACET
     pieces = FACET // share
     copies = []
@@ -304,7 +302,7 @@
     rank = basis.shape[3]
     bands = l21_weights.shape[0]
     plane = ("frow", "fcol")
-    me = lax.axis_index("spec").astype(jnp.int32).reshape(1)
+    me = jnp.stack([lax.axis_index("spec"), lax.axis_index("frow")]).astype(jnp.int32)
     local_basis = basis.reshape(chans, rank).T
     bands_here = band_of.reshape(chans)
     widths = margin_width.reshape(2)
@@ -321,20 +319,21 @@
     )
     centre, sides = column_operators()
     vertical, across = call(
-        prepare_kernel, "prepare", [SMEM, VMEM, VMEM, VMEM],
+        prepare_kernel, "prepare", [SMEM, SMEM, VMEM, VMEM, VMEM],
         [bf16(3 * FACET // 2, 6 * LANES), bf16(SLOTS, 6 * LANES, 2 * LANES)],
-        [widths, jnp.asarray(row_operator()), jnp.asarray(centre), jnp.asarray(sides)],
+        [me, widths, jnp.asarray(row_operator()), jnp.asarray(centre), jnp.asarray(sides)],
         scratch=[pltpu.VMEM((LANES, 2 * LANES), jnp.float32)],
     )
     strip = f32(chans + groups, EDGE, LANES)
-    facet, side, top, bottom = call(
+    facet, side, first, second = call(
         functools.partial(unpack_kernel, chans=chans, deal=deal, senders=senders),
-        "unpack", [VMEM],
+        "unpack", [SMEM, VMEM],
         [f32(chans, FACET, LANES), f32(groups, FACET, LANES), strip, strip],
-        [arrived.reshape(-1, LANES)],
-    )
-    above = lax.ppermute(bottom, "frow", [(i, i + 1) for i in range(rows - 1)])
-    below = lax.ppermute(top, "frow", [(i + 1, i) for i in range(rows - 1)])
+        [me, arrived.reshape(-1, LANES)],
+    )
+    first = lax.ppermute(first, "frow", [(i, i ^ 1) for i in range(rows)])
+    other = [(i, i - 1 if i % 2 == 0 else i + 1) for i in range(1, rows - 1)]
+    second = lax.ppermute(second, "frow", other)
     combined, partial = call(
         functools.partial(project_kernel, chans=chans, rank=rank),
         "project", [VMEM, VMEM, SMEM],
@@ -344,16 +343,14 @@
     )
     share = bands * FACET // spec
     chips = spec // 2
-    chunk, chunks = f32(FACET + share, LANES), f32(chips, FACET + share, LANES)
+    chunks = f32(chips, FACET + share, LANES)
     dual_sum, own, other = call(
         functools.partial(wavelet_kernel, chans=chans),
-        "wavelet", [SMEM, SMEM] + [VMEM] * 7 + [HBM],
+        "wavelet", [SMEM, SMEM] + [VMEM] * 8,
         [f32(chans, FACET, LANES), chunks, chunks],
-        [me, bands_here, facet, side, above, below, vertical, across, partial, wave_dual],
+        [me, bands_here, facet, side, first, second, vertical, across, partial, wave_dual],
         scratch=[
-            pltpu.VMEM((chans, FACET, LANES), jnp.float32),
             pltpu.VMEM((bands * FACET, LANES), jnp.float32),
-            pltpu.SemaphoreType.DMA((chans,)),
         ],
         flops=2 * chans * 3 * 192 * 256 * 600,
     )
@@ -361,23 +358,23 @@
     def swap(values):
         return lax.ppermute(values, "spec", [(i, i ^ 1) for i in range(spec)])
 
-    def onward(values, step):
-        return lax.ppermute(values, "spec", [(i, (i + 2 * step) % spec) for i in range(spec)])
-
-    steps = range(1, chips)
-    mine = call(pair_kernel, "pair", [SMEM, VMEM, VMEM], [chunk] * chips, [me, own, swap(other)])
-    came = [onward(mine[step], step) for step in steps]
+    def across_chips(values):
+        cores = [list(range(core, spec, 2)) for core in range(2)]
+        return lax.all_to_all(
+            values, "spec", split_axis=0, concat_axis=0, tiled=True, axis_index_groups=cores
+        )
+
+    (sums,) = call(pair_kernel, "pair", [VMEM, VMEM], [chunks], [own, swap(other)])
     (weighed,) = call(
-        weigh_kernel, "weigh", [SMEM, SMEM, VMEM] + [VMEM] * chips, [chunk],
-        [me, nuc_thresh.reshape(rank), l21_weights.reshape(spec, share, LANES), mine[0], *came],
-    )
-    gathered = [weighed] + [onward(weighed, step) for step in steps]
-    (stacked,) = call(stack_kernel, "stack", [VMEM] * chips, [chunks], gathered)
+        weigh_kernel, "weigh", [SMEM, SMEM, VMEM, VMEM], [chunks],
+        [me, nuc_thresh.reshape(rank), l21_weights.reshape(spec, share, LANES), across_chips(sums)],
+    )
+    own = across_chips(weighed)
     wave_new, nuc_new = call(
         functools.partial(finish_kernel, chans=chans, rank=rank),
         "finish", [SMEM, SMEM, SMEM] + [VMEM] * 4,
         [f32(chans, FACET, LANES), f32(chans, FACET, LANES)],
-        [me, bands_here, local_basis, combined, dual_sum, stacked, swap(stacked)],
+        [me, bands_here, local_basis, combined, dual_sum, own, swap(own)],
         scratch=[
             pltpu.VMEM((spec, FACET + share, LANES), jnp.float32),
             pltpu.VMEM((chans, FACET, LANES), jnp.float32),

time: 119 us -> 108 us (0.908)
  the two profiles are of different devices: /device:TPU:1 before, /device:TPU:3 now
where the time goes in v4:
time: 108 us; the launch traced here: 107 us
  waiting for transfers between devices  32.7 us (30%)
  starting transfers between devices  32.5 us (30%)
  blocking collectives  29.2 us (27%)
  Pallas kernels  10.7 us (10%)
  local copies, waits for them, and re-layouts  1.18 us (1%)
    all_to_all x2, blocking collectives, across_chips(): lax.all_to_all(values, 'spec', split_axis=0, concat_axis=0, tiled=True, a...  29.2 us
    all_to_all x1, waiting for transfers between devices, shards(): lax.all_to_all(packed.reshape(senders, block, LANES), plane, split_axis=0...  27.4 us
    all_to_all x1, starting transfers between devices, shards(): lax.all_to_all(packed.reshape(senders, block, LANES), plane, split_axis=0...  14.5 us
    ppermute x2, starting transfers between devices, swap(): return lax.ppermute(values, 'spec', [(i, i ^ 1) for i in range(spec)])  12.7 us
    pallas_call x8, Pallas kernels, call(): pl.pallas_call(kernel, name=name, in_specs=ins, out_specs=places or [VMEM...  10.7 us
    ppermute x1, starting transfers between devices, shards(): first = lax.ppermute(first, 'frow', [(i, i ^ 1) for i in range(rows)])  3.38 us
    ppermute x1, waiting for transfers between devices, shards(): second = lax.ppermute(second, 'frow', other)  2.85 us
    ppermute x2, waiting for transfers between devices, swap(): return lax.ppermute(values, 'spec', [(i, i ^ 1) for i in range(spec)])  2.47 us
  transfers between devices with their start and end apart: 5, of which 4 were waited for; matrix products, arithmetic and copies ran while one was open for 0% of the time, Pallas kernels for 2%

profile of v4, /device:TPU:3, one launch (start us, length us, event | category | flops | bytes accessed | tf_op | source)
XLA Modules:
  0.0 107.1 jit_solution(14996294392635919973)
XLA Ops:
  0.6 1.1 %copy-done = f32[12,16,1,1,1024]{4,3,2,1,0:T(1,128)S(1)} copy-done((f32[12,16,1,1,1024]{4,3,2,1,0:T(1,128)S(1)}, f32[12,16,1,1,1024]{4,3,2,1,0:T(1,128)}, u32[]{:S(2)}) %copy-start) | copy-done | bytes 786456
  1.8 1.8 %pack.1 = f32[2048,128]{1,0:T(8,128)} custom-call(f32[1536,128]{1,0:T(8,128)S(1)} %bitcast.13), custom_call_target="tpu_custom_call" | custom-call | bytes 1835008 | tf_op jit(solution)/shard_map/pack/pallas_call | solution.py:277
  3.6 14.5 %all-to-all-start = ((f32[64,32,128]{2,1,0:T(8,128)}), f32[64,32,128]{2,1,0:T(8,128)S(1)}, u32[]{:S(2)}, u32[]{:S(2)}) async-start(f32[64,32,128]{2,1,0:T(8,128)} %bitcast.6), calls=%async_computation | async-start | bytes 2097152 | tf_op jit(solution)/shard_map/all_to_all | solution.py:317
  18.1 0.0 copy-start.1
  18.1 0.0 copy-start.6
  18.1 0.1 pad_add_fusion.me_ref
  18.2 27.4 %all-to-all-done = f32[64,32,128]{2,1,0:T(8,128)S(1)} async-done(((f32[64,32,128]{2,1,0:T(8,128)}), f32[64,32,128]{2,1,0:T(8,128)S(1)}, u32[]{:S(2)}, u32[]{:S(2)}) %all-to-all-start) | async-done | bytes 1048608 | tf_op jit(solution)/shard_map/all_to_all | solution.py:317
  45.6 1.2 %unpack.1 = (f32[12,128,128]{2,1,0:T(8,128)S(1)}, f32[4,128,128]{2,1,0:T(8,128)S(1)}, f32[16,24,128]{2,1,0:T(8,128)S(1)}, f32[16,24,128]{2,1,0:T(8,128)S(1)}) custom-call(s32[2]{0:T(128)S(1)} %pad_add_fusion.me_ref, f32[2048,128]{1,0:T(8,128)S(1)} %bitcast.12), custom_call_target="tpu_custom_call" | custom-call | bytes 2490376 | tf_op jit(solution)/shard_map/unpack/pallas_call | solution.py:277
  46.8 0.0 copy-start.10
  46.8 3.4 %collective-permute-start = (f32[16,24,128]{2,1,0:T(8,128)S(1)}, f32[16,24,128]{2,1,0:T(8,128)S(1)}, u32[]{:S(2)}, u32[]{:S(2)}) collective-permute-start(f32[16,24,128]{2,1,0:T(8,128)S(1)} %get-tuple-element.16), channel_id=1, source_target_pairs={{0,8},{8,0},{16,24},{24,16},{32,40},{40,32},{48,56},{56,48},{1,9},... | collective-permute-start | bytes 589832 | tf_op jit(solution)/shard_map/ppermute | solution.py:334
  50.2 1.9 %collective-permute-start.1 = (f32[16,24,128]{2,1,0:T(8,128)S(1)}, f32[16,24,128]{2,1,0:T(8,128)S(1)}, u32[]{:S(2)}, u32[]{:S(2)}) collective-permute-start(f32[16,24,128]{2,1,0:T(8,128)S(1)} %get-tuple-element.17), channel_id=1, source_target_pairs={{8,16},{16,8},{24,32},{32,24},{40,48},{48,40},{9,17},{17,9},{25,33... | collective-permute-start | bytes 589832 | tf_op jit(solution)/shard_map/ppermute | solution.py:336
  52.2 0.7 prepare.1
  52.9 1.1 %project.1 = (f32[12,128,128]{2,1,0:T(8,128)S(1)}, f32[8,128,128]{2,1,0:T(8,128)S(1)}) custom-call(f32[12,128,128]{2,1,0:T(8,128)S(1)} %get-tuple-element.13.facet_ref, f32[12,128,128]{2,1,0:T(8,128)S(1)} %copy-done.1, f32[8,12]{1,0:T(8,128)S(1)} %bitcast.15), custom_call_target="tpu_custom_call" | custom-call | flops 3145728 | bytes 2883968 | tf_op jit(solution)/shard_map/project/pallas_call | solution.py:277
  54.1 2.9 %collective-permute-done.1.second_ref = f32[16,24,128]{2,1,0:T(8,128)S(1)} collective-permute-done((f32[16,24,128]{2,1,0:T(8,128)S(1)}, f32[16,24,128]{2,1,0:T(8,128)S(1)}, u32[]{:S(2)}, u32[]{:S(2)}) %collective-permute-start.1) | collective-permute-done | bytes 196640 | tf_op jit(solution)/shard_map/ppermute | solution.py:336
  56.9 3.1 %wavelet.1 = (f32[12,128,128]{2,1,0:T(8,128)S(1)}, f32[4,160,128]{2,1,0:T(8,128)S(1)}, f32[4,160,128]{2,1,0:T(8,128)S(1)}) custom-call(s32[2]{0:T(128)S(1)} %pad_add_fusion.me_ref, s32[12]{0:T(128)S(1)} %bitcast.19, f32[12,128,128]{2,1,0:T(8,128)S(1)} %get-tuple-element.13.facet_ref, f32[4,128,128]{2,1,0:T(8,128)S(1)} %get-tuple-element.15.side_ref, ...), custom_call_target="tpu_custom_call" | custom-call | flops 2123366400 | bytes 7143480 | tf_op jit(solution)/shard_map/wavelet/pallas_call | solution.py:277
  60.0 0.0 copy-start.3
  60.0 5.9 %collective-permute-start.2 = (f32[4,160,128]{2,1,0:T(8,128)S(1)}, f32[4,160,128]{2,1,0:T(8,128)S(1)}, u32[]{:S(2)}, u32[]{:S(2)}) collective-permute-start(f32[4,160,128]{2,1,0:T(8,128)S(1)} %get-tuple-element.23), channel_id=1, source_target_pairs={{0,64},{64,0},{128,192},{192,128},{256,320},{320,256},{384,448},{4... | collective-permute-start | bytes 983048 | tf_op jit(solution)/shard_map/ppermute | solution.py:359
  65.9 1.2 %collective-permute-done.2.came_ref = f32[4,160,128]{2,1,0:T(8,128)S(1)} collective-permute-done((f32[4,160,128]{2,1,0:T(8,128)S(1)}, f32[4,160,128]{2,1,0:T(8,128)S(1)}, u32[]{:S(2)}, u32[]{:S(2)}) %collective-permute-start.2) | collective-permute-done | bytes 327712 | tf_op jit(solution)/shard_map/ppermute | solution.py:359
  67.2 15.4 %all_to_all.15.parts_ref = f32[4,160,128]{2,1,0:T(8,128)S(1)} all-to-all(f32[4,160,128]{2,1,0:T(8,128)S(1)} %pair.1), channel_id=1, replica_groups={{0,128,256,384},{64,192,320,448},{1,129,257,385},{65,193,321,449},{2,13..., dimensions={0} | all-to-all | bytes 655360 | tf_op jit(solution)/shard_map/all_to_all | solution.py:363
  82.6 0.7 weigh.1
  83.3 13.8 %all_to_all.16.own_ref = f32[4,160,128]{2,1,0:T(8,128)S(1)} all-to-all(f32[4,160,128]{2,1,0:T(8,128)S(1)} %weigh.1), channel_id=1, replica_groups={{0,128,256,384},{64,192,320,448},{1,129,257,385},{65,193,321,449},{2,13..., dimensions={0} | all-to-all | bytes 655360 | tf_op jit(solution)/shard_map/all_to_all | solution.py:363
  97.1 6.8 %collective-permute-start.3 = (f32[4,160,128]{2,1,0:T(8,128)S(1)}, f32[4,160,128]{2,1,0:T(8,128)S(1)}, u32[]{:S(2)}, u32[]{:S(2)}) collective-permute-start(f32[4,160,128]{2,1,0:T(8,128)S(1)} %all_to_all.16.own_ref), channel_id=1, source_target_pairs={{0,64},{64,0},{128,192},{192,128},{256,320},{320,256},{384,448},{4... | collective-permute-start | bytes 983048 | tf_op jit(solution)/shard_map/ppermute | solution.py:359
  103.9 1.2 %collective-permute-done.3.other_ref = f32[4,160,128]{2,1,0:T(8,128)S(1)} collective-permute-done((f32[4,160,128]{2,1,0:T(8,128)S(1)}, f32[4,160,128]{2,1,0:T(8,128)S(1)}, u32[]{:S(2)}, u32[]{:S(2)}) %collective-permute-start.3) | collective-permute-done | bytes 327712 | tf_op jit(solution)/shard_map/ppermute | solution.py:359
  105.2 2.0 %finish.1 = (f32[12,128,128]{2,1,0:T(8,128)}, f32[12,128,128]{2,1,0:T(8,128)}) custom-call(s32[2]{0:T(128)S(1)} %pad_add_fusion.me_ref, s32[12]{0:T(128)S(1)} %bitcast.20, f32[8,12]{1,0:T(8,128)S(1)} %bitcast.16, f32[12,128,128]{2,1,0:T(8,128)S(1)} %get-tuple-element.14.combined_ref, f32[12,128,128]{2,1,0:T(8,128)S(1)} %get-tuple-element.21.dual_ref, ...), custom_call_target="tpu_custom_call" | custom-call | flops 3145728 | bytes 3801528 | tf_op jit(solution)/shard_map/finish/pallas_call | solution.py:277
  (19 shorter events, 0.1 us)
Async XLA Ops:
  0.6 1.1 %copy-start = (f32[12,16,1,1,1024]{4,3,2,1,0:T(1,128)S(1)}, f32[12,16,1,1,1024]{4,3,2,1,0:T(1,128)}, u32[]{:S(2)}) copy-start(f32[12,16,1,1,1024]{4,3,2,1,0:T(1,128)} %param.11) | copy-start | bytes 2359300
  3.6 48.6 %copy-start.2 = (f32[2,192,256]{2,1,0:T(8,128)S(1)}, f32[2,192,256]{2,1,0:T(8,128)}, u32[]{:S(2)}) copy-start(f32[2,192,256]{2,1,0:T(8,128)} %constant.15.clone.rows_ref) | copy-start | bytes 1179652
  3.6 48.6 %copy-start.4 = (f32[128,256]{1,0:T(8,128)S(1)}, f32[128,256]{1,0:T(8,128)}, u32[]{:S(2)}) copy-start(f32[128,256]{1,0:T(8,128)} %constant.16.clone.centre_ref) | copy-start | bytes 393220
  3.6 48.6 %copy-start.5 = (f32[2,24,256]{2,1,0:T(8,128)S(1)}, f32[2,24,256]{2,1,0:T(8,128)}, u32[]{:S(2)}) copy-start(f32[2,24,256]{2,1,0:T(8,128)} %constant.17.clone.sides_ref) | copy-start | bytes 147460
  3.6 48.6 %copy-start.7 = (s32[1,1,2]{2,1,0:T(1,128)S(1)}, s32[1,1,2]{2,1,0:T(1,128)}, u32[]{:S(2)}) copy-start(s32[1,1,2]{2,1,0:T(1,128)} %param.18) | copy-start | bytes 28
  3.6 42.0 %all-to-all-start = ((f32[64,32,128]{2,1,0:T(8,128)}), f32[64,32,128]{2,1,0:T(8,128)S(1)}, u32[]{:S(2)}, u32[]{:S(2)}) async-start(f32[64,32,128]{2,1,0:T(8,128)} %bitcast.6), calls=%async_computation | async-start | bytes 2097152 | tf_op jit(solution)/shard_map/all_to_all | solution.py:317
  18.1 34.8 %copy-start.1 = (f32[12,128,128]{2,1,0:T(8,128)S(1)}, f32[12,128,128]{2,1,0:T(8,128)}, u32[]{:S(2)}) copy-start(f32[12,128,128]{2,1,0:T(8,128)} %nuc_ref.1) | copy-start | bytes 2359300
  18.1 34.8 %copy-start.6 = (f32[1,1,12,8]{2,3,1,0:T(8,128)S(1)}, f32[1,1,12,8]{2,3,1,0:T(8,128)}, u32[]{:S(2)}) copy-start(f32[1,1,12,8]{2,3,1,0:T(8,128)} %param.16) | copy-start | bytes 1156
  46.8 10.1 %copy-start.9 = (s32[1,1,12]{2,1,0:T(1,128)S(1)}, s32[1,1,12]{2,1,0:T(1,128)}, u32[]{:S(2)}) copy-start(s32[1,1,12]{2,1,0:T(1,128)} %param.17) | copy-start | bytes 148
  46.8 10.1 %copy-start.10 = (f32[12,128,128]{2,1,0:T(8,128)S(1)}, f32[12,128,128]{2,1,0:T(8,128)}, u32[]{:S(2)}) copy-start(f32[12,128,128]{2,1,0:T(8,128)} %wave_ref.1) | copy-start | bytes 2359300
  46.8 7.2 %collective-permute-start = (f32[16,24,128]{2,1,0:T(8,128)S(1)}, f32[16,24,128]{2,1,0:T(8,128)S(1)}, u32[]{:S(2)}, u32[]{:S(2)}) collective-permute-start(f32[16,24,128]{2,1,0:T(8,128)S(1)} %get-tuple-element.16), channel_id=1, source_target_pairs={{0,8},{8,0},{16,24},{24,16},{32,40},{40,32},{48,56},{56,48},{1,9},... | collective-permute-start | bytes 589832 | tf_op jit(solution)/shard_map/ppermute | solution.py:334
  50.2 6.7 %collective-permute-start.1 = (f32[16,24,128]{2,1,0:T(8,128)S(1)}, f32[16,24,128]{2,1,0:T(8,128)S(1)}, u32[]{:S(2)}, u32[]{:S(2)}) collective-permute-start(f32[16,24,128]{2,1,0:T(8,128)S(1)} %get-tuple-element.17), channel_id=1, source_target_pairs={{8,16},{16,8},{24,32},{32,24},{40,48},{48,40},{9,17},{17,9},{25,33... | collective-permute-start | bytes 589832 | tf_op jit(solution)/shard_map/ppermute | solution.py:336
  60.0 22.6 %copy-start.3 = (f32[2,128,128]{2,1,0:T(8,128)S(1)}, f32[2,128,128]{2,1,0:T(8,128)}, u32[]{:S(2)}) copy-start(f32[2,128,128]{2,1,0:T(8,128)} %param.14) | copy-start | bytes 393220
  60.0 22.6 %copy-start.8 = (f32[1,1,8]{2,1,0:T(1,128)S(1)}, f32[1,1,8]{2,1,0:T(1,128)}, u32[]{:S(2)}) copy-start(f32[1,1,8]{2,1,0:T(1,128)} %param.15) | copy-start | bytes 100
  60.0 7.1 %collective-permute-start.2 = (f32[4,160,128]{2,1,0:T(8,128)S(1)}, f32[4,160,128]{2,1,0:T(8,128)S(1)}, u32[]{:S(2)}, u32[]{:S(2)}) collective-permute-start(f32[4,160,128]{2,1,0:T(8,128)S(1)} %get-tuple-element.23), channel_id=1, source_target_pairs={{0,64},{64,0},{128,192},{192,128},{256,320},{320,256},{384,448},{4... | collective-permute-start | bytes 983048 | tf_op jit(solution)/shard_map/ppermute | solution.py:359
  97.1 8.1 %collective-permute-start.3 = (f32[4,160,128]{2,1,0:T(8,128)S(1)}, f32[4,160,128]{2,1,0:T(8,128)S(1)}, u32[]{:S(2)}, u32[]{:S(2)}) collective-permute-start(f32[4,160,128]{2,1,0:T(8,128)S(1)} %all_to_all.16.own_ref), channel_id=1, source_target_pairs={{0,64},{64,0},{128,192},{192,128},{256,320},{320,256},{384,448},{4... | collective-permute-start | bytes 983048 | tf_op jit(solution)/shard_map/ppermute | solution.py:359

commit v5 on v4

v5 whole, which is shorter than its diff:
```python
import functools

import jax
import jax.numpy as jnp
import numpy as np
from jax import lax
from jax.experimental import pallas as pl
from jax.experimental.pallas import tpu as pltpu
from jax.sharding import PartitionSpec as P

HALO = 21
EDGE = 24
SLOTS = 3
LANES = 128
FACET = 128
HALF = FACET // 2
CUT = 40
EXT = HALF + 2 * EDGE
PIECES = (
    (0, 32, True, 0),
    (32, 8, True, 32),
    (40, 24, False, 40),
    (64, 32, False, 0),
    (96, 8, False, 32),
    (104, 24, True, 40),
)
VMEM = pl.BlockSpec(memory_space=pltpu.VMEM)
SMEM = pl.BlockSpec(memory_space=pltpu.SMEM)
HBM = pl.BlockSpec(memory_space=pltpu.HBM)

low_taps = [
    -0.00011747678400228192,
    0.0006754494059985568,
    -0.0003917403729959771,
    -0.00487035299301066,
    0.008746094047015655,
    0.013981027917015516,
    -0.04408825393106472,
    -0.01736930100202211,
    0.128747426620186,
    0.00047248457399797254,
    -0.2840155429624281,
    -0.015829105256023893,
    0.5853546836548691,
    0.6756307362980128,
    0.3128715909144659,
    0.05441584224308161,
]
tap_lag = 7
high_taps = [(-1.0) ** place * low_taps[15 - place] for place in range(16)]


def filter_matrix(in_length, taps, first, count):
    matrix = np.zeros((count, in_length))
    for out in range(count):
        matrix[out, 2 * (out + first) : 2 * (out + first) + 16] = taps
    return matrix


@functools.cache
def operators():
    length = FACET + 2 * HALO
    half, quarter = FACET // 2, FACET // 4
    low_all = filter_matrix(length, low_taps, 0, half + 14)
    high = filter_matrix(length, high_taps, tap_lag, half)
    low = low_all[tap_lag : tap_lag + half]
    coarse = np.concatenate(
        [
            filter_matrix(half + 14, low_taps, 0, quarter) @ low_all,
            filter_matrix(half + 14, high_taps, 0, quarter) @ low_all,
        ]
    )
    return coarse, low, high


def row_operators():
    whole = np.concatenate(operators()).astype(np.float32)
    above, facet, below = whole[:, :HALO], whole[:, HALO : HALO + FACET], whole[:, HALO + FACET :]
    outer = np.zeros((2, whole.shape[0], LANES), np.float32)
    outer[:, :, :HALF] = np.concatenate([facet[:, :CUT], facet[:, HALF + CUT :]], axis=1)
    outer[0, :, HALF : HALF + HALO] = below
    outer[0, :, HALF + 2 * EDGE - HALO : HALF + 2 * EDGE] = above
    outer[1, :, HALF + EDGE - HALO : HALF + EDGE] = above
    outer[1, :, HALF + EDGE : HALF + EDGE + HALO] = below
    inner = np.concatenate([facet[:, HALF : HALF + CUT], facet[:, CUT:HALF]], axis=1)
    return np.concatenate([outer] * 3, axis=2), np.concatenate([inner] * 3, axis=1)


def column_operators():
    coarse, low, high = operators()
    whole = np.concatenate([coarse, high, low, high]).T.astype(np.float32)
    sides = np.zeros((2, EDGE, 2 * LANES), np.float32)
    sides[0, :HALO] = whole[:HALO]
    sides[1, :HALO] = whole[HALO + FACET :]
    return whole[HALO : HALO + FACET], sides


def split(values):
    head = values.astype(jnp.bfloat16)
    return head, (values - head.astype(jnp.float32)).astype(jnp.bfloat16)


def pack_kernel(me_ref, rows_ref, outer_ref, inner_ref, *, chans, facet_rows, facet_cols):
    groups = chans // SLOTS
    block = chans + groups
    per_chan = 2 * facet_rows * facet_cols
    late = me_ref[1] * facet_cols >= CUT

    def store(i, first, size, stride, rows):
        place = pl.ds(i * facet_cols * block + first, size, stride=stride)
        outer_ref[place, :] = jnp.where(late, rows[1], rows[0])
        inner_ref[place, :] = jnp.where(late, rows[0], rows[1])

    for i in range(facet_rows):
        for j in range(facet_cols):
            rows = [
                rows_ref[pl.ds((2 * i + q) * facet_cols + j, chans, stride=per_chan), :] for q in range(2)
            ]
            store(i, j * block, chans, 1, rows)
    lane = lax.broadcasted_iota(jnp.int32, (per_chan, LANES), 1)
    column = lax.broadcasted_iota(jnp.int32, (per_chan, LANES), 0) % facet_cols
    for group in range(groups):
        left = jnp.zeros((per_chan, LANES), jnp.float32)
        right = jnp.zeros((per_chan, LANES), jnp.float32)
        on_left = lane < 0
        for slot in range(SLOTS):
            rows = rows_ref[pl.ds((group * SLOTS + slot) * per_chan, per_chan), :]
            start = 2 * HALO * slot
            here = (lane >= start) & (lane < start + HALO)
            on_left = on_left | here
            left = jnp.where(here, pltpu.roll(rows, (start + HALO) % LANES, 1), left)
            here = (lane >= start + HALO) & (lane < start + 2 * HALO)
            right = jnp.where(here, pltpu.roll(rows, start + HALO, 1), right)
        left = jnp.where(column > 0, pltpu.roll(left, 1, 0), 0.0)
        right = jnp.where(column < facet_cols - 1, pltpu.roll(right, per_chan - 1, 0), 0.0)
        sides = jnp.where(on_left, left, right)
        for i in range(facet_rows):
            first = 2 * i * facet_cols
            rows = [sides[first + q * facet_cols : first + (q + 1) * facet_cols] for q in range(2)]
            store(i, chans + group, facet_cols, block, rows)


def head_and_tail(values, lane, width):
    head, tail = split(values)
    middle = (lane >= width) & (lane < 2 * width)
    return jnp.where(middle, tail.astype(jnp.float32), head.astype(jnp.float32)).astype(jnp.bfloat16)


def prepare_kernel(me_ref, width_ref, outer_ref, inner_ref, centre_ref, sides_ref, vo_ref, vi_ref, w_ref, pad):
    odd = me_ref[1] % 2
    lane = lax.broadcasted_iota(jnp.int32, outer_ref.shape[1:], 1)
    place = lane % LANES
    first = jnp.where(odd == 1, HALF + EDGE - width_ref[0], EXT - width_ref[0])
    last = jnp.where(odd == 1, HALF + EDGE, HALF) + width_ref[0]
    above = (place >= first) & (place < first + width_ref[0])
    below = (place >= last - width_ref[0]) & (place < last)
    inside = (place < HALF) | above | below
    vo_ref[...] = head_and_tail(jnp.where(inside, outer_ref[odd], 0.0), lane, LANES)
    lane = lax.broadcasted_iota(jnp.int32, inner_ref.shape, 1)
    vi_ref[...] = head_and_tail(inner_ref[...], lane, HALF)
    place = lax.broadcasted_iota(jnp.int32, sides_ref.shape[1:], 0)
    before = jnp.where(place >= HALO - width_ref[1], sides_ref[0], 0.0)[:HALO]
    after = jnp.where(place < width_ref[1], sides_ref[1], 0.0)[:HALO]
    centre_head, centre_tail = split(centre_ref[...])
    for slot in range(SLOTS):
        pad[...] = jnp.zeros_like(pad)
        pad[2 * HALO * slot : 2 * HALO * slot + HALO, :] = before
        pad[2 * HALO * slot + HALO : 2 * HALO * (slot + 1), :] = after
        head, tail = split(pad[...])
        w_ref[slot] = jnp.concatenate(
            [centre_head, head, centre_head, head, centre_tail, tail], axis=0
        )


def outer_kernel(me_ref, in_ref, rows_ref, first_ref, second_ref, *, senders):
    odd = me_ref[1] % 2 == 1
    block = rows_ref.shape[0]
    for at in range(block):
        rows = in_ref[pl.ds(at, senders, stride=block), :]
        rows_ref[at] = rows
        top, bottom = rows[:EDGE], rows[CUT:]
        first_ref[at] = jnp.where(odd, top, bottom)
        second_ref[at] = jnp.where(odd, bottom, top)


def inner_kernel(in_ref, rows_ref, *, senders):
    block = rows_ref.shape[0]
    for at in range(block):
        rows_ref[at] = in_ref[pl.ds(at, senders, stride=block), :]


def project_kernel(rows_ref, nuc_ref, basis_ref, combined_ref, out_ref, *, chans, rank, outer):
    for start, size, is_outer, place in PIECES:
        if is_outer != outer:
            continue
        total = [None] * rank
        for ch in range(chans):
            block = nuc_ref[ch, pl.ds(start, size), :] + rows_ref[ch, pl.ds(place, size), :]
            combined_ref[ch, pl.ds(place, size), :] = block
            for k in range(rank):
                term = basis_ref[k, ch] * block
                total[k] = term if total[k] is None else total[k] + term
        for k in range(rank):
            out_ref[k, pl.ds(place, size), :] = total[k]


def filtered(ch, parts, sides, w_ref, v_ref, chans, gap):
    slot, group = ch % SLOTS, ch // SLOTS
    head, tail = split(jnp.concatenate([part[ch] for part in parts], axis=0))
    side_head, side_tail = sides[group]
    taken = jnp.concatenate([head, side_head, tail, side_tail, head, side_head], axis=1)
    across = jnp.dot(taken, w_ref[slot], preferred_element_type=jnp.float32)
    head, tail = split(across)
    stacked = [head, head, tail]
    if gap:
        nothing = jnp.zeros((gap, 2 * LANES), jnp.bfloat16)
        stacked = [head, nothing, head, nothing, tail, nothing]
    stacked = jnp.concatenate(stacked, axis=0)
    return jnp.dot(v_ref[...], stacked, preferred_element_type=jnp.float32)


def side_rows(parts, chans):
    return [
        split(jnp.concatenate([part[at] for part in parts], axis=0))
        for at in range(chans, parts[0].shape[0])
    ]


def order(chans):
    return [group * SLOTS + slot for slot in range(SLOTS) for group in range(chans // SLOTS)]


def quadrants(both):
    lane = lax.broadcasted_iota(jnp.int32, (HALF, LANES), 1)
    upper = jnp.where(lane < HALF, both[:HALF, :LANES], both[HALF:FACET, :LANES])
    return jnp.concatenate([upper, both[FACET:, LANES:]], axis=0)


def begin_kernel(rows_ref, first_ref, second_ref, v_ref, w_ref, wave_ref, out_ref, *, chans):
    parts = (rows_ref, first_ref, second_ref)
    sides = side_rows(parts, chans)
    for ch in order(chans):
        out_ref[ch] = wave_ref[ch] + quadrants(
            filtered(ch, parts, sides, w_ref, v_ref, chans, LANES - EXT)
        )


def wavelet_kernel(
    me_ref, band_ref, rows_ref, v_ref, w_ref, begun_ref, outer_ref, inner_ref,
    out_ref, own_ref, other_ref, squares, *, chans,
):
    core = me_ref[0] % 2
    chips = own_ref.shape[0]
    share = own_ref.shape[1] - FACET
    for chip in range(chips):
        for held, source in ((own_ref, 2 * chip + core), (other_ref, 2 * chip + 1 - core)):
            for start, size, is_outer, place in PIECES:
                part = outer_ref if is_outer else inner_ref
                held[chip, pl.ds(start, size), :] = part[source, pl.ds(place, size), :]
    squares[...] = jnp.zeros_like(squares)
    sides = side_rows((rows_ref,), chans)
    for ch in order(chans):
        dual = begun_ref[ch] + quadrants(filtered(ch, (rows_ref,), sides, w_ref, v_ref, chans, 0))
        out_ref[ch] = dual
        rows = pl.ds(pl.multiple_of(band_ref[ch] * FACET, FACET), FACET)
        squares[rows, :] = squares[rows, :] + dual * dual
    for chip in range(chips):
        first = pl.multiple_of((2 * chip + core) * share, share)
        own_ref[chip, FACET:, :] = squares[pl.ds(first, share), :]
        first = pl.multiple_of((2 * chip + 1 - core) * share, share)
        other_ref[chip, FACET:, :] = squares[pl.ds(first, share), :]


def pair_kernel(own_ref, came_ref, out_ref):
    out_ref[...] = own_ref[...] + came_ref[...]


def weigh_kernel(me_ref, thresh_ref, weight_ref, parts_ref, out_ref):
    chips = parts_ref.shape[0]
    total = parts_ref[0]
    for chip in range(1, chips):
        total = total + parts_ref[chip]
    spectrum, squares = total[:FACET], total[FACET:]
    threshold = thresh_ref[me_ref[0]]
    singular = jnp.sqrt(jnp.sum(spectrum * spectrum, keepdims=True))
    scaled = spectrum * (1.0 - threshold / jnp.maximum(singular, threshold))
    weight = weight_ref[me_ref[0]]
    ratio = weight / jnp.maximum(jnp.sqrt(squares), weight)
    for chip in range(chips):
        out_ref[chip, :FACET] = scaled
        out_ref[chip, FACET:] = ratio


def finish_kernel(
    me_ref, band_ref, basis_ref, outer_ref, inner_ref, dual_ref, own_ref, other_ref, wave_ref, nuc_ref,
    ordered, wave, nuc, sems, *, chans, rank,
):
    core, chips = me_ref[0] % 2, own_ref.shape[0]
    for chip in range(chips):
        ordered[2 * chip + core] = own_ref[chip]
        ordered[2 * chip + 1 - core] = other_ref[chip]
    share = ordered.shape[1] - FACET
    quarters = FACET // share
    copies = []
    for step, (start, size, is_outer, place) in enumerate(PIECES):
        rows = pl.ds(start, size)
        combined_ref = outer_ref if is_outer else inner_ref
        scaled = [ordered[k, rows, :] for k in range(rank)]
        for ch in range(chans):
            total = basis_ref[0, ch] * scaled[0]
            for k in range(1, rank):
                total = total + basis_ref[k, ch] * scaled[k]
            nuc[ch, rows, :] = combined_ref[ch, pl.ds(place, size), :] - total
            source = band_ref[ch] * quarters + start // share
            ratio = ordered[source, pl.ds(FACET + start % share, size), :]
            wave[ch, rows, :] = dual_ref[ch, rows, :] * ratio
        for kind, (held, out) in enumerate(((nuc, nuc_ref), (wave, wave_ref))):
            copy = pltpu.make_async_copy(held.at[:, rows, :], out.at[:, rows, :], sems.at[kind, step])
            copy.start()
            copies.append(copy)
    for copy in copies:
        copy.wait()


def call(kernel, name, ins, outs, operands, scratch=(), flops=0, limit=24, places=None):
    size = sum(4 * int(np.prod(o.shape)) for o in outs) + sum(4 * int(np.prod(o.shape)) for o in operands)
    return pl.pallas_call(
        kernel,
        name=name,
        in_specs=ins,
        out_specs=places or [VMEM] * len(outs),
        out_shape=outs,
        scratch_shapes=list(scratch),
        compiler_params=pltpu.CompilerParams(vmem_limit_bytes=limit * 1024 * 1024),
        cost_estimate=pl.CostEstimate(flops=flops, bytes_accessed=size, transcendentals=0),
    )(*operands)


def f32(*shape):
    return jax.ShapeDtypeStruct(shape, jnp.float32)


def bf16(*shape):
    return jax.ShapeDtypeStruct(shape, jnp.bfloat16)


def shards(primal_slab, wave_dual, nuc_dual, l21_weights, nuc_thresh, basis, band_of, margin_width):
    chans = wave_dual.shape[0]
    spec, rows, cols = (lax.axis_size(a) for a in ("spec", "frow", "fcol"))
    senders = rows * cols
    rank = basis.shape[3]
    bands = l21_weights.shape[0]
    plane = ("frow", "fcol")
    me = jnp.stack([lax.axis_index("spec"), lax.axis_index("frow")]).astype(jnp.int32)
    local_basis = basis.reshape(chans, rank).T
    bands_here = band_of.reshape(chans)
    widths = margin_width.reshape(2)

    block = chans + chans // SLOTS

    def redistribute(values):
        arrived = lax.all_to_all(
            values.reshape(senders, block, LANES), plane, split_axis=0, concat_axis=0, tiled=True
        )
        return arrived.reshape(-1, LANES)

    outer, inner = call(
        functools.partial(pack_kernel, chans=chans, facet_rows=rows, facet_cols=cols),
        "pack", [SMEM, VMEM], [f32(senders * block, LANES)] * 2,
        [me, primal_slab.reshape(-1, LANES)],
    )
    outer, inner = redistribute(outer), redistribute(inner)
    centre, sides = column_operators()
    outer_rows, inner_rows = row_operators()
    outer_filter, inner_filter, across = call(
        prepare_kernel, "prepare", [SMEM, SMEM] + [VMEM] * 4,
        [bf16(3 * HALF, 3 * LANES), bf16(3 * HALF, 3 * HALF), bf16(SLOTS, 6 * LANES, 2 * LANES)],
        [me, widths] + [jnp.asarray(m) for m in (outer_rows, inner_rows, centre, sides)],
        scratch=[pltpu.VMEM((LANES, 2 * LANES), jnp.float32)],
    )
    strip, halves = f32(block, EDGE, LANES), f32(block, HALF, LANES)
    outer, first, second = call(
        functools.partial(outer_kernel, senders=senders),
        "outer", [SMEM, VMEM], [halves, strip, strip], [me, outer],
    )
    first = lax.ppermute(first, "frow", [(i, i ^ 1) for i in range(rows)])
    other = [(i, i - 1 if i % 2 == 0 else i + 1) for i in range(1, rows - 1)]
    second = lax.ppermute(second, "frow", other)

    def project(values, is_outer):
        return call(
            functools.partial(project_kernel, chans=chans, rank=rank, outer=is_outer),
            "project", [VMEM, VMEM, SMEM],
            [f32(chans, HALF, LANES), f32(rank, HALF, LANES)],
            [values, nuc_dual, local_basis],
            flops=2 * chans * rank * HALF * LANES,
        )

    combined_outer, partial_outer = project(outer, True)
    (begun,) = call(
        functools.partial(begin_kernel, chans=chans),
        "begin", [VMEM] * 6, [f32(chans, FACET, LANES)],
        [outer, first, second, outer_filter, across, wave_dual],
        flops=2 * chans * 3 * 192 * 256 * 300,
    )
    (inner,) = call(functools.partial(inner_kernel, senders=senders), "inner", [VMEM], [halves], [inner])
    combined_inner, partial_inner = project(inner, False)
    share = bands * FACET // spec
    chips = spec // 2
    chunks = f32(chips, FACET + share, LANES)
    dual_sum, own, other = call(
        functools.partial(wavelet_kernel, chans=chans),
        "wavelet", [SMEM, SMEM] + [VMEM] * 6,
        [f32(chans, FACET, LANES), chunks, chunks],
        [me, bands_here, inner, inner_filter, across, begun, partial_outer, partial_inner],
        scratch=[pltpu.VMEM((bands * FACET, LANES), jnp.float32)],
        flops=2 * chans * 3 * 192 * 256 * 300,
    )

    def swap(values):
        return lax.ppermute(values, "spec", [(i, i ^ 1) for i in range(spec)])

    def across_chips(values):
        cores = [list(range(core, spec, 2)) for core in range(2)]
        return lax.all_to_all(
            values, "spec", split_axis=0, concat_axis=0, tiled=True, axis_index_groups=cores
        )

    (sums,) = call(pair_kernel, "pair", [VMEM, VMEM], [chunks], [own, swap(other)])
    (weighed,) = call(
        weigh_kernel, "weigh", [SMEM, SMEM, VMEM, VMEM], [chunks],
        [me, nuc_thresh.reshape(rank), l21_weights.reshape(spec, share, LANES), across_chips(sums)],
    )
    own = across_chips(weighed)
    wave_new, nuc_new = call(
        functools.partial(finish_kernel, chans=chans, rank=rank),
        "finish", [SMEM, SMEM, SMEM] + [VMEM] * 5,
        [f32(chans, FACET, LANES), f32(chans, FACET, LANES)],
        [me, bands_here, local_basis, combined_outer, combined_inner, dual_sum, own, swap(own)],
        scratch=[
            pltpu.VMEM((spec, FACET + share, LANES), jnp.float32),
            pltpu.VMEM((chans, FACET, LANES), jnp.float32),
            pltpu.VMEM((chans, FACET, LANES), jnp.float32),
            pltpu.SemaphoreType.DMA((2, len(PIECES))),
        ],
        flops=2 * chans * rank * FACET * LANES,
        places=[HBM, HBM],
    )
    return (wave_new, nuc_new)


def solution(mesh):
    return jax.shard_map(
        shards,
        mesh=mesh,
        in_specs=(
            P("spec", None, "frow", "fcol", None),
            P("spec", "frow", "fcol"),
            P("spec", "frow", "fcol"),
            P(None, "frow", "fcol"),
            P("frow", "fcol", None),
            P("frow", "fcol", "spec", None),
            P("frow", "fcol", "spec"),
            P("frow", "fcol", None),
        ),
        out_specs=(P("spec", "frow", "fcol"), P("spec", "frow", "fcol")),
        check_vma=False,
    )
```

time: 108 us -> 116 us (1.074)
  the two profiles are of different devices: /device:TPU:3 before, /device:TPU:1 now
where the time goes in v5:
time: 116 us
  blocking collectives  61.3 us (53%)
  starting transfers between devices  20.8 us (18%)
  Pallas kernels  18 us (16%)
  waiting for transfers between devices  12.5 us (11%)
  local copies, waits for them, and re-layouts  2.36 us (2%)
    all_to_all x1, blocking collectives, redistribute(): lax.all_to_all(values.reshape(senders, block, LANES), plane, split_axis=0...  32.8 us
    all_to_all x2, blocking collectives, across_chips(): lax.all_to_all(values, 'spec', split_axis=0, concat_axis=0, tiled=True, a...  28.5 us
    pallas_call x11, Pallas kernels, call(): pl.pallas_call(kernel, name=name, in_specs=ins, out_specs=places or [VMEM...  18 us
    ppermute x2, starting transfers between devices, swap(): return lax.ppermute(values, 'spec', [(i, i ^ 1) for i in range(spec)])  10.5 us
    all_to_all x1, waiting for transfers between devices, redistribute(): lax.all_to_all(values.reshape(senders, block, LANES), plane, split_axis=0...  9.98 us
    all_to_all x1, starting transfers between devices, redistribute(): lax.all_to_all(values.reshape(senders, block, LANES), plane, split_axis=0...  6.01 us
    ppermute x1, starting transfers between devices, shards(): first = lax.ppermute(first, 'frow', [(i, i ^ 1) for i in range(rows)])  2.91 us
    ppermute x2, waiting for transfers between devices, swap(): return lax.ppermute(values, 'spec', [(i, i ^ 1) for i in range(spec)])  2.47 us
  transfers between devices with their start and end apart: 5, of which 3 were waited for; matrix products, arithmetic and copies ran while one was open for 0% of the time, Pallas kernels for 3%

profile of v5, /device:TPU:1, one launch (start us, length us, event | category | flops | bytes accessed | tf_op | source)
XLA Modules:
  0.0 115.8 jit_solution(8038812977702089826)
XLA Ops:
  0.7 1.1 copy-done.1
  1.8 2.1 %pack.1 = (f32[1024,128]{1,0:T(8,128)S(1)}, f32[1024,128]{1,0:T(8,128)}) custom-call(s32[2]{0:T(128)S(1)} %pad_add_fusion.me_ref, f32[1536,128]{1,0:T(8,128)S(1)} %bitcast.16), custom_call_target="tpu_custom_call" | custom-call | bytes 1835016 | tf_op jit(solution)/shard_map/pack/pallas_call | solution.py:327
  4.0 32.8 %all_to_all.20 = f32[64,16,128]{2,1,0:T(8,128)S(1)} all-to-all(f32[64,16,128]{2,1,0:T(8,128)S(1)} %bitcast.17), channel_id=1, replica_groups=mesh['spec'=8,'frow'=8,'fcol'=8] {'frow','fcol'}, dimensions={0} | all-to-all | bytes 1048576 | tf_op jit(solution)/shard_map/all_to_all | solution.py:362
  36.7 6.0 %all-to-all-start.1 = ((f32[64,16,128]{2,1,0:T(8,128)}), f32[64,16,128]{2,1,0:T(8,128)S(1)}, u32[]{:S(2)}, u32[]{:S(2)}) async-start(f32[64,16,128]{2,1,0:T(8,128)} %bitcast.9), calls=%async_computation.1 | async-start | bytes 1048576 | tf_op jit(solution)/shard_map/all_to_all | solution.py:362
  42.8 1.4 %outer.1 = (f32[16,64,128]{2,1,0:T(8,128)S(1)}, f32[16,24,128]{2,1,0:T(8,128)}, f32[16,24,128]{2,1,0:T(8,128)S(1)}) custom-call(s32[2]{0:T(128)S(1)} %pad_add_fusion.me_ref, f32[1024,128]{1,0:T(8,128)S(1)} %bitcast.15), custom_call_target="tpu_custom_call" | custom-call | bytes 1441800 | tf_op jit(solution)/shard_map/outer/pallas_call | solution.py:327
  44.2 2.9 %collective-permute-start = (f32[16,24,128]{2,1,0:T(8,128)}, f32[16,24,128]{2,1,0:T(8,128)S(1)}, u32[]{:S(2)}, u32[]{:S(2)}) collective-permute-start(f32[16,24,128]{2,1,0:T(8,128)} %get-tuple-element.24), channel_id=1, source_target_pairs={{0,8},{8,0},{16,24},{24,16},{32,40},{40,32},{48,56},{56,48},{1,9},... | collective-permute-start | bytes 589832 | tf_op jit(solution)/shard_map/ppermute | solution.py:386
  47.1 1.3 %collective-permute-start.1 = (f32[16,24,128]{2,1,0:T(8,128)S(1)}, f32[16,24,128]{2,1,0:T(8,128)}, u32[]{:S(2)}, u32[]{:S(2)}) collective-permute-start(f32[16,24,128]{2,1,0:T(8,128)S(1)} %get-tuple-element.25), channel_id=1, source_target_pairs={{8,16},{16,8},{24,32},{32,24},{40,48},{48,40},{9,17},{17,9},{25,33... | collective-permute-start | bytes 589832 | tf_op jit(solution)/shard_map/ppermute | solution.py:388
  48.5 0.7 prepare.1
  49.2 1.0 copy-done.11
  50.2 10.0 %all-to-all-done.1 = f32[64,16,128]{2,1,0:T(8,128)S(1)} async-done(((f32[64,16,128]{2,1,0:T(8,128)}), f32[64,16,128]{2,1,0:T(8,128)S(1)}, u32[]{:S(2)}, u32[]{:S(2)}) %all-to-all-start.1) | async-done | bytes 524320 | tf_op jit(solution)/shard_map/all_to_all | solution.py:362
  60.2 0.2 inner.1.rows_ref
  60.4 0.9 project.2
  61.3 0.9 project.3
  62.2 0.1 copy-done.15
  62.4 5.1 %begin.1.begun_ref = f32[12,128,128]{2,1,0:T(8,128)S(1)} custom-call(f32[16,64,128]{2,1,0:T(8,128)S(1)} %get-tuple-element.18.rows_ref, f32[16,24,128]{2,1,0:T(8,128)S(1)} %collective-permute-done.first_ref, f32[16,24,128]{2,1,0:T(8,128)} %collective-permute-done.1.second_ref, bf16[192,384]{1,0:T(8,128)(2,1)S(1)} %copy-done.15, ...), custom_call_target="tpu_custom_call" | custom-call | flops 1061683200 | bytes 5144576 | tf_op jit(solution)/shard_map/begin/pallas_call | solution.py:327
  67.5 4.0 %wavelet.1 = (f32[12,128,128]{2,1,0:T(8,128)S(1)}, f32[4,160,128]{2,1,0:T(8,128)S(1)}, f32[4,160,128]{2,1,0:T(8,128)S(1)}) custom-call(s32[2]{0:T(128)S(1)} %pad_add_fusion.me_ref, s32[12]{0:T(128)S(1)} %bitcast.24, f32[16,64,128]{2,1,0:T(8,128)S(1)} %inner.1.rows_ref, bf16[192,192]{1,0:T(8,128)(2,1)S(1)} %copy-done.17, bf16[3,768,256]{2,1,0:T(8,128)(2,1)S(1)} %copy-done.12, ...), custom_call_target="tpu_custom_call" | custom-call | flops 1061683200 | bytes 5783608 | tf_op jit(solution)/shard_map/wavelet/pallas_call | solution.py:327
  71.5 4.6 %collective-permute-start.2 = (f32[4,160,128]{2,1,0:T(8,128)S(1)}, f32[4,160,128]{2,1,0:T(8,128)S(1)}, u32[]{:S(2)}, u32[]{:S(2)}) collective-permute-start(f32[4,160,128]{2,1,0:T(8,128)S(1)} %get-tuple-element.31), channel_id=1, source_target_pairs={{0,64},{64,0},{128,192},{192,128},{256,320},{320,256},{384,448},{4... | collective-permute-start | bytes 983048 | tf_op jit(solution)/shard_map/ppermute | solution.py:421
  76.1 1.2 %collective-permute-done.2.came_ref = f32[4,160,128]{2,1,0:T(8,128)S(1)} collective-permute-done((f32[4,160,128]{2,1,0:T(8,128)S(1)}, f32[4,160,128]{2,1,0:T(8,128)S(1)}, u32[]{:S(2)}, u32[]{:S(2)}) %collective-permute-start.2) | collective-permute-done | bytes 327712 | tf_op jit(solution)/shard_map/ppermute | solution.py:421
  77.4 16.6 %all_to_all.21.parts_ref = f32[4,160,128]{2,1,0:T(8,128)S(1)} all-to-all(f32[4,160,128]{2,1,0:T(8,128)S(1)} %pair.1), channel_id=1, replica_groups={{0,128,256,384},{64,192,320,448},{1,129,257,385},{65,193,321,449},{2,13..., dimensions={0} | all-to-all | bytes 655360 | tf_op jit(solution)/shard_map/all_to_all | solution.py:425
  94.0 0.7 weigh.1
  94.7 12.0 %all_to_all.22.own_ref = f32[4,160,128]{2,1,0:T(8,128)S(1)} all-to-all(f32[4,160,128]{2,1,0:T(8,128)S(1)} %weigh.1), channel_id=1, replica_groups={{0,128,256,384},{64,192,320,448},{1,129,257,385},{65,193,321,449},{2,13..., dimensions={0} | all-to-all | bytes 655360 | tf_op jit(solution)/shard_map/all_to_all | solution.py:425
  106.6 5.9 %collective-permute-start.3 = (f32[4,160,128]{2,1,0:T(8,128)S(1)}, f32[4,160,128]{2,1,0:T(8,128)S(1)}, u32[]{:S(2)}, u32[]{:S(2)}) collective-permute-start(f32[4,160,128]{2,1,0:T(8,128)S(1)} %all_to_all.22.own_ref), channel_id=1, source_target_pairs={{0,64},{64,0},{128,192},{192,128},{256,320},{320,256},{384,448},{4... | collective-permute-start | bytes 983048 | tf_op jit(solution)/shard_map/ppermute | solution.py:421
  112.6 1.2 %collective-permute-done.3.other_ref = f32[4,160,128]{2,1,0:T(8,128)S(1)} collective-permute-done((f32[4,160,128]{2,1,0:T(8,128)S(1)}, f32[4,160,128]{2,1,0:T(8,128)S(1)}, u32[]{:S(2)}, u32[]{:S(2)}) %collective-permute-start.3) | collective-permute-done | bytes 327712 | tf_op jit(solution)/shard_map/ppermute | solution.py:421
  113.8 2.0 %finish.1 = (f32[12,128,128]{2,1,0:T(8,128)}, f32[12,128,128]{2,1,0:T(8,128)}) custom-call(s32[2]{0:T(128)S(1)} %pad_add_fusion.me_ref, s32[12]{0:T(128)S(1)} %bitcast.25, f32[8,12]{1,0:T(8,128)S(1)} %bitcast.21, f32[12,64,128]{2,1,0:T(8,128)S(1)} %get-tuple-element.19.outer_ref, f32[12,64,128]{2,1,0:T(8,128)S(1)} %get-tuple-element.21.inner_ref, ...), custom_call_target="tpu_custom_call" | custom-call | flops 3145728 | bytes 3801528 | tf_op jit(solution)/shard_map/finish/pallas_call | solution.py:327
  (37 shorter events, 0.2 us)
Async XLA Ops:
  0.7 1.1 copy-start.1
  3.9 44.5 %copy-start.2 = (f32[2,192,384]{2,1,0:T(8,128)S(1)}, f32[2,192,384]{2,1,0:T(8,128)}, u32[]{:S(2)}) copy-start(f32[2,192,384]{2,1,0:T(8,128)} %constant.17.clone.outer_ref) | copy-start | bytes 1769476
  3.9 44.5 %copy-start.3 = (f32[192,192]{1,0:T(8,128)S(1)}, f32[192,192]{1,0:T(8,128)}, u32[]{:S(2)}) copy-start(f32[192,192]{1,0:T(8,128)} %constant.18.clone.inner_ref) | copy-start | bytes 442372
  3.9 44.5 %copy-start.5 = (f32[128,256]{1,0:T(8,128)S(1)}, f32[128,256]{1,0:T(8,128)}, u32[]{:S(2)}) copy-start(f32[128,256]{1,0:T(8,128)} %constant.19.clone.centre_ref) | copy-start | bytes 393220
  3.9 44.5 %copy-start.6 = (f32[2,24,256]{2,1,0:T(8,128)S(1)}, f32[2,24,256]{2,1,0:T(8,128)}, u32[]{:S(2)}) copy-start(f32[2,24,256]{2,1,0:T(8,128)} %constant.20.clone.sides_ref) | copy-start | bytes 147460
  3.9 44.5 %copy-start.8 = (s32[1,1,2]{2,1,0:T(1,128)S(1)}, s32[1,1,2]{2,1,0:T(1,128)}, u32[]{:S(2)}) copy-start(s32[1,1,2]{2,1,0:T(1,128)} %param.19) | copy-start | bytes 28
  36.7 23.5 %all-to-all-start.1 = ((f32[64,16,128]{2,1,0:T(8,128)}), f32[64,16,128]{2,1,0:T(8,128)S(1)}, u32[]{:S(2)}, u32[]{:S(2)}) async-start(f32[64,16,128]{2,1,0:T(8,128)} %bitcast.9), calls=%async_computation.1 | async-start | bytes 1048576 | tf_op jit(solution)/shard_map/all_to_all | solution.py:362
  42.8 17.6 %copy-start = (f32[12,128,128]{2,1,0:T(8,128)S(1)}, f32[12,128,128]{2,1,0:T(8,128)}, u32[]{:S(2)}) copy-start(f32[12,128,128]{2,1,0:T(8,128)} %nuc_ref.3) | copy-start | bytes 2359300
  42.8 17.6 %copy-start.7 = (f32[1,1,12,8]{2,3,1,0:T(8,128)S(1)}, f32[1,1,12,8]{2,3,1,0:T(8,128)}, u32[]{:S(2)}) copy-start(f32[1,1,12,8]{2,3,1,0:T(8,128)} %param.17) | copy-start | bytes 1156
  44.2 18.0 %collective-permute-start = (f32[16,24,128]{2,1,0:T(8,128)}, f32[16,24,128]{2,1,0:T(8,128)S(1)}, u32[]{:S(2)}, u32[]{:S(2)}) collective-permute-start(f32[16,24,128]{2,1,0:T(8,128)} %get-tuple-element.24), channel_id=1, source_target_pairs={{0,8},{8,0},{16,24},{24,16},{32,40},{40,32},{48,56},{56,48},{1,9},... | collective-permute-start | bytes 589832 | tf_op jit(solution)/shard_map/ppermute | solution.py:386
  47.1 15.1 %collective-permute-start.1 = (f32[16,24,128]{2,1,0:T(8,128)S(1)}, f32[16,24,128]{2,1,0:T(8,128)}, u32[]{:S(2)}, u32[]{:S(2)}) collective-permute-start(f32[16,24,128]{2,1,0:T(8,128)S(1)} %get-tuple-element.25), channel_id=1, source_target_pairs={{8,16},{16,8},{24,32},{32,24},{40,48},{48,40},{9,17},{17,9},{25,33... | collective-permute-start | bytes 589832 | tf_op jit(solution)/shard_map/ppermute | solution.py:388
  49.2 1.0 copy-start.11
  50.2 10.2 %copy-start.14 = (bf16[192,384]{1,0:T(8,128)(2,1)}, bf16[192,384]{1,0:T(8,128)(2,1)S(1)}, u32[]{:S(2)}) copy-start(bf16[192,384]{1,0:T(8,128)(2,1)S(1)} %get-tuple-element.26.v_ref) | copy-start | bytes 442372
  50.2 10.2 %copy-start.16 = (bf16[192,192]{1,0:T(8,128)(2,1)}, bf16[192,192]{1,0:T(8,128)(2,1)S(1)}, u32[]{:S(2)}) copy-start(bf16[192,192]{1,0:T(8,128)(2,1)S(1)} %get-tuple-element.22.v_ref) | copy-start | bytes 221188
  60.4 1.8 %copy-start.12 = (bf16[3,768,256]{2,1,0:T(8,128)(2,1)S(1)}, bf16[3,768,256]{2,1,0:T(8,128)(2,1)}, u32[]{:S(2)}) copy-start(bf16[3,768,256]{2,1,0:T(8,128)(2,1)} %copy-done.11) | copy-start | bytes 3538948
  60.4 1.8 %copy-start.13 = (f32[12,128,128]{2,1,0:T(8,128)S(1)}, f32[12,128,128]{2,1,0:T(8,128)}, u32[]{:S(2)}) copy-start(f32[12,128,128]{2,1,0:T(8,128)} %wave_ref.1) | copy-start | bytes 2359300
  61.3 1.1 copy-start.15
  62.3 5.1 %copy-start.10 = (s32[1,1,12]{2,1,0:T(1,128)S(1)}, s32[1,1,12]{2,1,0:T(1,128)}, u32[]{:S(2)}) copy-start(s32[1,1,12]{2,1,0:T(1,128)} %param.18) | copy-start | bytes 148
  62.3 5.1 %copy-start.17 = (bf16[192,192]{1,0:T(8,128)(2,1)S(1)}, bf16[192,192]{1,0:T(8,128)(2,1)}, u32[]{:S(2)}) copy-start(bf16[192,192]{1,0:T(8,128)(2,1)} %copy-done.16) | copy-start | bytes 221188
  71.5 22.5 %copy-start.4 = (f32[2,128,128]{2,1,0:T(8,128)S(1)}, f32[2,128,128]{2,1,0:T(8,128)}, u32[]{:S(2)}) copy-start(f32[2,128,128]{2,1,0:T(8,128)} %param.15) | copy-start | bytes 393220
  71.5 22.5 %copy-start.9 = (f32[1,1,8]{2,1,0:T(1,128)S(1)}, f32[1,1,8]{2,1,0:T(1,128)}, u32[]{:S(2)}) copy-start(f32[1,1,8]{2,1,0:T(1,128)} %param.16) | copy-start | bytes 100
  71.5 5.8 %collective-permute-start.2 = (f32[4,160,128]{2,1,0:T(8,128)S(1)}, f32[4,160,128]{2,1,0:T(8,128)S(1)}, u32[]{:S(2)}, u32[]{:S(2)}) collective-permute-start(f32[4,160,128]{2,1,0:T(8,128)S(1)} %get-tuple-element.31), channel_id=1, source_target_pairs={{0,64},{64,0},{128,192},{192,128},{256,320},{320,256},{384,448},{4... | collective-permute-start | bytes 983048 | tf_op jit(solution)/shard_map/ppermute | solution.py:421
  106.6 7.2 %collective-permute-start.3 = (f32[4,160,128]{2,1,0:T(8,128)S(1)}, f32[4,160,128]{2,1,0:T(8,128)S(1)}, u32[]{:S(2)}, u32[]{:S(2)}) collective-permute-start(f32[4,160,128]{2,1,0:T(8,128)S(1)} %all_to_all.22.own_ref), channel_id=1, source_target_pairs={{0,64},{64,0},{128,192},{192,128},{256,320},{320,256},{384,448},{4... | collective-permute-start | bytes 983048 | tf_op jit(solution)/shard_map/ppermute | solution.py:421

commit v6 on v4

--- a/solution.py
+++ b/solution.py
@@ -89,7 +89,7 @@
     return head, (values - head.astype(jnp.float32)).astype(jnp.bfloat16)
 
 
-def pack_kernel(rows_ref, out_ref, *, chans, facet_rows, facet_cols, deal):
+def pack_kernel(me_ref, rows_ref, out_ref, *, chans, facet_rows, facet_cols, deal):
     block = deal * (chans + chans // SLOTS)
     per_chan = deal * facet_rows * facet_cols
     for i in range(facet_rows):
@@ -124,7 +124,7 @@
 
 
 def prepare_kernel(me_ref, width_ref, rows_ref, centre_ref, sides_ref, v_ref, w_ref, pad):
-    odd = me_ref[1] % 2
+    odd = 1 - me_ref[1] % 2
     lane = lax.broadcasted_iota(jnp.int32, rows_ref.shape[1:], 1)
     first = jnp.where(odd == 1, FACET + EDGE - width_ref[0], EXT - width_ref[0])
     last = jnp.where(odd == 1, FACET + EDGE, FACET) + width_ref[0]
@@ -151,9 +151,7 @@
 def unpack_kernel(me_ref, in_ref, facet_ref, side_ref, first_ref, second_ref, *, chans, deal, senders):
     groups = chans // SLOTS
     block = deal * (chans + groups)
-    odd = me_ref[1] % 2
-    first = pl.ds(pl.multiple_of((FACET - EDGE) * (1 - odd), 8), EDGE)
-    second = pl.ds(pl.multiple_of((FACET - EDGE) * odd, 8), EDGE)
+    odd = 1 - me_ref[1] % 2
     for at in range(chans + groups):
         if at < chans:
             starts = [q * chans + at for q in range(deal)]
@@ -162,8 +160,9 @@
         rows = jnp.concatenate([in_ref[pl.ds(s, senders, stride=block), :] for s in starts], axis=0)
         held, place = (facet_ref, at) if at < chans else (side_ref, at - chans)
         held[place] = rows
-        first_ref[at] = held[place, first, :]
-        second_ref[at] = held[place, second, :]
+        top, bottom = rows[:EDGE], rows[FACET - EDGE :]
+        first_ref[at] = jnp.where(odd == 1, top, bottom)
+        second_ref[at] = jnp.where(odd == 1, bottom, top)
 
 
 def project_kernel(facet_ref, nuc_ref, basis_ref, combined_ref, out_ref, *, chans, rank):
@@ -200,14 +199,18 @@
         for g in range(groups)
     ]
     for slot in range(SLOTS):
+        taken = []
         for group in range(groups):
             ch = group * SLOTS + slot
-            rows = jnp.concatenate([facet_ref[ch], first_ref[ch], second_ref[ch]], axis=0)
-            head, tail = split(rows)
+            head, tail = split(jnp.concatenate([facet_ref[ch], first_ref[ch], second_ref[ch]], axis=0))
             side_head, side_tail = sides[group]
-            taken = jnp.concatenate([head, side_head, tail, side_tail, head, side_head], axis=1)
-            across = jnp.dot(taken, w_ref[slot], preferred_element_type=jnp.float32)
-            head, tail = split(across)
+            taken.append(jnp.concatenate([head, side_head, tail, side_tail, head, side_head], axis=1))
+        across = jnp.dot(
+            jnp.concatenate(taken, axis=0), w_ref[slot], preferred_element_type=jnp.float32
+        )
+        for group in range(groups):
+            ch = group * SLOTS + slot
+            head, tail = split(across[group * EXT : (group + 1) * EXT])
             stacked = jnp.concatenate([head, nothing, head, nothing, tail, nothing], axis=0)
             both = jnp.dot(v_ref[...], stacked, preferred_element_type=jnp.float32)
             upper = jnp.where(lane < half, both[:half, :LANES], both[half:FACET, :LANES])
@@ -311,8 +314,8 @@
     block = deal * (chans + groups)
     (packed,) = call(
         functools.partial(pack_kernel, chans=chans, facet_rows=rows, facet_cols=cols, deal=deal),
-        "pack", [VMEM], [f32(senders * block, LANES)],
-        [primal_slab.reshape(-1, LANES)],
+        "pack", [SMEM, VMEM], [f32(senders * block, LANES)],
+        [me, primal_slab.reshape(-1, LANES)],
     )
     arrived = lax.all_to_all(
         packed.reshape(senders, block, LANES), plane, split_axis=0, concat_axis=0, tiled=True
@@ -331,9 +334,9 @@
         [f32(chans, FACET, LANES), f32(groups, FACET, LANES), strip, strip],
         [me, arrived.reshape(-1, LANES)],
     )
-    first = lax.ppermute(first, "frow", [(i, i ^ 1) for i in range(rows)])
-    other = [(i, i - 1 if i % 2 == 0 else i + 1) for i in range(1, rows - 1)]
-    second = lax.ppermute(second, "frow", other)
+    inward = [(i, i - 1 if i % 2 == 0 else i + 1) for i in range(1, rows - 1)]
+    first = lax.ppermute(first, "frow", inward)
+    second = lax.ppermute(second, "frow", [(i, i ^ 1) for i in range(rows)])
     combined, partial = call(
         functools.partial(project_kernel, chans=chans, rank=rank),
         "project", [VMEM, VMEM, SMEM],

time: 108 us -> 106 us (0.981)
  the two profiles are of different devices: /device:TPU:3 before, /device:TPU:1 now
where the time goes in v6:
time: 106 us
  blocking collectives  73.1 us (69%)
  starting transfers between devices  16.4 us (15%)
  Pallas kernels  10.3 us (10%)
  waiting for transfers between devices  3.65 us (3%)
  local copies, waits for them, and re-layouts  1.19 us (1%)
    all_to_all x1, blocking collectives, shards(): lax.all_to_all(packed.reshape(senders, block, LANES), plane, split_axis=0...  43.7 us
    all_to_all x2, blocking collectives, across_chips(): lax.all_to_all(values, 'spec', split_axis=0, concat_axis=0, tiled=True, a...  29.4 us
    ppermute x2, starting transfers between devices, swap(): return lax.ppermute(values, 'spec', [(i, i ^ 1) for i in range(spec)])  12.3 us
    pallas_call x8, Pallas kernels, call(): pl.pallas_call(kernel, name=name, in_specs=ins, out_specs=places or [VMEM...  10.3 us
    ppermute x1, starting transfers between devices, shards(): second = lax.ppermute(second, 'frow', [(i, i ^ 1) for i in range(rows)])  3.28 us
    ppermute x2, waiting for transfers between devices, swap(): return lax.ppermute(values, 'spec', [(i, i ^ 1) for i in range(spec)])  2.47 us
  transfers between devices with their start and end apart: 4, of which 3 were waited for; matrix products, arithmetic and copies ran while one was open for 0% of the time, Pallas kernels for 2%

profile of v6, /device:TPU:1, one launch (start us, length us, event | category | flops | bytes accessed | tf_op | source)
XLA Modules:
  0.0 105.6 jit_solution(13522754510026673950)
XLA Ops:
  0.6 0.1 pad_add_fusion.me_ref
  0.7 1.1 %copy-done = f32[12,16,1,1,1024]{4,3,2,1,0:T(1,128)S(1)} copy-done((f32[12,16,1,1,1024]{4,3,2,1,0:T(1,128)S(1)}, f32[12,16,1,1,1024]{4,3,2,1,0:T(1,128)}, u32[]{:S(2)}) %copy-start) | copy-done | bytes 786456
  1.8 1.4 %pack.1 = f32[2048,128]{1,0:T(8,128)S(1)} custom-call(s32[2]{0:T(128)S(1)} %pad_add_fusion.me_ref, f32[1536,128]{1,0:T(8,128)S(1)} %bitcast.14), custom_call_target="tpu_custom_call" | custom-call | bytes 1835016 | tf_op jit(solution)/shard_map/pack/pallas_call | solution.py:280
  3.2 0.0 copy-start.2
  3.2 0.0 copy-start.4
  3.3 0.0 copy-start.5
  3.3 0.0 copy-start.7
  3.3 43.7 %all_to_all.15 = f32[64,32,128]{2,1,0:T(8,128)S(1)} all-to-all(f32[64,32,128]{2,1,0:T(8,128)S(1)} %bitcast.13), channel_id=1, replica_groups=mesh['spec'=8,'frow'=8,'fcol'=8] {'frow','fcol'}, dimensions={0} | all-to-all | bytes 2097152 | tf_op jit(solution)/shard_map/all_to_all | solution.py:320
  47.0 1.2 %unpack.1 = (f32[12,128,128]{2,1,0:T(8,128)S(1)}, f32[4,128,128]{2,1,0:T(8,128)S(1)}, f32[16,24,128]{2,1,0:T(8,128)S(1)}, f32[16,24,128]{2,1,0:T(8,128)S(1)}) custom-call(s32[2]{0:T(128)S(1)} %pad_add_fusion.me_ref, f32[2048,128]{1,0:T(8,128)S(1)} %bitcast.12), custom_call_target="tpu_custom_call" | custom-call | bytes 2490376 | tf_op jit(solution)/shard_map/unpack/pallas_call | solution.py:280
  48.2 0.0 copy-start.10
  48.2 0.8 collective-permute-start
  49.0 3.3 %collective-permute-start.1 = (f32[16,24,128]{2,1,0:T(8,128)S(1)}, f32[16,24,128]{2,1,0:T(8,128)S(1)}, u32[]{:S(2)}, u32[]{:S(2)}) collective-permute-start(f32[16,24,128]{2,1,0:T(8,128)S(1)} %get-tuple-element.17), channel_id=1, source_target_pairs={{0,8},{8,0},{16,24},{24,16},{32,40},{40,32},{48,56},{56,48},{1,9},... | collective-permute-start | bytes 589832 | tf_op jit(solution)/shard_map/ppermute | solution.py:339
  52.4 0.7 prepare.1
  53.1 1.2 %project.1 = (f32[12,128,128]{2,1,0:T(8,128)S(1)}, f32[8,128,128]{2,1,0:T(8,128)S(1)}) custom-call(f32[12,128,128]{2,1,0:T(8,128)S(1)} %get-tuple-element.13.facet_ref, f32[12,128,128]{2,1,0:T(8,128)S(1)} %copy-done.1, f32[8,12]{1,0:T(8,128)S(1)} %bitcast.16), custom_call_target="tpu_custom_call" | custom-call | flops 3145728 | bytes 2883968 | tf_op jit(solution)/shard_map/project/pallas_call | solution.py:280
  54.3 1.2 %collective-permute-done.1.second_ref = f32[16,24,128]{2,1,0:T(8,128)S(1)} collective-permute-done((f32[16,24,128]{2,1,0:T(8,128)S(1)}, f32[16,24,128]{2,1,0:T(8,128)S(1)}, u32[]{:S(2)}, u32[]{:S(2)}) %collective-permute-start.1) | collective-permute-done | bytes 196640 | tf_op jit(solution)/shard_map/ppermute | solution.py:339
  55.4 3.1 %wavelet.1 = (f32[12,128,128]{2,1,0:T(8,128)S(1)}, f32[4,160,128]{2,1,0:T(8,128)S(1)}, f32[4,160,128]{2,1,0:T(8,128)S(1)}) custom-call(s32[2]{0:T(128)S(1)} %pad_add_fusion.me_ref, s32[12]{0:T(128)S(1)} %bitcast.20, f32[12,128,128]{2,1,0:T(8,128)S(1)} %get-tuple-element.13.facet_ref, f32[4,128,128]{2,1,0:T(8,128)S(1)} %get-tuple-element.15.side_ref, ...), custom_call_target="tpu_custom_call" | custom-call | flops 2123366400 | bytes 7143480 | tf_op jit(solution)/shard_map/wavelet/pallas_call | solution.py:280
  58.6 5.9 %collective-permute-start.2 = (f32[4,160,128]{2,1,0:T(8,128)S(1)}, f32[4,160,128]{2,1,0:T(8,128)S(1)}, u32[]{:S(2)}, u32[]{:S(2)}) collective-permute-start(f32[4,160,128]{2,1,0:T(8,128)S(1)} %get-tuple-element.23), channel_id=1, source_target_pairs={{0,64},{64,0},{128,192},{192,128},{256,320},{320,256},{384,448},{4... | collective-permute-start | bytes 983048 | tf_op jit(solution)/shard_map/ppermute | solution.py:362
  64.5 1.2 %collective-permute-done.2.came_ref = f32[4,160,128]{2,1,0:T(8,128)S(1)} collective-permute-done((f32[4,160,128]{2,1,0:T(8,128)S(1)}, f32[4,160,128]{2,1,0:T(8,128)S(1)}, u32[]{:S(2)}, u32[]{:S(2)}) %collective-permute-start.2) | collective-permute-done | bytes 327712 | tf_op jit(solution)/shard_map/ppermute | solution.py:362
  65.8 15.4 %all_to_all.16.parts_ref = f32[4,160,128]{2,1,0:T(8,128)S(1)} all-to-all(f32[4,160,128]{2,1,0:T(8,128)S(1)} %pair.1), channel_id=1, replica_groups={{0,128,256,384},{64,192,320,448},{1,129,257,385},{65,193,321,449},{2,13..., dimensions={0} | all-to-all | bytes 655360 | tf_op jit(solution)/shard_map/all_to_all | solution.py:366
  81.2 0.7 weigh.1
  81.9 14.0 %all_to_all.17.own_ref = f32[4,160,128]{2,1,0:T(8,128)S(1)} all-to-all(f32[4,160,128]{2,1,0:T(8,128)S(1)} %weigh.1), channel_id=1, replica_groups={{0,128,256,384},{64,192,320,448},{1,129,257,385},{65,193,321,449},{2,13..., dimensions={0} | all-to-all | bytes 655360 | tf_op jit(solution)/shard_map/all_to_all | solution.py:366
  95.9 6.5 %collective-permute-start.3 = (f32[4,160,128]{2,1,0:T(8,128)S(1)}, f32[4,160,128]{2,1,0:T(8,128)S(1)}, u32[]{:S(2)}, u32[]{:S(2)}) collective-permute-start(f32[4,160,128]{2,1,0:T(8,128)S(1)} %all_to_all.17.own_ref), channel_id=1, source_target_pairs={{0,64},{64,0},{128,192},{192,128},{256,320},{320,256},{384,448},{4... | collective-permute-start | bytes 983048 | tf_op jit(solution)/shard_map/ppermute | solution.py:362
  102.4 1.2 %collective-permute-done.3.other_ref = f32[4,160,128]{2,1,0:T(8,128)S(1)} collective-permute-done((f32[4,160,128]{2,1,0:T(8,128)S(1)}, f32[4,160,128]{2,1,0:T(8,128)S(1)}, u32[]{:S(2)}, u32[]{:S(2)}) %collective-permute-start.3) | collective-permute-done | bytes 327712 | tf_op jit(solution)/shard_map/ppermute | solution.py:362
  103.6 2.0 %finish.1 = (f32[12,128,128]{2,1,0:T(8,128)}, f32[12,128,128]{2,1,0:T(8,128)}) custom-call(s32[2]{0:T(128)S(1)} %pad_add_fusion.me_ref, s32[12]{0:T(128)S(1)} %bitcast.21, f32[8,12]{1,0:T(8,128)S(1)} %bitcast.17, f32[12,128,128]{2,1,0:T(8,128)S(1)} %get-tuple-element.14.combined_ref, f32[12,128,128]{2,1,0:T(8,128)S(1)} %get-tuple-element.21.dual_ref, ...), custom_call_target="tpu_custom_call" | custom-call | flops 3145728 | bytes 3801528 | tf_op jit(solution)/shard_map/finish/pallas_call | solution.py:280
  (18 shorter events, 0.1 us)
Async XLA Ops:
  0.7 1.1 %copy-start = (f32[12,16,1,1,1024]{4,3,2,1,0:T(1,128)S(1)}, f32[12,16,1,1,1024]{4,3,2,1,0:T(1,128)}, u32[]{:S(2)}) copy-start(f32[12,16,1,1,1024]{4,3,2,1,0:T(1,128)} %param.11) | copy-start | bytes 2359300
  3.2 49.1 %copy-start.2 = (f32[2,192,256]{2,1,0:T(8,128)S(1)}, f32[2,192,256]{2,1,0:T(8,128)}, u32[]{:S(2)}) copy-start(f32[2,192,256]{2,1,0:T(8,128)} %constant.15.clone.rows_ref) | copy-start | bytes 1179652
  3.2 49.1 %copy-start.4 = (f32[128,256]{1,0:T(8,128)S(1)}, f32[128,256]{1,0:T(8,128)}, u32[]{:S(2)}) copy-start(f32[128,256]{1,0:T(8,128)} %constant.16.clone.centre_ref) | copy-start | bytes 393220
  3.3 49.1 %copy-start.5 = (f32[2,24,256]{2,1,0:T(8,128)S(1)}, f32[2,24,256]{2,1,0:T(8,128)}, u32[]{:S(2)}) copy-start(f32[2,24,256]{2,1,0:T(8,128)} %constant.17.clone.sides_ref) | copy-start | bytes 147460
  3.3 49.1 %copy-start.7 = (s32[1,1,2]{2,1,0:T(1,128)S(1)}, s32[1,1,2]{2,1,0:T(1,128)}, u32[]{:S(2)}) copy-start(s32[1,1,2]{2,1,0:T(1,128)} %param.18) | copy-start | bytes 28
  47.0 6.1 %copy-start.1 = (f32[12,128,128]{2,1,0:T(8,128)S(1)}, f32[12,128,128]{2,1,0:T(8,128)}, u32[]{:S(2)}) copy-start(f32[12,128,128]{2,1,0:T(8,128)} %nuc_ref.1) | copy-start | bytes 2359300
  47.0 6.1 %copy-start.6 = (f32[1,1,12,8]{2,3,1,0:T(8,128)S(1)}, f32[1,1,12,8]{2,3,1,0:T(8,128)}, u32[]{:S(2)}) copy-start(f32[1,1,12,8]{2,3,1,0:T(8,128)} %param.16) | copy-start | bytes 1156
  48.2 7.3 %copy-start.9 = (s32[1,1,12]{2,1,0:T(1,128)S(1)}, s32[1,1,12]{2,1,0:T(1,128)}, u32[]{:S(2)}) copy-start(s32[1,1,12]{2,1,0:T(1,128)} %param.17) | copy-start | bytes 148
  48.2 7.2 %copy-start.10 = (f32[12,128,128]{2,1,0:T(8,128)S(1)}, f32[12,128,128]{2,1,0:T(8,128)}, u32[]{:S(2)}) copy-start(f32[12,128,128]{2,1,0:T(8,128)} %wave_ref.1) | copy-start | bytes 2359300
  48.2 6.0 %collective-permute-start = (f32[16,24,128]{2,1,0:T(8,128)S(1)}, f32[16,24,128]{2,1,0:T(8,128)S(1)}, u32[]{:S(2)}, u32[]{:S(2)}) collective-permute-start(f32[16,24,128]{2,1,0:T(8,128)S(1)} %get-tuple-element.16), channel_id=1, source_target_pairs={{8,16},{16,8},{24,32},{32,24},{40,48},{48,40},{9,17},{17,9},{25,33... | collective-permute-start | bytes 589832 | tf_op jit(solution)/shard_map/ppermute | solution.py:338
  49.0 6.4 %collective-permute-start.1 = (f32[16,24,128]{2,1,0:T(8,128)S(1)}, f32[16,24,128]{2,1,0:T(8,128)S(1)}, u32[]{:S(2)}, u32[]{:S(2)}) collective-permute-start(f32[16,24,128]{2,1,0:T(8,128)S(1)} %get-tuple-element.17), channel_id=1, source_target_pairs={{0,8},{8,0},{16,24},{24,16},{32,40},{40,32},{48,56},{56,48},{1,9},... | collective-permute-start | bytes 589832 | tf_op jit(solution)/shard_map/ppermute | solution.py:339
  58.6 22.6 %copy-start.3 = (f32[2,128,128]{2,1,0:T(8,128)S(1)}, f32[2,128,128]{2,1,0:T(8,128)}, u32[]{:S(2)}) copy-start(f32[2,128,128]{2,1,0:T(8,128)} %param.14) | copy-start | bytes 393220
  58.6 22.6 %copy-start.8 = (f32[1,1,8]{2,1,0:T(1,128)S(1)}, f32[1,1,8]{2,1,0:T(1,128)}, u32[]{:S(2)}) copy-start(f32[1,1,8]{2,1,0:T(1,128)} %param.15) | copy-start | bytes 100
  58.6 7.1 %collective-permute-start.2 = (f32[4,160,128]{2,1,0:T(8,128)S(1)}, f32[4,160,128]{2,1,0:T(8,128)S(1)}, u32[]{:S(2)}, u32[]{:S(2)}) collective-permute-start(f32[4,160,128]{2,1,0:T(8,128)S(1)} %get-tuple-element.23), channel_id=1, source_target_pairs={{0,64},{64,0},{128,192},{192,128},{256,320},{320,256},{384,448},{4... | collective-permute-start | bytes 983048 | tf_op jit(solution)/shard_map/ppermute | solution.py:362
  95.9 7.7 %collective-permute-start.3 = (f32[4,160,128]{2,1,0:T(8,128)S(1)}, f32[4,160,128]{2,1,0:T(8,128)S(1)}, u32[]{:S(2)}, u32[]{:S(2)}) collective-permute-start(f32[4,160,128]{2,1,0:T(8,128)S(1)} %all_to_all.17.own_ref), channel_id=1, source_target_pairs={{0,64},{64,0},{128,192},{192,128},{256,320},{320,256},{384,448},{4... | collective-permute-start | bytes 983048 | tf_op jit(solution)/shard_map/ppermute | solution.py:362

commit v7 on v6

--- a/solution.py
+++ b/solution.py
@@ -165,7 +165,10 @@
         second_ref[at] = jnp.where(odd == 1, bottom, top)
 
 
-def project_kernel(facet_ref, nuc_ref, basis_ref, combined_ref, out_ref, *, chans, rank):
+def project_kernel(
+    me_ref, facet_ref, nuc_ref, basis_ref, combined_ref, own_ref, other_ref, *, chans, rank
+):
+    even = me_ref[0] % 2 == 0
     for part in range(0, FACET, 32):
         rows = pl.ds(part, 32)
         total = [None] * rank
@@ -175,20 +178,16 @@
             for k in range(rank):
                 term = basis_ref[k, ch] * block
                 total[k] = term if total[k] is None else total[k] + term
-        for k in range(rank):
-            out_ref[k, rows, :] = total[k]
+        for chip in range(rank // 2):
+            first, second = total[2 * chip], total[2 * chip + 1]
+            own_ref[chip, rows, :] = jnp.where(even, first, second)
+            other_ref[chip, rows, :] = jnp.where(even, second, first)
 
 
 def wavelet_kernel(
-    me_ref, band_ref, facet_ref, side_ref, first_ref, second_ref, v_ref, w_ref, partial_ref, wave_ref,
+    me_ref, band_ref, facet_ref, side_ref, first_ref, second_ref, v_ref, w_ref, wave_ref,
     out_ref, own_ref, other_ref, squares, *, chans,
 ):
-    core = me_ref[0] % 2
-    chips = own_ref.shape[0]
-    share = own_ref.shape[1] - FACET
-    for chip in range(chips):
-        own_ref[chip, :FACET, :] = partial_ref[2 * chip + core]
-        other_ref[chip, :FACET, :] = partial_ref[2 * chip + 1 - core]
     squares[...] = jnp.zeros_like(squares)
     groups = chans // SLOTS
     half = FACET // 2
@@ -219,56 +218,60 @@
             out_ref[ch] = dual
             rows = pl.ds(pl.multiple_of(band_ref[ch] * FACET, FACET), FACET)
             squares[rows, :] = squares[rows, :] + dual * dual
-    for chip in range(chips):
-        first = pl.multiple_of((2 * chip + core) * share, share)
-        own_ref[chip, FACET:, :] = squares[pl.ds(first, share), :]
-        first = pl.multiple_of((2 * chip + 1 - core) * share, share)
-        other_ref[chip, FACET:, :] = squares[pl.ds(first, share), :]
+    core = me_ref[0] % 2
+    own_ref[...] = squares[pl.ds(pl.multiple_of(core * FACET, FACET), FACET), :]
+    other_ref[...] = squares[pl.ds(pl.multiple_of((1 - core) * FACET, FACET), FACET), :]
 
 
 def pair_kernel(own_ref, came_ref, out_ref):
     out_ref[...] = own_ref[...] + came_ref[...]
 
 
-def weigh_kernel(me_ref, thresh_ref, weight_ref, parts_ref, out_ref):
+def weigh_kernel(me_ref, thresh_ref, parts_ref, own_ref, came_ref, out_ref):
     chips = parts_ref.shape[0]
-    total = parts_ref[0]
+    spectrum = parts_ref[0]
     for chip in range(1, chips):
-        total = total + parts_ref[chip]
-    spectrum, squares = total[:FACET], total[FACET:]
+        spectrum = spectrum + parts_ref[chip]
     threshold = thresh_ref[me_ref[0]]
     singular = jnp.sqrt(jnp.sum(spectrum * spectrum, keepdims=True))
     scaled = spectrum * (1.0 - threshold / jnp.maximum(singular, threshold))
-    weight = weight_ref[me_ref[0]]
-    ratio = weight / jnp.maximum(jnp.sqrt(squares), weight)
+    squares = own_ref[...] + came_ref[...]
     for chip in range(chips):
         out_ref[chip, :FACET] = scaled
-        out_ref[chip, FACET:] = ratio
+        out_ref[chip, FACET:] = squares
+
+
+def ratio_kernel(me_ref, weight_ref, parts_ref, out_ref):
+    chips = parts_ref.shape[0]
+    squares = parts_ref[0, FACET:]
+    for chip in range(1, chips):
+        squares = squares + parts_ref[chip, FACET:]
+    weight = weight_ref[me_ref[0] % 2]
+    for chip in range(chips):
+        out_ref[chip] = parts_ref[chip, :FACET]
+    out_ref[chips] = weight / jnp.maximum(jnp.sqrt(squares), weight)
 
 
 def finish_kernel(
     me_ref, band_ref, basis_ref, combined_ref, dual_ref, own_ref, other_ref, wave_ref, nuc_ref,
     ordered, wave, nuc, sems, *, chans, rank,
 ):
-    core, chips = me_ref[0] % 2, own_ref.shape[0]
-    for chip in range(chips):
-        ordered[2 * chip + core] = own_ref[chip]
-        ordered[2 * chip + 1 - core] = other_ref[chip]
-    share = ordered.shape[1] - FACET
-    pieces = FACET // share
+    core, places = me_ref[0] % 2, own_ref.shape[0]
+    for place in range(places):
+        ordered[2 * place + core] = own_ref[place]
+        ordered[2 * place + 1 - core] = other_ref[place]
     copies = []
-    for part in range(pieces):
-        rows = pl.ds(part * share, share)
+    for step, start in enumerate(range(0, FACET, 32)):
+        rows = pl.ds(start, 32)
         scaled = [ordered[k, rows, :] for k in range(rank)]
         for ch in range(chans):
             total = basis_ref[0, ch] * scaled[0]
             for k in range(1, rank):
                 total = total + basis_ref[k, ch] * scaled[k]
             nuc[ch, rows, :] = combined_ref[ch, rows, :] - total
-            ratio = ordered[band_ref[ch] * pieces + part, FACET:, :]
-            wave[ch, rows, :] = dual_ref[ch, rows, :] * ratio
-        for place, (held, out) in enumerate(((nuc, nuc_ref), (wave, wave_ref))):
-            copy = pltpu.make_async_copy(held.at[:, rows, :], out.at[:, rows, :], sems.at[place, part])
+            wave[ch, rows, :] = dual_ref[ch, rows, :] * ordered[rank + band_ref[ch], rows, :]
+        for kind, (held, out) in enumerate(((nuc, nuc_ref), (wave, wave_ref))):
+            copy = pltpu.make_async_copy(held.at[:, rows, :], out.at[:, rows, :], sems.at[kind, step])
             copy.start()
             copies.append(copy)
     for copy in copies:
@@ -337,26 +340,8 @@
     inward = [(i, i - 1 if i % 2 == 0 else i + 1) for i in range(1, rows - 1)]
     first = lax.ppermute(first, "frow", inward)
     second = lax.ppermute(second, "frow", [(i, i ^ 1) for i in range(rows)])
-    combined, partial = call(
-        functools.partial(project_kernel, chans=chans, rank=rank),
-        "project", [VMEM, VMEM, SMEM],
-        [f32(chans, FACET, LANES), f32(rank, FACET, LANES)],
-        [facet, nuc_dual, local_basis],
-        flops=2 * chans * rank * FACET * LANES,
-    )
-    share = bands * FACET // spec
     chips = spec // 2
-    chunks = f32(chips, FACET + share, LANES)
-    dual_sum, own, other = call(
-        functools.partial(wavelet_kernel, chans=chans),
-        "wavelet", [SMEM, SMEM] + [VMEM] * 8,
-        [f32(chans, FACET, LANES), chunks, chunks],
-        [me, bands_here, facet, side, first, second, vertical, across, partial, wave_dual],
-        scratch=[
-            pltpu.VMEM((bands * FACET, LANES), jnp.float32),
-        ],
-        flops=2 * chans * 3 * 192 * 256 * 600,
-    )
+    plane_sums, ranks = f32(FACET, LANES), f32(chips, FACET, LANES)
 
     def swap(values):
         return lax.ppermute(values, "spec", [(i, i ^ 1) for i in range(spec)])
@@ -367,22 +352,41 @@
             values, "spec", split_axis=0, concat_axis=0, tiled=True, axis_index_groups=cores
         )
 
-    (sums,) = call(pair_kernel, "pair", [VMEM, VMEM], [chunks], [own, swap(other)])
+    combined, own, other = call(
+        functools.partial(project_kernel, chans=chans, rank=rank),
+        "project", [SMEM, VMEM, VMEM, SMEM],
+        [f32(chans, FACET, LANES), ranks, ranks],
+        [me, facet, nuc_dual, local_basis],
+        flops=2 * chans * rank * FACET * LANES,
+    )
+    (sums,) = call(pair_kernel, "pair", [VMEM, VMEM], [ranks], [own, swap(other)])
+    parts = across_chips(sums)
+    dual_sum, own, other = call(
+        functools.partial(wavelet_kernel, chans=chans),
+        "wavelet", [SMEM, SMEM] + [VMEM] * 7,
+        [f32(chans, FACET, LANES), plane_sums, plane_sums],
+        [me, bands_here, facet, side, first, second, vertical, across, wave_dual],
+        scratch=[pltpu.VMEM((bands * FACET, LANES), jnp.float32)],
+        flops=2 * chans * 3 * 192 * 256 * 600,
+    )
     (weighed,) = call(
-        weigh_kernel, "weigh", [SMEM, SMEM, VMEM, VMEM], [chunks],
-        [me, nuc_thresh.reshape(rank), l21_weights.reshape(spec, share, LANES), across_chips(sums)],
-    )
-    own = across_chips(weighed)
+        weigh_kernel, "weigh", [SMEM, SMEM, VMEM, VMEM, VMEM], [f32(chips, 2 * FACET, LANES)],
+        [me, nuc_thresh.reshape(rank), parts, own, swap(other)],
+    )
+    (own,) = call(
+        ratio_kernel, "ratio", [SMEM, VMEM, VMEM], [f32(chips + 1, FACET, LANES)],
+        [me, l21_weights, across_chips(weighed)],
+    )
     wave_new, nuc_new = call(
         functools.partial(finish_kernel, chans=chans, rank=rank),
         "finish", [SMEM, SMEM, SMEM] + [VMEM] * 4,
         [f32(chans, FACET, LANES), f32(chans, FACET, LANES)],
         [me, bands_here, local_basis, combined, dual_sum, own, swap(own)],
         scratch=[
-            pltpu.VMEM((spec, FACET + share, LANES), jnp.float32),
+            pltpu.VMEM((rank + bands, FACET, LANES), jnp.float32),
             pltpu.VMEM((chans, FACET, LANES), jnp.float32),
             pltpu.VMEM((chans, FACET, LANES), jnp.float32),
-            pltpu.SemaphoreType.DMA((2, FACET // share)),
+            pltpu.SemaphoreType.DMA((2, FACET // 32)),
         ],
         flops=2 * chans * rank * FACET * LANES,
         places=[HBM, HBM],

time: 106 us -> 107 us (level)
  blocking collectives: 73.1 us -> 63.9 us
  starting transfers between devices: 16.4 us -> 23.6 us
  Pallas kernels: 10.3 us -> 12.8 us
  local copies, waits for them, and re-layouts: 1.19 us -> 2.84 us
  waiting for transfers between devices: 3.65 us -> 2.12 us
    all_to_all x2 -> x1, blocking collectives: 29.4 us -> 20.3 us  [across_chips(): lax.all_to_all(values, 'spec', split_axis=0, concat_axis=0, tiled=True, a...]
    all_to_all x0 -> x1, starting transfers between devices: none -> 5.91 us  [across_chips(): lax.all_to_all(values, 'spec', split_axis=0, concat_axis=0, tiled=True, a...]
    pallas_call x8 -> x9, Pallas kernels: 10.3 us -> 12.8 us  [call(): pl.pallas_call(kernel, name=name, in_specs=ins, out_specs=places or [VMEM...]
    unnamed x22 -> x26, local copies, waits for them, and re-layouts: 1.19 us -> 2.84 us
    ppermute x1, waiting for transfers between devices: 1.18 us -> 0.01 us  [shards(): second = lax.ppermute(second, 'frow', [(i, i ^ 1) for i in range(rows)])]
    ppermute x2 -> x3, starting transfers between devices: 12.3 us -> 13.5 us  [swap(): return lax.ppermute(values, 'spec', [(i, i ^ 1) for i in range(spec)])]
    ppermute x2 -> x3, waiting for transfers between devices: 2.47 us -> 2.12 us  [swap(): return lax.ppermute(values, 'spec', [(i, i ^ 1) for i in range(spec)])]
  transfers between devices with their start and end apart: 4 -> 6, of which waited for: 3 -> 2; matrix products, arithmetic and copies ran while one was open for 0% -> 0% of each run, Pallas kernels for 2% -> 5%
where the time goes in v7:
time: 107 us; the launch traced here: 106 us
  blocking collectives  63.9 us (60%)
  starting transfers between devices  23.6 us (22%)
  Pallas kernels  12.8 us (12%)
  local copies, waits for them, and re-layouts  2.84 us (3%)
  waiting for transfers between devices  2.12 us (2%)
    all_to_all x1, blocking collectives, shards(): lax.all_to_all(packed.reshape(senders, block, LANES), plane, split_axis=0...  43.7 us
    all_to_all x1, blocking collectives, across_chips(): lax.all_to_all(values, 'spec', split_axis=0, concat_axis=0, tiled=True, a...  20.3 us
    ppermute x3, starting transfers between devices, swap(): return lax.ppermute(values, 'spec', [(i, i ^ 1) for i in range(spec)])  13.5 us
    pallas_call x9, Pallas kernels, call(): pl.pallas_call(kernel, name=name, in_specs=ins, out_specs=places or [VMEM...  12.8 us
    all_to_all x1, starting transfers between devices, across_chips(): lax.all_to_all(values, 'spec', split_axis=0, concat_axis=0, tiled=True, a...  5.91 us
    unnamed x26, local copies, waits for them, and re-layouts  2.84 us
    ppermute x1, starting transfers between devices, shards(): second = lax.ppermute(second, 'frow', [(i, i ^ 1) for i in range(rows)])  2.83 us
  transfers between devices with their start and end apart: 6, of which 2 were waited for; matrix products, arithmetic and copies ran while one was open for 0% of the time, Pallas kernels for 5%

profile of v7, /device:TPU:1, one launch (start us, length us, event | category | flops | bytes accessed | tf_op | source)
XLA Modules:
  0.0 106.2 jit_solution(8351290019025040468)
XLA Ops:
  0.6 0.1 pad_add_fusion.me_ref
  0.7 1.1 %copy-done = f32[12,16,1,1,1024]{4,3,2,1,0:T(1,128)S(1)} copy-done((f32[12,16,1,1,1024]{4,3,2,1,0:T(1,128)S(1)}, f32[12,16,1,1,1024]{4,3,2,1,0:T(1,128)}, u32[]{:S(2)}) %copy-start) | copy-done | bytes 786456
  1.8 1.4 %pack.1 = f32[2048,128]{1,0:T(8,128)S(1)} custom-call(s32[2]{0:T(128)S(1)} %pad_add_fusion.me_ref, f32[1536,128]{1,0:T(8,128)S(1)} %bitcast.13), custom_call_target="tpu_custom_call" | custom-call | bytes 1835016 | tf_op jit(solution)/shard_map/pack/pallas_call | solution.py:283
  3.3 43.7 %all_to_all.15 = f32[64,32,128]{2,1,0:T(8,128)S(1)} all-to-all(f32[64,32,128]{2,1,0:T(8,128)S(1)} %bitcast.12), channel_id=1, replica_groups=mesh['spec'=8,'frow'=8,'fcol'=8] {'frow','fcol'}, dimensions={0} | all-to-all | bytes 2097152 | tf_op jit(solution)/shard_map/all_to_all | solution.py:323
  46.9 1.9 %unpack.1 = (f32[12,128,128]{2,1,0:T(8,128)S(1)}, f32[4,128,128]{2,1,0:T(8,128)S(1)}, f32[16,24,128]{2,1,0:T(8,128)}, f32[16,24,128]{2,1,0:T(8,128)}) custom-call(s32[2]{0:T(128)S(1)} %pad_add_fusion.me_ref, f32[2048,128]{1,0:T(8,128)S(1)} %bitcast.11), custom_call_target="tpu_custom_call" | custom-call | bytes 2490376 | tf_op jit(solution)/shard_map/unpack/pallas_call | solution.py:283
  48.8 0.7 copy-done.11
  49.6 0.0 copy-start.5
  49.6 1.1 %project.1 = (f32[12,128,128]{2,1,0:T(8,128)S(1)}, f32[4,128,128]{2,1,0:T(8,128)S(1)}, f32[4,128,128]{2,1,0:T(8,128)S(1)}) custom-call(s32[2]{0:T(128)S(1)} %pad_add_fusion.me_ref, f32[12,128,128]{2,1,0:T(8,128)S(1)} %get-tuple-element.14.facet_ref, f32[12,128,128]{2,1,0:T(8,128)S(1)} %copy-done.1, f32[8,12]{1,0:T(8,128)S(1)} %bitcast.14), custom_call_target="tpu_custom_call" | custom-call | flops 3145728 | bytes 2883976 | tf_op jit(solution)/shard_map/project/pallas_call | solution.py:283
  50.8 4.7 %collective-permute-start.2 = (f32[4,128,128]{2,1,0:T(8,128)S(1)}, f32[4,128,128]{2,1,0:T(8,128)S(1)}, u32[]{:S(2)}, u32[]{:S(2)}) collective-permute-start(f32[4,128,128]{2,1,0:T(8,128)S(1)} %get-tuple-element.23), channel_id=1, source_target_pairs={{0,64},{64,0},{128,192},{192,128},{256,320},{320,256},{384,448},{4... | collective-permute-start | bytes 786440 | tf_op jit(solution)/shard_map/ppermute | solution.py:347
  55.5 1.3 %collective-permute-start = (f32[16,24,128]{2,1,0:T(8,128)}, f32[16,24,128]{2,1,0:T(8,128)}, u32[]{:S(2)}, u32[]{:S(2)}) collective-permute-start(f32[16,24,128]{2,1,0:T(8,128)} %get-tuple-element.17), channel_id=1, source_target_pairs={{8,16},{16,8},{24,32},{32,24},{40,48},{48,40},{9,17},{17,9},{25,33... | collective-permute-start | bytes 589832 | tf_op jit(solution)/shard_map/ppermute | solution.py:341
  56.9 2.8 %collective-permute-start.1 = (f32[16,24,128]{2,1,0:T(8,128)}, f32[16,24,128]{2,1,0:T(8,128)}, u32[]{:S(2)}, u32[]{:S(2)}) collective-permute-start(f32[16,24,128]{2,1,0:T(8,128)} %get-tuple-element.18), channel_id=1, source_target_pairs={{0,8},{8,0},{16,24},{24,16},{32,40},{40,32},{48,56},{56,48},{1,9},... | collective-permute-start | bytes 589832 | tf_op jit(solution)/shard_map/ppermute | solution.py:342
  59.7 0.7 pair.1
  60.4 5.9 %all-to-all-start.1 = ((f32[4,128,128]{2,1,0:T(8,128)}), f32[4,128,128]{2,1,0:T(8,128)S(1)}, u32[]{:S(2)}, u32[]{:S(2)}) async-start(f32[4,128,128]{2,1,0:T(8,128)} %pair.1), calls=%async_computation.1 | async-start | bytes 524288 | tf_op jit(solution)/shard_map/all_to_all | solution.py:351
  66.4 0.7 prepare.1
  67.1 0.9 copy-done.12
  68.1 3.6 %wavelet.1 = (f32[12,128,128]{2,1,0:T(8,128)S(1)}, f32[128,128]{1,0:T(8,128)S(1)}, f32[128,128]{1,0:T(8,128)S(1)}) custom-call(s32[2]{0:T(128)S(1)} %pad_add_fusion.me_ref, s32[12]{0:T(128)S(1)} %bitcast.18, f32[12,128,128]{2,1,0:T(8,128)S(1)} %get-tuple-element.14.facet_ref, f32[4,128,128]{2,1,0:T(8,128)S(1)} %copy-done.12, ...), custom_call_target="tpu_custom_call" | custom-call | flops 2123366400 | bytes 6094904 | tf_op jit(solution)/shard_map/wavelet/pallas_call | solution.py:283
  71.7 2.6 %collective-permute-start.3 = (f32[128,128]{1,0:T(8,128)S(1)}, f32[128,128]{1,0:T(8,128)S(1)}, u32[]{:S(2)}, u32[]{:S(2)}) collective-permute-start(f32[128,128]{1,0:T(8,128)S(1)} %get-tuple-element.25), channel_id=1, source_target_pairs={{0,64},{64,0},{128,192},{192,128},{256,320},{320,256},{384,448},{4... | collective-permute-start | bytes 196616 | tf_op jit(solution)/shard_map/ppermute | solution.py:347
  74.3 0.9 collective-permute-done.3.came_ref
  75.2 0.7 weigh.1
  75.9 20.3 %all_to_all.16.parts_ref = f32[4,256,128]{2,1,0:T(8,128)S(1)} all-to-all(f32[4,256,128]{2,1,0:T(8,128)S(1)} %weigh.1), channel_id=1, replica_groups={{0,128,256,384},{64,192,320,448},{1,129,257,385},{65,193,321,449},{2,13..., dimensions={0} | all-to-all | bytes 1048576 | tf_op jit(solution)/shard_map/all_to_all | solution.py:351
  96.2 0.6 ratio.1.own_ref
  96.8 6.1 %collective-permute-start.4 = (f32[5,128,128]{2,1,0:T(8,128)S(1)}, f32[5,128,128]{2,1,0:T(8,128)S(1)}, u32[]{:S(2)}, u32[]{:S(2)}) collective-permute-start(f32[5,128,128]{2,1,0:T(8,128)S(1)} %ratio.1.own_ref), channel_id=1, source_target_pairs={{0,64},{64,0},{128,192},{192,128},{256,320},{320,256},{384,448},{4... | collective-permute-start | bytes 983048 | tf_op jit(solution)/shard_map/ppermute | solution.py:347
  102.9 1.2 %collective-permute-done.4.other_ref = f32[5,128,128]{2,1,0:T(8,128)S(1)} collective-permute-done((f32[5,128,128]{2,1,0:T(8,128)S(1)}, f32[5,128,128]{2,1,0:T(8,128)S(1)}, u32[]{:S(2)}, u32[]{:S(2)}) %collective-permute-start.4) | collective-permute-done | bytes 327712 | tf_op jit(solution)/shard_map/ppermute | solution.py:347
  104.2 2.0 %finish.1 = (f32[12,128,128]{2,1,0:T(8,128)}, f32[12,128,128]{2,1,0:T(8,128)}) custom-call(s32[2]{0:T(128)S(1)} %pad_add_fusion.me_ref, s32[12]{0:T(128)S(1)} %bitcast.19, f32[8,12]{1,0:T(8,128)S(1)} %bitcast.15, f32[12,128,128]{2,1,0:T(8,128)S(1)} %get-tuple-element.15.combined_ref, f32[12,128,128]{2,1,0:T(8,128)S(1)} %get-tuple-element.21.dual_ref, ...), custom_call_target="tpu_custom_call" | custom-call | flops 3145728 | bytes 3801528 | tf_op jit(solution)/shard_map/finish/pallas_call | solution.py:283
  (26 shorter events, 0.1 us)
Async XLA Ops:
  0.7 1.1 %copy-start = (f32[12,16,1,1,1024]{4,3,2,1,0:T(1,128)S(1)}, f32[12,16,1,1,1024]{4,3,2,1,0:T(1,128)}, u32[]{:S(2)}) copy-start(f32[12,16,1,1,1024]{4,3,2,1,0:T(1,128)} %param.11) | copy-start | bytes 2359300
  3.2 46.3 %copy-start.1 = (f32[12,128,128]{2,1,0:T(8,128)S(1)}, f32[12,128,128]{2,1,0:T(8,128)}, u32[]{:S(2)}) copy-start(f32[12,128,128]{2,1,0:T(8,128)} %nuc_ref.1) | copy-start | bytes 2359300
  3.2 46.3 %copy-start.6 = (f32[1,1,12,8]{2,3,1,0:T(8,128)S(1)}, f32[1,1,12,8]{2,3,1,0:T(8,128)}, u32[]{:S(2)}) copy-start(f32[1,1,12,8]{2,3,1,0:T(8,128)} %param.16) | copy-start | bytes 1156
  48.8 0.7 copy-start.11
  49.6 16.8 %copy-start.2 = (f32[2,192,256]{2,1,0:T(8,128)S(1)}, f32[2,192,256]{2,1,0:T(8,128)}, u32[]{:S(2)}) copy-start(f32[2,192,256]{2,1,0:T(8,128)} %constant.15.clone.rows_ref) | copy-start | bytes 1179652
  49.6 16.8 %copy-start.4 = (f32[128,256]{1,0:T(8,128)S(1)}, f32[128,256]{1,0:T(8,128)}, u32[]{:S(2)}) copy-start(f32[128,256]{1,0:T(8,128)} %constant.16.clone.centre_ref) | copy-start | bytes 393220
  49.6 16.8 %copy-start.5 = (f32[2,24,256]{2,1,0:T(8,128)S(1)}, f32[2,24,256]{2,1,0:T(8,128)}, u32[]{:S(2)}) copy-start(f32[2,24,256]{2,1,0:T(8,128)} %constant.17.clone.sides_ref) | copy-start | bytes 147460
  49.6 16.8 %copy-start.7 = (s32[1,1,2]{2,1,0:T(1,128)S(1)}, s32[1,1,2]{2,1,0:T(1,128)}, u32[]{:S(2)}) copy-start(s32[1,1,2]{2,1,0:T(1,128)} %param.18) | copy-start | bytes 28
  50.7 16.4 %copy-start.9 = (s32[1,1,12]{2,1,0:T(1,128)S(1)}, s32[1,1,12]{2,1,0:T(1,128)}, u32[]{:S(2)}) copy-start(s32[1,1,12]{2,1,0:T(1,128)} %param.17) | copy-start | bytes 148
  50.7 16.4 %copy-start.10 = (f32[12,128,128]{2,1,0:T(8,128)S(1)}, f32[12,128,128]{2,1,0:T(8,128)}, u32[]{:S(2)}) copy-start(f32[12,128,128]{2,1,0:T(8,128)} %wave_ref.1) | copy-start | bytes 2359300
  50.8 8.9 %collective-permute-start.2 = (f32[4,128,128]{2,1,0:T(8,128)S(1)}, f32[4,128,128]{2,1,0:T(8,128)S(1)}, u32[]{:S(2)}, u32[]{:S(2)}) collective-permute-start(f32[4,128,128]{2,1,0:T(8,128)S(1)} %get-tuple-element.23), channel_id=1, source_target_pairs={{0,64},{64,0},{128,192},{192,128},{256,320},{320,256},{384,448},{4... | collective-permute-start | bytes 786440 | tf_op jit(solution)/shard_map/ppermute | solution.py:347
  55.5 11.6 %collective-permute-start = (f32[16,24,128]{2,1,0:T(8,128)}, f32[16,24,128]{2,1,0:T(8,128)}, u32[]{:S(2)}, u32[]{:S(2)}) collective-permute-start(f32[16,24,128]{2,1,0:T(8,128)} %get-tuple-element.17), channel_id=1, source_target_pairs={{8,16},{16,8},{24,32},{32,24},{40,48},{48,40},{9,17},{17,9},{25,33... | collective-permute-start | bytes 589832 | tf_op jit(solution)/shard_map/ppermute | solution.py:341
  56.9 10.2 %collective-permute-start.1 = (f32[16,24,128]{2,1,0:T(8,128)}, f32[16,24,128]{2,1,0:T(8,128)}, u32[]{:S(2)}, u32[]{:S(2)}) collective-permute-start(f32[16,24,128]{2,1,0:T(8,128)} %get-tuple-element.18), channel_id=1, source_target_pairs={{0,8},{8,0},{16,24},{24,16},{32,40},{40,32},{48,56},{56,48},{1,9},... | collective-permute-start | bytes 589832 | tf_op jit(solution)/shard_map/ppermute | solution.py:342
  60.4 14.8 %all-to-all-start.1 = ((f32[4,128,128]{2,1,0:T(8,128)}), f32[4,128,128]{2,1,0:T(8,128)S(1)}, u32[]{:S(2)}, u32[]{:S(2)}) async-start(f32[4,128,128]{2,1,0:T(8,128)} %pair.1), calls=%async_computation.1 | async-start | bytes 524288 | tf_op jit(solution)/shard_map/all_to_all | solution.py:351
  67.1 1.0 copy-start.12
  68.1 7.1 %copy-start.8 = (f32[1,1,8]{2,1,0:T(1,128)S(1)}, f32[1,1,8]{2,1,0:T(1,128)}, u32[]{:S(2)}) copy-start(f32[1,1,8]{2,1,0:T(1,128)} %param.15) | copy-start | bytes 100
  71.7 24.5 %copy-start.3 = (f32[2,128,128]{2,1,0:T(8,128)S(1)}, f32[2,128,128]{2,1,0:T(8,128)}, u32[]{:S(2)}) copy-start(f32[2,128,128]{2,1,0:T(8,128)} %weight_ref.1) | copy-start | bytes 393220
  71.7 3.5 %collective-permute-start.3 = (f32[128,128]{1,0:T(8,128)S(1)}, f32[128,128]{1,0:T(8,128)S(1)}, u32[]{:S(2)}, u32[]{:S(2)}) collective-permute-start(f32[128,128]{1,0:T(8,128)S(1)} %get-tuple-element.25), channel_id=1, source_target_pairs={{0,64},{64,0},{128,192},{192,128},{256,320},{320,256},{384,448},{4... | collective-permute-start | bytes 196616 | tf_op jit(solution)/shard_map/ppermute | solution.py:347
  96.8 7.4 %collective-permute-start.4 = (f32[5,128,128]{2,1,0:T(8,128)S(1)}, f32[5,128,128]{2,1,0:T(8,128)S(1)}, u32[]{:S(2)}, u32[]{:S(2)}) collective-permute-start(f32[5,128,128]{2,1,0:T(8,128)S(1)} %ratio.1.own_ref), channel_id=1, source_target_pairs={{0,64},{64,0},{128,192},{192,128},{256,320},{320,256},{384,448},{4... | collective-permute-start | bytes 983048 | tf_op jit(solution)/shard_map/ppermute | solution.py:347

commit v8 on v6

--- a/solution.py
+++ b/solution.py
@@ -84,12 +84,20 @@
     return whole[HALO : HALO + FACET], sides
 
 
+def spec_index():
+    return lax.axis_index("spec").astype(jnp.int32)
+
+
+def even_row():
+    return lax.rem(lax.axis_index("frow").astype(jnp.int32), 2) == 0
+
+
 def split(values):
     head = values.astype(jnp.bfloat16)
     return head, (values - head.astype(jnp.float32)).astype(jnp.bfloat16)
 
 
-def pack_kernel(me_ref, rows_ref, out_ref, *, chans, facet_rows, facet_cols, deal):
+def pack_kernel(rows_ref, out_ref, *, chans, facet_rows, facet_cols, deal):
     block = deal * (chans + chans // SLOTS)
     per_chan = deal * facet_rows * facet_cols
     for i in range(facet_rows):
@@ -123,8 +131,16 @@
                 out_ref[pl.ds(place, facet_cols, stride=block), :] = sides[first : first + facet_cols]
 
 
-def prepare_kernel(me_ref, width_ref, rows_ref, centre_ref, sides_ref, v_ref, w_ref, pad):
-    odd = 1 - me_ref[1] % 2
+def prepare_kernel(
+    width_ref, basis_ref, band_ref, rows_ref, centre_ref, sides_ref,
+    v_ref, w_ref, spread_ref, pick_ref, pad,
+):
+    rank, chans = basis_ref.shape
+    for ch in range(chans):
+        pick_ref[ch] = jnp.full((8, LANES), band_ref[ch], jnp.int32)
+        for k in range(rank):
+            spread_ref[k, ch] = jnp.full((8, LANES), basis_ref[k, ch], jnp.float32)
+    odd = even_row().astype(jnp.int32)
     lane = lax.broadcasted_iota(jnp.int32, rows_ref.shape[1:], 1)
     first = jnp.where(odd == 1, FACET + EDGE - width_ref[0], EXT - width_ref[0])
     last = jnp.where(odd == 1, FACET + EDGE, FACET) + width_ref[0]
@@ -148,10 +164,10 @@
         )
 
 
-def unpack_kernel(me_ref, in_ref, facet_ref, side_ref, first_ref, second_ref, *, chans, deal, senders):
+def unpack_kernel(in_ref, facet_ref, side_ref, first_ref, second_ref, *, chans, deal, senders):
     groups = chans // SLOTS
     block = deal * (chans + groups)
-    odd = 1 - me_ref[1] % 2
+    odd = even_row()
     for at in range(chans + groups):
         if at < chans:
             starts = [q * chans + at for q in range(deal)]
@@ -161,8 +177,8 @@
         held, place = (facet_ref, at) if at < chans else (side_ref, at - chans)
         held[place] = rows
         top, bottom = rows[:EDGE], rows[FACET - EDGE :]
-        first_ref[at] = jnp.where(odd == 1, top, bottom)
-        second_ref[at] = jnp.where(odd == 1, bottom, top)
+        first_ref[at] = jnp.where(odd, top, bottom)
+        second_ref[at] = jnp.where(odd, bottom, top)
 
 
 def project_kernel(facet_ref, nuc_ref, basis_ref, combined_ref, out_ref, *, chans, rank):
@@ -180,10 +196,10 @@
 
 
 def wavelet_kernel(
-    me_ref, band_ref, facet_ref, side_ref, first_ref, second_ref, v_ref, w_ref, partial_ref, wave_ref,
+    pick_ref, facet_ref, side_ref, first_ref, second_ref, v_ref, w_ref, partial_ref, wave_ref,
     out_ref, own_ref, other_ref, squares, *, chans,
 ):
-    core = me_ref[0] % 2
+    core = lax.rem(spec_index(), 2)
     chips = own_ref.shape[0]
     share = own_ref.shape[1] - FACET
     for chip in range(chips):
@@ -217,8 +233,10 @@
             coeffs = jnp.concatenate([upper, both[FACET:, LANES:]], axis=0)
             dual = wave_ref[ch] + coeffs
             out_ref[ch] = dual
-            rows = pl.ds(pl.multiple_of(band_ref[ch] * FACET, FACET), FACET)
-            squares[rows, :] = squares[rows, :] + dual * dual
+            square = dual * dual
+            high = jnp.tile(pick_ref[ch], (FACET // 8, 1)) == 1
+            squares[:FACET, :] += jnp.where(high, 0.0, square)
+            squares[FACET:, :] += jnp.where(high, square, 0.0)
     for chip in range(chips):
         first = pl.multiple_of((2 * chip + core) * share, share)
         own_ref[chip, FACET:, :] = squares[pl.ds(first, share), :]
@@ -230,16 +248,18 @@
     out_ref[...] = own_ref[...] + came_ref[...]
 
 
-def weigh_kernel(me_ref, thresh_ref, weight_ref, parts_ref, out_ref):
+def weigh_kernel(thresh_ref, weight_ref, parts_ref, out_ref):
     chips = parts_ref.shape[0]
     total = parts_ref[0]
     for chip in range(1, chips):
         total = total + parts_ref[chip]
     spectrum, squares = total[:FACET], total[FACET:]
-    threshold = thresh_ref[me_ref[0]]
+    me = spec_index()
+    mine = lax.broadcasted_iota(jnp.int32, thresh_ref.shape, 1) == me
+    threshold = jnp.sum(jnp.where(mine, thresh_ref[...], 0.0), keepdims=True)
     singular = jnp.sqrt(jnp.sum(spectrum * spectrum, keepdims=True))
     scaled = spectrum * (1.0 - threshold / jnp.maximum(singular, threshold))
-    weight = weight_ref[me_ref[0]]
+    weight = weight_ref[me]
     ratio = weight / jnp.maximum(jnp.sqrt(squares), weight)
     for chip in range(chips):
         out_ref[chip, :FACET] = scaled
@@ -247,26 +267,28 @@
 
 
 def finish_kernel(
-    me_ref, band_ref, basis_ref, combined_ref, dual_ref, own_ref, other_ref, wave_ref, nuc_ref,
+    spread_ref, pick_ref, combined_ref, dual_ref, own_ref, other_ref, wave_ref, nuc_ref,
     ordered, wave, nuc, sems, *, chans, rank,
 ):
-    core, chips = me_ref[0] % 2, own_ref.shape[0]
+    core, chips = lax.rem(spec_index(), 2), own_ref.shape[0]
     for chip in range(chips):
         ordered[2 * chip + core] = own_ref[chip]
         ordered[2 * chip + 1 - core] = other_ref[chip]
     share = ordered.shape[1] - FACET
     pieces = FACET // share
+    tiles = (share // 8, 8, LANES)
     copies = []
     for part in range(pieces):
         rows = pl.ds(part * share, share)
-        scaled = [ordered[k, rows, :] for k in range(rank)]
+        scaled = [ordered[k, rows, :].reshape(tiles) for k in range(rank)]
+        ratios = [ordered[band * pieces + part, FACET:, :].reshape(tiles) for band in range(2)]
         for ch in range(chans):
-            total = basis_ref[0, ch] * scaled[0]
+            total = spread_ref[0, ch] * scaled[0]
             for k in range(1, rank):
-                total = total + basis_ref[k, ch] * scaled[k]
-            nuc[ch, rows, :] = combined_ref[ch, rows, :] - total
-            ratio = ordered[band_ref[ch] * pieces + part, FACET:, :]
-            wave[ch, rows, :] = dual_ref[ch, rows, :] * ratio
+                total = total + spread_ref[k, ch] * scaled[k]
+            nuc[ch, rows, :] = combined_ref[ch, rows, :] - total.reshape(share, LANES)
+            ratio = jnp.where(jnp.broadcast_to(pick_ref[ch] == 1, tiles), ratios[1], ratios[0])
+            wave[ch, rows, :] = dual_ref[ch, rows, :] * ratio.reshape(share, LANES)
         for place, (held, out) in enumerate(((nuc, nuc_ref), (wave, wave_ref))):
             copy = pltpu.make_async_copy(held.at[:, rows, :], out.at[:, rows, :], sems.at[place, part])
             copy.start()
@@ -305,7 +327,6 @@
     rank = basis.shape[3]
     bands = l21_weights.shape[0]
     plane = ("frow", "fcol")
-    me = jnp.stack([lax.axis_index("spec"), lax.axis_index("frow")]).astype(jnp.int32)
     local_basis = basis.reshape(chans, rank).T
     bands_here = band_of.reshape(chans)
     widths = margin_width.reshape(2)
@@ -314,25 +335,26 @@
     block = deal * (chans + groups)
     (packed,) = call(
         functools.partial(pack_kernel, chans=chans, facet_rows=rows, facet_cols=cols, deal=deal),
-        "pack", [SMEM, VMEM], [f32(senders * block, LANES)],
-        [me, primal_slab.reshape(-1, LANES)],
+        "pack", [VMEM], [f32(senders * block, LANES)],
+        [primal_slab.reshape(-1, LANES)],
     )
     arrived = lax.all_to_all(
         packed.reshape(senders, block, LANES), plane, split_axis=0, concat_axis=0, tiled=True
     )
     centre, sides = column_operators()
-    vertical, across = call(
-        prepare_kernel, "prepare", [SMEM, SMEM, VMEM, VMEM, VMEM],
-        [bf16(3 * FACET // 2, 6 * LANES), bf16(SLOTS, 6 * LANES, 2 * LANES)],
-        [me, widths, jnp.asarray(row_operator()), jnp.asarray(centre), jnp.asarray(sides)],
+    vertical, across, spread, pick = call(
+        prepare_kernel, "prepare", [SMEM] * 3 + [VMEM] * 3,
+        [bf16(3 * FACET // 2, 6 * LANES), bf16(SLOTS, 6 * LANES, 2 * LANES),
+         f32(rank, chans, 8, LANES), jax.ShapeDtypeStruct((chans, 8, LANES), jnp.int32)],
+        [widths, local_basis, bands_here, jnp.asarray(row_operator()), jnp.asarray(centre), jnp.asarray(sides)],
         scratch=[pltpu.VMEM((LANES, 2 * LANES), jnp.float32)],
     )
     strip = f32(chans + groups, EDGE, LANES)
     facet, side, first, second = call(
         functools.partial(unpack_kernel, chans=chans, deal=deal, senders=senders),
-        "unpack", [SMEM, VMEM],
+        "unpack", [VMEM],
         [f32(chans, FACET, LANES), f32(groups, FACET, LANES), strip, strip],
-        [me, arrived.reshape(-1, LANES)],
+        [arrived.reshape(-1, LANES)],
     )
     inward = [(i, i - 1 if i % 2 == 0 else i + 1) for i in range(1, rows - 1)]
     first = lax.ppermute(first, "frow", inward)
@@ -349,9 +371,9 @@
     chunks = f32(chips, FACET + share, LANES)
     dual_sum, own, other = call(
         functools.partial(wavelet_kernel, chans=chans),
-        "wavelet", [SMEM, SMEM] + [VMEM] * 8,
+        "wavelet", [VMEM] * 9,
         [f32(chans, FACET, LANES), chunks, chunks],
-        [me, bands_here, facet, side, first, second, vertical, across, partial, wave_dual],
+        [pick, facet, side, first, second, vertical, across, partial, wave_dual],
         scratch=[
             pltpu.VMEM((bands * FACET, LANES), jnp.float32),
         ],
@@ -369,15 +391,15 @@
 
     (sums,) = call(pair_kernel, "pair", [VMEM, VMEM], [chunks], [own, swap(other)])
     (weighed,) = call(
-        weigh_kernel, "weigh", [SMEM, SMEM, VMEM, VMEM], [chunks],
-        [me, nuc_thresh.reshape(rank), l21_weights.reshape(spec, share, LANES), across_chips(sums)],
+        weigh_kernel, "weigh", [VMEM] * 3, [chunks],
+        [nuc_thresh.reshape(1, rank), l21_weights.reshape(spec, share, LANES), across_chips(sums)],
     )
     own = across_chips(weighed)
     wave_new, nuc_new = call(
         functools.partial(finish_kernel, chans=chans, rank=rank),
-        "finish", [SMEM, SMEM, SMEM] + [VMEM] * 4,
+        "finish", [VMEM] * 6,
         [f32(chans, FACET, LANES), f32(chans, FACET, LANES)],
-        [me, bands_here, local_basis, combined, dual_sum, own, swap(own)],
+        [spread, pick, combined, dual_sum, own, swap(own)],
         scratch=[
             pltpu.VMEM((spec, FACET + share, LANES), jnp.float32),
             pltpu.VMEM((chans, FACET, LANES), jnp.float32),

time: 106 us -> 103 us (0.972)
  Pallas kernels: 10.3 us -> 7.57 us
    pallas_call x8, Pallas kernels: 10.3 us -> 7.57 us  [call(): pl.pallas_call(kernel, name=name, in_specs=ins, out_specs=places or [VMEM...]
where the time goes in v8:
time: 103 us
  blocking collectives  73.1 us (71%)
  starting transfers between devices  16.4 us (16%)
  Pallas kernels  7.57 us (7%)
  waiting for transfers between devices  3.6 us (3%)
  local copies, waits for them, and re-layouts  1.19 us (1%)
    all_to_all x1, blocking collectives, shards(): lax.all_to_all(packed.reshape(senders, block, LANES), plane, split_axis=0...  43.7 us
    all_to_all x2, blocking collectives, across_chips(): lax.all_to_all(values, 'spec', split_axis=0, concat_axis=0, tiled=True, a...  29.4 us
    ppermute x2, starting transfers between devices, swap(): return lax.ppermute(values, 'spec', [(i, i ^ 1) for i in range(spec)])  12.4 us
    pallas_call x8, Pallas kernels, call(): pl.pallas_call(kernel, name=name, in_specs=ins, out_specs=places or [VMEM...  7.57 us
    ppermute x1, starting transfers between devices, shards(): second = lax.ppermute(second, 'frow', [(i, i ^ 1) for i in range(rows)])  3.28 us
    ppermute x2, waiting for transfers between devices, swap(): return lax.ppermute(values, 'spec', [(i, i ^ 1) for i in range(spec)])  2.47 us
  transfers between devices with their start and end apart: 4, of which 3 were waited for; matrix products, arithmetic and copies ran while one was open for 0% of the time, Pallas kernels for 2%

profile of v8, /device:TPU:1, one launch (start us, length us, event | category | flops | bytes accessed | tf_op | source)
XLA Modules:
  0.0 102.7 jit_solution(9191793994006446533)
XLA Ops:
  0.6 1.1 %copy-done = f32[12,16,1,1,1024]{4,3,2,1,0:T(1,128)S(1)} copy-done((f32[12,16,1,1,1024]{4,3,2,1,0:T(1,128)S(1)}, f32[12,16,1,1,1024]{4,3,2,1,0:T(1,128)}, u32[]{:S(2)}) %copy-start) | copy-done | bytes 786456
  1.8 0.8 pack.1
  2.6 0.0 copy-start.2
  2.6 0.0 copy-start.4
  2.6 0.0 copy-start.5
  2.6 0.0 copy-start.6
  2.7 0.0 copy-start.7
  2.7 43.7 %all_to_all.15 = f32[64,32,128]{2,1,0:T(8,128)S(1)} all-to-all(f32[64,32,128]{2,1,0:T(8,128)S(1)} %bitcast.10), channel_id=1, replica_groups=mesh['spec'=8,'frow'=8,'fcol'=8] {'frow','fcol'}, dimensions={0} | all-to-all | bytes 2097152 | tf_op jit(solution)/shard_map/all_to_all | solution.py:341
  46.4 0.7 unpack.1
  47.1 0.8 collective-permute-start
  47.9 3.3 %collective-permute-start.1 = (f32[16,24,128]{2,1,0:T(8,128)S(1)}, f32[16,24,128]{2,1,0:T(8,128)S(1)}, u32[]{:S(2)}, u32[]{:S(2)}) collective-permute-start(f32[16,24,128]{2,1,0:T(8,128)S(1)} %get-tuple-element.21), channel_id=1, source_target_pairs={{0,8},{8,0},{16,24},{24,16},{32,40},{40,32},{48,56},{56,48},{1,9},... | collective-permute-start | bytes 589832 | tf_op jit(solution)/shard_map/ppermute | solution.py:361
  51.2 0.8 prepare.1
  52.0 1.1 %project.1 = (f32[12,128,128]{2,1,0:T(8,128)S(1)}, f32[8,128,128]{2,1,0:T(8,128)S(1)}) custom-call(f32[12,128,128]{2,1,0:T(8,128)S(1)} %get-tuple-element.17.facet_ref, f32[12,128,128]{2,1,0:T(8,128)S(1)} %copy-done.1, f32[8,12]{1,0:T(8,128)S(1)} %bitcast.15), custom_call_target="tpu_custom_call" | custom-call | flops 3145728 | bytes 2883968 | tf_op jit(solution)/shard_map/project/pallas_call | solution.py:302
  53.2 1.1 %collective-permute-done.1.second_ref = f32[16,24,128]{2,1,0:T(8,128)S(1)} collective-permute-done((f32[16,24,128]{2,1,0:T(8,128)S(1)}, f32[16,24,128]{2,1,0:T(8,128)S(1)}, u32[]{:S(2)}, u32[]{:S(2)}) %collective-permute-start.1) | collective-permute-done | bytes 196640 | tf_op jit(solution)/shard_map/ppermute | solution.py:361
  54.3 2.6 %wavelet.1 = (f32[12,128,128]{2,1,0:T(8,128)S(1)}, f32[4,160,128]{2,1,0:T(8,128)S(1)}, f32[4,160,128]{2,1,0:T(8,128)S(1)}) custom-call(s32[12,8,128]{2,1,0:T(8,128)S(1)} %get-tuple-element.16.pick_ref, f32[12,128,128]{2,1,0:T(8,128)S(1)} %get-tuple-element.17.facet_ref, f32[4,128,128]{2,1,0:T(8,128)S(1)} %get-tuple-element.19.side_ref, ...), custom_call_target="tpu_custom_call" | custom-call | flops 2123366400 | bytes 7192576 | tf_op jit(solution)/shard_map/wavelet/pallas_call | solution.py:302
  56.9 0.0 copy-start.3
  56.9 5.9 %collective-permute-start.2 = (f32[4,160,128]{2,1,0:T(8,128)S(1)}, f32[4,160,128]{2,1,0:T(8,128)S(1)}, u32[]{:S(2)}, u32[]{:S(2)}) collective-permute-start(f32[4,160,128]{2,1,0:T(8,128)S(1)} %get-tuple-element.27), channel_id=1, source_target_pairs={{0,64},{64,0},{128,192},{192,128},{256,320},{320,256},{384,448},{4... | collective-permute-start | bytes 983048 | tf_op jit(solution)/shard_map/ppermute | solution.py:384
  62.8 1.2 %collective-permute-done.2.came_ref = f32[4,160,128]{2,1,0:T(8,128)S(1)} collective-permute-done((f32[4,160,128]{2,1,0:T(8,128)S(1)}, f32[4,160,128]{2,1,0:T(8,128)S(1)}, u32[]{:S(2)}, u32[]{:S(2)}) %collective-permute-start.2) | collective-permute-done | bytes 327712 | tf_op jit(solution)/shard_map/ppermute | solution.py:384
  64.1 15.4 %all_to_all.16.parts_ref = f32[4,160,128]{2,1,0:T(8,128)S(1)} all-to-all(f32[4,160,128]{2,1,0:T(8,128)S(1)} %pair.1), channel_id=1, replica_groups={{0,128,256,384},{64,192,320,448},{1,129,257,385},{65,193,321,449},{2,13..., dimensions={0} | all-to-all | bytes 655360 | tf_op jit(solution)/shard_map/all_to_all | solution.py:388
  79.5 0.2 weigh.1
  79.7 14.0 %all_to_all.17.own_ref = f32[4,160,128]{2,1,0:T(8,128)S(1)} all-to-all(f32[4,160,128]{2,1,0:T(8,128)S(1)} %weigh.1), channel_id=1, replica_groups={{0,128,256,384},{64,192,320,448},{1,129,257,385},{65,193,321,449},{2,13..., dimensions={0} | all-to-all | bytes 655360 | tf_op jit(solution)/shard_map/all_to_all | solution.py:388
  93.6 6.5 %collective-permute-start.3 = (f32[4,160,128]{2,1,0:T(8,128)S(1)}, f32[4,160,128]{2,1,0:T(8,128)S(1)}, u32[]{:S(2)}, u32[]{:S(2)}) collective-permute-start(f32[4,160,128]{2,1,0:T(8,128)S(1)} %all_to_all.17.own_ref), channel_id=1, source_target_pairs={{0,64},{64,0},{128,192},{192,128},{256,320},{320,256},{384,448},{4... | collective-permute-start | bytes 983048 | tf_op jit(solution)/shard_map/ppermute | solution.py:384
  100.1 1.2 %collective-permute-done.3.other_ref = f32[4,160,128]{2,1,0:T(8,128)S(1)} collective-permute-done((f32[4,160,128]{2,1,0:T(8,128)S(1)}, f32[4,160,128]{2,1,0:T(8,128)S(1)}, u32[]{:S(2)}, u32[]{:S(2)}) %collective-permute-start.3) | collective-permute-done | bytes 327712 | tf_op jit(solution)/shard_map/ppermute | solution.py:384
  101.3 1.4 %finish.1 = (f32[12,128,128]{2,1,0:T(8,128)}, f32[12,128,128]{2,1,0:T(8,128)}) custom-call(f32[8,12,8,128]{3,2,1,0:T(8,128)S(1)} %get-tuple-element.15.spread_ref, s32[12,8,128]{2,1,0:T(8,128)S(1)} %get-tuple-element.16.pick_ref, f32[12,128,128]{2,1,0:T(8,128)S(1)} %get-tuple-element.18.combined_ref, f32[12,128,128]{2,1,0:T(8,128)S(1)} %get-tuple-element.25.dual_ref, ...), custom_call_target="tpu_custom_call" | custom-call | flops 3145728 | bytes 4243456 | tf_op jit(solution)/shard_map/finish/pallas_call | solution.py:302
  (17 shorter events, 0.1 us)
Async XLA Ops:
  0.6 1.1 %copy-start = (f32[12,16,1,1,1024]{4,3,2,1,0:T(1,128)S(1)}, f32[12,16,1,1,1024]{4,3,2,1,0:T(1,128)}, u32[]{:S(2)}) copy-start(f32[12,16,1,1,1024]{4,3,2,1,0:T(1,128)} %param.11) | copy-start | bytes 2359300
  2.6 48.6 %copy-start.2 = (f32[2,192,256]{2,1,0:T(8,128)S(1)}, f32[2,192,256]{2,1,0:T(8,128)}, u32[]{:S(2)}) copy-start(f32[2,192,256]{2,1,0:T(8,128)} %constant.6.clone.rows_ref) | copy-start | bytes 1179652
  2.6 48.5 %copy-start.4 = (f32[128,256]{1,0:T(8,128)S(1)}, f32[128,256]{1,0:T(8,128)}, u32[]{:S(2)}) copy-start(f32[128,256]{1,0:T(8,128)} %constant.7.clone.centre_ref) | copy-start | bytes 393220
  2.6 48.5 %copy-start.5 = (f32[2,24,256]{2,1,0:T(8,128)S(1)}, f32[2,24,256]{2,1,0:T(8,128)}, u32[]{:S(2)}) copy-start(f32[2,24,256]{2,1,0:T(8,128)} %constant.8.clone.sides_ref) | copy-start | bytes 147460
  2.6 48.5 %copy-start.6 = (f32[1,1,12,8]{2,3,1,0:T(8,128)S(1)}, f32[1,1,12,8]{2,3,1,0:T(8,128)}, u32[]{:S(2)}) copy-start(f32[1,1,12,8]{2,3,1,0:T(8,128)} %param.16) | copy-start | bytes 1156
  2.7 48.5 %copy-start.7 = (s32[1,1,2]{2,1,0:T(1,128)S(1)}, s32[1,1,2]{2,1,0:T(1,128)}, u32[]{:S(2)}) copy-start(s32[1,1,2]{2,1,0:T(1,128)} %param.18) | copy-start | bytes 28
  2.7 48.5 %copy-start.8 = (s32[1,1,12]{2,1,0:T(1,128)S(1)}, s32[1,1,12]{2,1,0:T(1,128)}, u32[]{:S(2)}) copy-start(s32[1,1,12]{2,1,0:T(1,128)} %param.17) | copy-start | bytes 148
  46.4 5.6 %copy-start.1 = (f32[12,128,128]{2,1,0:T(8,128)S(1)}, f32[12,128,128]{2,1,0:T(8,128)}, u32[]{:S(2)}) copy-start(f32[12,128,128]{2,1,0:T(8,128)} %nuc_ref.1) | copy-start | bytes 2359300
  47.0 7.2 %copy-start.10 = (f32[12,128,128]{2,1,0:T(8,128)S(1)}, f32[12,128,128]{2,1,0:T(8,128)}, u32[]{:S(2)}) copy-start(f32[12,128,128]{2,1,0:T(8,128)} %wave_ref.1) | copy-start | bytes 2359300
  47.1 6.1 %collective-permute-start = (f32[16,24,128]{2,1,0:T(8,128)S(1)}, f32[16,24,128]{2,1,0:T(8,128)S(1)}, u32[]{:S(2)}, u32[]{:S(2)}) collective-permute-start(f32[16,24,128]{2,1,0:T(8,128)S(1)} %get-tuple-element.20), channel_id=1, source_target_pairs={{8,16},{16,8},{24,32},{32,24},{40,48},{48,40},{9,17},{17,9},{25,33... | collective-permute-start | bytes 589832 | tf_op jit(solution)/shard_map/ppermute | solution.py:360
  47.9 6.4 %collective-permute-start.1 = (f32[16,24,128]{2,1,0:T(8,128)S(1)}, f32[16,24,128]{2,1,0:T(8,128)S(1)}, u32[]{:S(2)}, u32[]{:S(2)}) collective-permute-start(f32[16,24,128]{2,1,0:T(8,128)S(1)} %get-tuple-element.21), channel_id=1, source_target_pairs={{0,8},{8,0},{16,24},{24,16},{32,40},{40,32},{48,56},{56,48},{1,9},... | collective-permute-start | bytes 589832 | tf_op jit(solution)/shard_map/ppermute | solution.py:361
  56.9 22.6 %copy-start.3 = (f32[2,128,128]{2,1,0:T(8,128)S(1)}, f32[2,128,128]{2,1,0:T(8,128)}, u32[]{:S(2)}) copy-start(f32[2,128,128]{2,1,0:T(8,128)} %param.14) | copy-start | bytes 393220
  56.9 22.6 %copy-start.9 = (f32[1,1,8]{2,1,0:T(1,128)S(1)}, f32[1,1,8]{2,1,0:T(1,128)}, u32[]{:S(2)}) copy-start(f32[1,1,8]{2,1,0:T(1,128)} %param.15) | copy-start | bytes 100
  56.9 7.1 %collective-permute-start.2 = (f32[4,160,128]{2,1,0:T(8,128)S(1)}, f32[4,160,128]{2,1,0:T(8,128)S(1)}, u32[]{:S(2)}, u32[]{:S(2)}) collective-permute-start(f32[4,160,128]{2,1,0:T(8,128)S(1)} %get-tuple-element.27), channel_id=1, source_target_pairs={{0,64},{64,0},{128,192},{192,128},{256,320},{320,256},{384,448},{4... | collective-permute-start | bytes 983048 | tf_op jit(solution)/shard_map/ppermute | solution.py:384
  93.6 7.7 %collective-permute-start.3 = (f32[4,160,128]{2,1,0:T(8,128)S(1)}, f32[4,160,128]{2,1,0:T(8,128)S(1)}, u32[]{:S(2)}, u32[]{:S(2)}) collective-permute-start(f32[4,160,128]{2,1,0:T(8,128)S(1)} %all_to_all.17.own_ref), channel_id=1, source_target_pairs={{0,64},{64,0},{128,192},{192,128},{256,320},{320,256},{384,448},{4... | collective-permute-start | bytes 983048 | tf_op jit(solution)/shard_map/ppermute | solution.py:384

commit v9 on v8

--- a/solution.py
+++ b/solution.py
@@ -195,8 +195,27 @@
             out_ref[k, rows, :] = total[k]
 
 
+def along_columns(chans, slot, rows, sides, w_ref):
+    taken = []
+    for group in range(chans // SLOTS):
+        head, tail = split(rows(group * SLOTS + slot))
+        side_head, side_tail = sides[group]
+        taken.append(jnp.concatenate([head, side_head, tail, side_tail, head, side_head], axis=1))
+    return jnp.dot(jnp.concatenate(taken, axis=0), w_ref[slot], preferred_element_type=jnp.float32)
+
+
+def columns_kernel(facet_ref, side_ref, w_ref, out_ref, *, chans):
+    sides = [split(side_ref[group]) for group in range(chans // SLOTS)]
+    for slot in range(SLOTS):
+        across = along_columns(chans, slot, lambda ch: facet_ref[ch], sides, w_ref)
+        for group in range(chans // SLOTS):
+            head, tail = split(across[group * FACET : (group + 1) * FACET])
+            out_ref[group * SLOTS + slot, 0] = head
+            out_ref[group * SLOTS + slot, 1] = tail
+
+
 def wavelet_kernel(
-    pick_ref, facet_ref, side_ref, first_ref, second_ref, v_ref, w_ref, partial_ref, wave_ref,
+    pick_ref, columns_ref, first_ref, second_ref, v_ref, w_ref, partial_ref, wave_ref,
     out_ref, own_ref, other_ref, squares, *, chans,
 ):
     core = lax.rem(spec_index(), 2)
@@ -210,24 +229,19 @@
     half = FACET // 2
     lane = lax.broadcasted_iota(jnp.int32, (half, LANES), 1)
     nothing = jnp.zeros((2 * LANES - EXT, 2 * LANES), jnp.bfloat16)
-    sides = [
-        split(jnp.concatenate([side_ref[g], first_ref[chans + g], second_ref[chans + g]], axis=0))
-        for g in range(groups)
-    ]
+    margin = EXT - FACET
+
+    def margins(ch):
+        return jnp.concatenate([first_ref[ch], second_ref[ch]], axis=0)
+
+    sides = [split(margins(chans + group)) for group in range(groups)]
     for slot in range(SLOTS):
-        taken = []
+        across = along_columns(chans, slot, margins, sides, w_ref)
         for group in range(groups):
             ch = group * SLOTS + slot
-            head, tail = split(jnp.concatenate([facet_ref[ch], first_ref[ch], second_ref[ch]], axis=0))
-            side_head, side_tail = sides[group]
-            taken.append(jnp.concatenate([head, side_head, tail, side_tail, head, side_head], axis=1))
-        across = jnp.dot(
-            jnp.concatenate(taken, axis=0), w_ref[slot], preferred_element_type=jnp.float32
-        )
-        for group in range(groups):
-            ch = group * SLOTS + slot
-            head, tail = split(across[group * EXT : (group + 1) * EXT])
-            stacked = jnp.concatenate([head, nothing, head, nothing, tail, nothing], axis=0)
+            head, tail = split(across[group * margin : (group + 1) * margin])
+            head = [columns_ref[ch, 0], head, nothing]
+            stacked = jnp.concatenate(head + head + [columns_ref[ch, 1], tail, nothing], axis=0)
             both = jnp.dot(v_ref[...], stacked, preferred_element_type=jnp.float32)
             upper = jnp.where(lane < half, both[:half, :LANES], both[half:FACET, :LANES])
             coeffs = jnp.concatenate([upper, both[FACET:, LANES:]], axis=0)
@@ -369,11 +383,16 @@
     share = bands * FACET // spec
     chips = spec // 2
     chunks = f32(chips, FACET + share, LANES)
+    (columns,) = call(
+        functools.partial(columns_kernel, chans=chans),
+        "columns", [VMEM] * 3, [bf16(chans, 2, FACET, 2 * LANES)], [facet, side, across],
+        flops=2 * chans * 3 * 128 * 256 * 256,
+    )
     dual_sum, own, other = call(
         functools.partial(wavelet_kernel, chans=chans),
-        "wavelet", [VMEM] * 9,
+        "wavelet", [VMEM] * 8,
         [f32(chans, FACET, LANES), chunks, chunks],
-        [pick, facet, side, first, second, vertical, across, partial, wave_dual],
+        [pick, columns, first, second, vertical, across, partial, wave_dual],
         scratch=[
             pltpu.VMEM((bands * FACET, LANES), jnp.float32),
         ],

time: 103 us -> 102 us (level)
    pallas_call x8 -> x9, Pallas kernels: 7.57 us -> 7.51 us  [call(): pl.pallas_call(kernel, name=name, in_specs=ins, out_specs=places or [VMEM...]
  transfers between devices with their start and end apart: 4 -> 4, of which waited for: 3 -> 3; matrix products, arithmetic and copies ran while one was open for 0% -> 0% of each run, Pallas kernels for 2% -> 3%
where the time goes in v9:
time: 102 us
  blocking collectives  73.1 us (72%)
  starting transfers between devices  16.3 us (16%)
  Pallas kernels  7.51 us (7%)
  waiting for transfers between devices  2.79 us (3%)
  local copies, waits for them, and re-layouts  1.19 us (1%)
    all_to_all x1, blocking collectives, shards(): lax.all_to_all(packed.reshape(senders, block, LANES), plane, split_axis=0...  43.7 us
    all_to_all x2, blocking collectives, across_chips(): lax.all_to_all(values, 'spec', split_axis=0, concat_axis=0, tiled=True, a...  29.4 us
    ppermute x2, starting transfers between devices, swap(): return lax.ppermute(values, 'spec', [(i, i ^ 1) for i in range(spec)])  12.4 us
    pallas_call x9, Pallas kernels, call(): pl.pallas_call(kernel, name=name, in_specs=ins, out_specs=places or [VMEM...  7.51 us
    ppermute x1, starting transfers between devices, shards(): second = lax.ppermute(second, 'frow', [(i, i ^ 1) for i in range(rows)])  3.28 us
    ppermute x2, waiting for transfers between devices, swap(): return lax.ppermute(values, 'spec', [(i, i ^ 1) for i in range(spec)])  2.47 us
  transfers between devices with their start and end apart: 4, of which 3 were waited for; matrix products, arithmetic and copies ran while one was open for 0% of the time, Pallas kernels for 3%

profile of v9, /device:TPU:1, one launch (start us, length us, event | category | flops | bytes accessed | tf_op | source)
XLA Modules:
  0.0 101.7 jit_solution(5321432790204100844)
XLA Ops:
  0.6 1.1 %copy-done = f32[12,16,1,1,1024]{4,3,2,1,0:T(1,128)S(1)} copy-done((f32[12,16,1,1,1024]{4,3,2,1,0:T(1,128)S(1)}, f32[12,16,1,1,1024]{4,3,2,1,0:T(1,128)}, u32[]{:S(2)}) %copy-start) | copy-done | bytes 786456
  1.8 0.8 pack.1
  2.6 0.0 copy-start.2
  2.6 0.0 copy-start.4
  2.6 0.0 copy-start.5
  2.7 0.0 copy-start.8
  2.7 0.0 copy-start.1
  2.7 43.7 %all_to_all.15 = f32[64,32,128]{2,1,0:T(8,128)S(1)} all-to-all(f32[64,32,128]{2,1,0:T(8,128)S(1)} %bitcast.10), channel_id=1, replica_groups=mesh['spec'=8,'frow'=8,'fcol'=8] {'frow','fcol'}, dimensions={0} | all-to-all | bytes 2097152 | tf_op jit(solution)/shard_map/all_to_all | solution.py:355
  46.4 0.7 unpack.1
  47.0 0.7 collective-permute-start
  47.7 3.3 %collective-permute-start.1 = (f32[16,24,128]{2,1,0:T(8,128)S(1)}, f32[16,24,128]{2,1,0:T(8,128)S(1)}, u32[]{:S(2)}, u32[]{:S(2)}) collective-permute-start(f32[16,24,128]{2,1,0:T(8,128)S(1)} %get-tuple-element.22), channel_id=1, source_target_pairs={{0,8},{8,0},{16,24},{24,16},{32,40},{40,32},{48,56},{56,48},{1,9},... | collective-permute-start | bytes 589832 | tf_op jit(solution)/shard_map/ppermute | solution.py:375
  51.1 0.8 prepare.1
  51.9 1.1 %project.1 = (f32[12,128,128]{2,1,0:T(8,128)S(1)}, f32[8,128,128]{2,1,0:T(8,128)S(1)}) custom-call(f32[12,128,128]{2,1,0:T(8,128)S(1)} %get-tuple-element.17.facet_ref, f32[12,128,128]{2,1,0:T(8,128)S(1)} %copy-done.1, f32[8,12]{1,0:T(8,128)S(1)} %bitcast.15), custom_call_target="tpu_custom_call" | custom-call | flops 3145728 | bytes 2883968 | tf_op jit(solution)/shard_map/project/pallas_call | solution.py:316
  53.0 0.8 columns.1.columns_ref
  53.8 0.3 collective-permute-done.1.second_ref
  54.1 1.7 %wavelet.1 = (f32[12,128,128]{2,1,0:T(8,128)S(1)}, f32[4,160,128]{2,1,0:T(8,128)S(1)}, f32[4,160,128]{2,1,0:T(8,128)S(1)}) custom-call(s32[12,8,128]{2,1,0:T(8,128)S(1)} %get-tuple-element.16.pick_ref, bf16[12,2,128,256]{3,2,1,0:T(8,128)(2,1)S(1)} %columns.1.columns_ref, f32[16,24,128]{2,1,0:T(8,128)S(1)} %collective-permute-done.first_ref, ...), custom_call_target="tpu_custom_call" | custom-call | flops 2123366400 | bytes 9289728 | tf_op jit(solution)/shard_map/wavelet/pallas_call | solution.py:316
  55.9 5.9 %collective-permute-start.2 = (f32[4,160,128]{2,1,0:T(8,128)S(1)}, f32[4,160,128]{2,1,0:T(8,128)S(1)}, u32[]{:S(2)}, u32[]{:S(2)}) collective-permute-start(f32[4,160,128]{2,1,0:T(8,128)S(1)} %get-tuple-element.27), channel_id=1, source_target_pairs={{0,64},{64,0},{128,192},{192,128},{256,320},{320,256},{384,448},{4... | collective-permute-start | bytes 983048 | tf_op jit(solution)/shard_map/ppermute | solution.py:403
  61.8 1.2 %collective-permute-done.2.came_ref = f32[4,160,128]{2,1,0:T(8,128)S(1)} collective-permute-done((f32[4,160,128]{2,1,0:T(8,128)S(1)}, f32[4,160,128]{2,1,0:T(8,128)S(1)}, u32[]{:S(2)}, u32[]{:S(2)}) %collective-permute-start.2) | collective-permute-done | bytes 327712 | tf_op jit(solution)/shard_map/ppermute | solution.py:403
  63.1 15.4 %all_to_all.16.parts_ref = f32[4,160,128]{2,1,0:T(8,128)S(1)} all-to-all(f32[4,160,128]{2,1,0:T(8,128)S(1)} %pair.1), channel_id=1, replica_groups={{0,128,256,384},{64,192,320,448},{1,129,257,385},{65,193,321,449},{2,13..., dimensions={0} | all-to-all | bytes 655360 | tf_op jit(solution)/shard_map/all_to_all | solution.py:407
  78.5 0.2 weigh.1
  78.7 14.0 %all_to_all.17.own_ref = f32[4,160,128]{2,1,0:T(8,128)S(1)} all-to-all(f32[4,160,128]{2,1,0:T(8,128)S(1)} %weigh.1), channel_id=1, replica_groups={{0,128,256,384},{64,192,320,448},{1,129,257,385},{65,193,321,449},{2,13..., dimensions={0} | all-to-all | bytes 655360 | tf_op jit(solution)/shard_map/all_to_all | solution.py:407
  92.7 6.5 %collective-permute-start.3 = (f32[4,160,128]{2,1,0:T(8,128)S(1)}, f32[4,160,128]{2,1,0:T(8,128)S(1)}, u32[]{:S(2)}, u32[]{:S(2)}) collective-permute-start(f32[4,160,128]{2,1,0:T(8,128)S(1)} %all_to_all.17.own_ref), channel_id=1, source_target_pairs={{0,64},{64,0},{128,192},{192,128},{256,320},{320,256},{384,448},{4... | collective-permute-start | bytes 983048 | tf_op jit(solution)/shard_map/ppermute | solution.py:403
  99.1 1.2 %collective-permute-done.3.other_ref = f32[4,160,128]{2,1,0:T(8,128)S(1)} collective-permute-done((f32[4,160,128]{2,1,0:T(8,128)S(1)}, f32[4,160,128]{2,1,0:T(8,128)S(1)}, u32[]{:S(2)}, u32[]{:S(2)}) %collective-permute-start.3) | collective-permute-done | bytes 327712 | tf_op jit(solution)/shard_map/ppermute | solution.py:403
  100.4 1.4 %finish.1 = (f32[12,128,128]{2,1,0:T(8,128)}, f32[12,128,128]{2,1,0:T(8,128)}) custom-call(f32[8,12,8,128]{3,2,1,0:T(8,128)S(1)} %get-tuple-element.15.spread_ref, s32[12,8,128]{2,1,0:T(8,128)S(1)} %get-tuple-element.16.pick_ref, f32[12,128,128]{2,1,0:T(8,128)S(1)} %get-tuple-element.18.combined_ref, f32[12,128,128]{2,1,0:T(8,128)S(1)} %get-tuple-element.25.dual_ref, ...), custom_call_target="tpu_custom_call" | custom-call | flops 3145728 | bytes 4243456 | tf_op jit(solution)/shard_map/finish/pallas_call | solution.py:316
  (18 shorter events, 0.1 us)
Async XLA Ops:
  0.6 1.1 %copy-start = (f32[12,16,1,1,1024]{4,3,2,1,0:T(1,128)S(1)}, f32[12,16,1,1,1024]{4,3,2,1,0:T(1,128)}, u32[]{:S(2)}) copy-start(f32[12,16,1,1,1024]{4,3,2,1,0:T(1,128)} %param.11) | copy-start | bytes 2359300
  2.6 48.4 %copy-start.2 = (f32[2,192,256]{2,1,0:T(8,128)S(1)}, f32[2,192,256]{2,1,0:T(8,128)}, u32[]{:S(2)}) copy-start(f32[2,192,256]{2,1,0:T(8,128)} %constant.6.clone.rows_ref) | copy-start | bytes 1179652
  2.6 48.4 %copy-start.4 = (f32[128,256]{1,0:T(8,128)S(1)}, f32[128,256]{1,0:T(8,128)}, u32[]{:S(2)}) copy-start(f32[128,256]{1,0:T(8,128)} %constant.7.clone.centre_ref) | copy-start | bytes 393220
  2.6 48.4 %copy-start.5 = (f32[2,24,256]{2,1,0:T(8,128)S(1)}, f32[2,24,256]{2,1,0:T(8,128)}, u32[]{:S(2)}) copy-start(f32[2,24,256]{2,1,0:T(8,128)} %constant.8.clone.sides_ref) | copy-start | bytes 147460
  2.6 48.4 %copy-start.6 = (f32[1,1,12,8]{2,3,1,0:T(8,128)S(1)}, f32[1,1,12,8]{2,3,1,0:T(8,128)}, u32[]{:S(2)}) copy-start(f32[1,1,12,8]{2,3,1,0:T(8,128)} %param.16) | copy-start | bytes 1156
  2.7 48.4 %copy-start.7 = (s32[1,1,2]{2,1,0:T(1,128)S(1)}, s32[1,1,2]{2,1,0:T(1,128)}, u32[]{:S(2)}) copy-start(s32[1,1,2]{2,1,0:T(1,128)} %param.18) | copy-start | bytes 28
  2.7 48.4 %copy-start.8 = (s32[1,1,12]{2,1,0:T(1,128)S(1)}, s32[1,1,12]{2,1,0:T(1,128)}, u32[]{:S(2)}) copy-start(s32[1,1,12]{2,1,0:T(1,128)} %param.17) | copy-start | bytes 148
  2.7 49.2 %copy-start.1 = (f32[12,128,128]{2,1,0:T(8,128)S(1)}, f32[12,128,128]{2,1,0:T(8,128)}, u32[]{:S(2)}) copy-start(f32[12,128,128]{2,1,0:T(8,128)} %nuc_ref.1) | copy-start | bytes 2359300
  47.0 6.8 %collective-permute-start = (f32[16,24,128]{2,1,0:T(8,128)S(1)}, f32[16,24,128]{2,1,0:T(8,128)S(1)}, u32[]{:S(2)}, u32[]{:S(2)}) collective-permute-start(f32[16,24,128]{2,1,0:T(8,128)S(1)} %get-tuple-element.21), channel_id=1, source_target_pairs={{8,16},{16,8},{24,32},{32,24},{40,48},{48,40},{9,17},{17,9},{25,33... | collective-permute-start | bytes 589832 | tf_op jit(solution)/shard_map/ppermute | solution.py:374
  47.7 6.4 %collective-permute-start.1 = (f32[16,24,128]{2,1,0:T(8,128)S(1)}, f32[16,24,128]{2,1,0:T(8,128)S(1)}, u32[]{:S(2)}, u32[]{:S(2)}) collective-permute-start(f32[16,24,128]{2,1,0:T(8,128)S(1)} %get-tuple-element.22), channel_id=1, source_target_pairs={{0,8},{8,0},{16,24},{24,16},{32,40},{40,32},{48,56},{56,48},{1,9},... | collective-permute-start | bytes 589832 | tf_op jit(solution)/shard_map/ppermute | solution.py:375
  53.0 1.1 %copy-start.10 = (f32[12,128,128]{2,1,0:T(8,128)S(1)}, f32[12,128,128]{2,1,0:T(8,128)}, u32[]{:S(2)}) copy-start(f32[12,128,128]{2,1,0:T(8,128)} %wave_ref.1) | copy-start | bytes 2359300
  55.9 22.6 %copy-start.3 = (f32[2,128,128]{2,1,0:T(8,128)S(1)}, f32[2,128,128]{2,1,0:T(8,128)}, u32[]{:S(2)}) copy-start(f32[2,128,128]{2,1,0:T(8,128)} %param.14) | copy-start | bytes 393220
  55.9 22.6 %copy-start.9 = (f32[1,1,8]{2,1,0:T(1,128)S(1)}, f32[1,1,8]{2,1,0:T(1,128)}, u32[]{:S(2)}) copy-start(f32[1,1,8]{2,1,0:T(1,128)} %param.15) | copy-start | bytes 100
  55.9 7.1 %collective-permute-start.2 = (f32[4,160,128]{2,1,0:T(8,128)S(1)}, f32[4,160,128]{2,1,0:T(8,128)S(1)}, u32[]{:S(2)}, u32[]{:S(2)}) collective-permute-start(f32[4,160,128]{2,1,0:T(8,128)S(1)} %get-tuple-element.27), channel_id=1, source_target_pairs={{0,64},{64,0},{128,192},{192,128},{256,320},{320,256},{384,448},{4... | collective-permute-start | bytes 983048 | tf_op jit(solution)/shard_map/ppermute | solution.py:403
  92.7 7.7 %collective-permute-start.3 = (f32[4,160,128]{2,1,0:T(8,128)S(1)}, f32[4,160,128]{2,1,0:T(8,128)S(1)}, u32[]{:S(2)}, u32[]{:S(2)}) collective-permute-start(f32[4,160,128]{2,1,0:T(8,128)S(1)} %all_to_all.17.own_ref), channel_id=1, source_target_pairs={{0,64},{64,0},{128,192},{192,128},{256,320},{320,256},{384,448},{4... | collective-permute-start | bytes 983048 | tf_op jit(solution)/shard_map/ppermute | solution.py:403

commit v10 on v9

--- a/solution.py
+++ b/solution.py
@@ -104,7 +104,7 @@
         for q in range(deal):
             for j in range(facet_cols):
                 first = (deal * i + q) * facet_cols + j
-                out_ref[pl.ds((i * facet_cols + j) * block + q * chans, chans), :] = rows_ref[
+                out_ref[pl.ds((j * facet_rows + i) * block + q * chans, chans), :] = rows_ref[
                     pl.ds(first, chans, stride=per_chan), :
                 ]
     lane = lax.broadcasted_iota(jnp.int32, (per_chan, LANES), 1)
@@ -127,8 +127,8 @@
         for i in range(facet_rows):
             for q in range(deal):
                 first = (deal * i + q) * facet_cols
-                place = i * facet_cols * block + deal * chans + q * (chans // SLOTS) + group
-                out_ref[pl.ds(place, facet_cols, stride=block), :] = sides[first : first + facet_cols]
+                place = i * block + deal * chans + q * (chans // SLOTS) + group
+                out_ref[pl.ds(place, facet_cols, stride=facet_rows * block), :] = sides[first : first + facet_cols]
 
 
 def prepare_kernel(
@@ -164,7 +164,9 @@
         )
 
 
-def unpack_kernel(in_ref, facet_ref, side_ref, first_ref, second_ref, *, chans, deal, senders):
+def unpack_kernel(
+    in_ref, facet_ref, side_ref, first_ref, second_ref, *, chans, deal, facet_rows, facet_cols
+):
     groups = chans // SLOTS
     block = deal * (chans + groups)
     odd = even_row()
@@ -173,7 +175,12 @@
             starts = [q * chans + at for q in range(deal)]
         else:
             starts = [deal * chans + q * groups + at - chans for q in range(deal)]
-        rows = jnp.concatenate([in_ref[pl.ds(s, senders, stride=block), :] for s in starts], axis=0)
+        rows = [
+            in_ref[pl.ds(r * block + start, facet_cols, stride=facet_rows * block), :]
+            for start in starts
+            for r in range(facet_rows)
+        ]
+        rows = jnp.concatenate(rows, axis=0)
         held, place = (facet_ref, at) if at < chans else (side_ref, at - chans)
         held[place] = rows
         top, bottom = rows[:EDGE], rows[FACET - EDGE :]
@@ -340,7 +347,7 @@
     deal = primal_slab.shape[1] // rows
     rank = basis.shape[3]
     bands = l21_weights.shape[0]
-    plane = ("frow", "fcol")
+    plane = ("fcol", "frow")
     local_basis = basis.reshape(chans, rank).T
     bands_here = band_of.reshape(chans)
     widths = margin_width.reshape(2)
@@ -365,7 +372,7 @@
     )
     strip = f32(chans + groups, EDGE, LANES)
     facet, side, first, second = call(
-        functools.partial(unpack_kernel, chans=chans, deal=deal, senders=senders),
+        functools.partial(unpack_kernel, chans=chans, deal=deal, facet_rows=rows, facet_cols=cols),
         "unpack", [VMEM],
         [f32(chans, FACET, LANES), f32(groups, FACET, LANES), strip, strip],
         [arrived.reshape(-1, LANES)],

time: 102 us -> 102 us (level)
  starting transfers between devices: 16.3 us -> 17.8 us
  blocking collectives: 73.1 us -> 71.7 us
    ppermute x1, starting transfers between devices: 3.28 us -> 4.71 us  [shards(): second = lax.ppermute(second, 'frow', [(i, i ^ 1) for i in range(rows)])]
    all_to_all x1, blocking collectives: 43.7 us -> 42.3 us  [shards(): lax.all_to_all(packed.reshape(senders, block, LANES), plane, split_axis=0...]
where the time goes in v10:
time: 102 us
  blocking collectives  71.7 us (70%)
  starting transfers between devices  17.8 us (17%)
  Pallas kernels  7.5 us (7%)
  waiting for transfers between devices  2.71 us (3%)
  local copies, waits for them, and re-layouts  1.27 us (1%)
    all_to_all x1, blocking collectives, shards(): lax.all_to_all(packed.reshape(senders, block, LANES), plane, split_axis=0...  42.3 us
    all_to_all x2, blocking collectives, across_chips(): lax.all_to_all(values, 'spec', split_axis=0, concat_axis=0, tiled=True, a...  29.4 us
    ppermute x2, starting transfers between devices, swap(): return lax.ppermute(values, 'spec', [(i, i ^ 1) for i in range(spec)])  12.4 us
    pallas_call x9, Pallas kernels, call(): pl.pallas_call(kernel, name=name, in_specs=ins, out_specs=places or [VMEM...  7.5 us
    ppermute x1, starting transfers between devices, shards(): second = lax.ppermute(second, 'frow', [(i, i ^ 1) for i in range(rows)])  4.71 us
    ppermute x2, waiting for transfers between devices, swap(): return lax.ppermute(values, 'spec', [(i, i ^ 1) for i in range(spec)])  2.47 us
  transfers between devices with their start and end apart: 4, of which 3 were waited for; matrix products, arithmetic and copies ran while one was open for 0% of the time, Pallas kernels for 3%

profile of v10, /device:TPU:1, one launch (start us, length us, event | category | flops | bytes accessed | tf_op | source)
XLA Modules:
  0.0 101.8 jit_solution(3199821846469833814)
XLA Ops:
  0.6 1.1 %copy-done = f32[12,16,1,1,1024]{4,3,2,1,0:T(1,128)S(1)} copy-done((f32[12,16,1,1,1024]{4,3,2,1,0:T(1,128)S(1)}, f32[12,16,1,1,1024]{4,3,2,1,0:T(1,128)}, u32[]{:S(2)}) %copy-start) | copy-done | bytes 786456
  1.8 0.8 pack.1
  2.6 0.0 copy-start.2
  2.6 0.0 copy-start.4
  2.6 0.0 copy-start.5
  2.7 0.0 copy-start.7
  2.7 42.3 %all_to_all.15 = f32[64,32,128]{2,1,0:T(8,128)S(1)} all-to-all(f32[64,32,128]{2,1,0:T(8,128)S(1)} %bitcast.10), channel_id=1, replica_groups=mesh['spec'=8,'frow'=8,'fcol'=8] {'fcol','frow'}, dimensions={0} | all-to-all | bytes 2097152 | tf_op jit(solution)/shard_map/all_to_all | solution.py:362
  45.0 0.7 unpack.1
  45.6 0.7 collective-permute-start
  46.3 4.7 %collective-permute-start.1 = (f32[16,24,128]{2,1,0:T(8,128)S(1)}, f32[16,24,128]{2,1,0:T(8,128)S(1)}, u32[]{:S(2)}, u32[]{:S(2)}) collective-permute-start(f32[16,24,128]{2,1,0:T(8,128)S(1)} %get-tuple-element.22), channel_id=1, source_target_pairs={{0,8},{8,0},{16,24},{24,16},{32,40},{40,32},{48,56},{56,48},{1,9},... | collective-permute-start | bytes 589832 | tf_op jit(solution)/shard_map/ppermute | solution.py:382
  51.1 0.8 prepare.1
  51.9 1.1 %project.1 = (f32[12,128,128]{2,1,0:T(8,128)S(1)}, f32[8,128,128]{2,1,0:T(8,128)S(1)}) custom-call(f32[12,128,128]{2,1,0:T(8,128)S(1)} %get-tuple-element.17.facet_ref, f32[12,128,128]{2,1,0:T(8,128)S(1)} %copy-done.1, f32[8,12]{1,0:T(8,128)S(1)} %bitcast.15), custom_call_target="tpu_custom_call" | custom-call | flops 3145728 | bytes 2883968 | tf_op jit(solution)/shard_map/project/pallas_call | solution.py:323
  53.0 0.8 columns.1.columns_ref
  53.8 0.2 collective-permute-done.1.second_ref
  54.1 0.1 copy-done.10
  54.2 1.7 %wavelet.1 = (f32[12,128,128]{2,1,0:T(8,128)S(1)}, f32[4,160,128]{2,1,0:T(8,128)S(1)}, f32[4,160,128]{2,1,0:T(8,128)S(1)}) custom-call(s32[12,8,128]{2,1,0:T(8,128)S(1)} %get-tuple-element.16.pick_ref, bf16[12,2,128,256]{3,2,1,0:T(8,128)(2,1)S(1)} %columns.1.columns_ref, f32[16,24,128]{2,1,0:T(8,128)S(1)} %collective-permute-done.first_ref, ...), custom_call_target="tpu_custom_call" | custom-call | flops 2123366400 | bytes 9289728 | tf_op jit(solution)/shard_map/wavelet/pallas_call | solution.py:323
  55.9 6.0 %collective-permute-start.2 = (f32[4,160,128]{2,1,0:T(8,128)S(1)}, f32[4,160,128]{2,1,0:T(8,128)S(1)}, u32[]{:S(2)}, u32[]{:S(2)}) collective-permute-start(f32[4,160,128]{2,1,0:T(8,128)S(1)} %get-tuple-element.27), channel_id=1, source_target_pairs={{0,64},{64,0},{128,192},{192,128},{256,320},{320,256},{384,448},{4... | collective-permute-start | bytes 983048 | tf_op jit(solution)/shard_map/ppermute | solution.py:410
  61.9 1.2 %collective-permute-done.2.came_ref = f32[4,160,128]{2,1,0:T(8,128)S(1)} collective-permute-done((f32[4,160,128]{2,1,0:T(8,128)S(1)}, f32[4,160,128]{2,1,0:T(8,128)S(1)}, u32[]{:S(2)}, u32[]{:S(2)}) %collective-permute-start.2) | collective-permute-done | bytes 327712 | tf_op jit(solution)/shard_map/ppermute | solution.py:410
  63.2 15.4 %all_to_all.16.parts_ref = f32[4,160,128]{2,1,0:T(8,128)S(1)} all-to-all(f32[4,160,128]{2,1,0:T(8,128)S(1)} %pair.1), channel_id=1, replica_groups={{0,128,256,384},{64,192,320,448},{1,129,257,385},{65,193,321,449},{2,13..., dimensions={0} | all-to-all | bytes 655360 | tf_op jit(solution)/shard_map/all_to_all | solution.py:414
  78.6 0.2 weigh.1
  78.8 14.0 %all_to_all.17.own_ref = f32[4,160,128]{2,1,0:T(8,128)S(1)} all-to-all(f32[4,160,128]{2,1,0:T(8,128)S(1)} %weigh.1), channel_id=1, replica_groups={{0,128,256,384},{64,192,320,448},{1,129,257,385},{65,193,321,449},{2,13..., dimensions={0} | all-to-all | bytes 655360 | tf_op jit(solution)/shard_map/all_to_all | solution.py:414
  92.8 6.5 %collective-permute-start.3 = (f32[4,160,128]{2,1,0:T(8,128)S(1)}, f32[4,160,128]{2,1,0:T(8,128)S(1)}, u32[]{:S(2)}, u32[]{:S(2)}) collective-permute-start(f32[4,160,128]{2,1,0:T(8,128)S(1)} %all_to_all.17.own_ref), channel_id=1, source_target_pairs={{0,64},{64,0},{128,192},{192,128},{256,320},{320,256},{384,448},{4... | collective-permute-start | bytes 983048 | tf_op jit(solution)/shard_map/ppermute | solution.py:410
  99.2 1.2 %collective-permute-done.3.other_ref = f32[4,160,128]{2,1,0:T(8,128)S(1)} collective-permute-done((f32[4,160,128]{2,1,0:T(8,128)S(1)}, f32[4,160,128]{2,1,0:T(8,128)S(1)}, u32[]{:S(2)}, u32[]{:S(2)}) %collective-permute-start.3) | collective-permute-done | bytes 327712 | tf_op jit(solution)/shard_map/ppermute | solution.py:410
  100.5 1.4 %finish.1 = (f32[12,128,128]{2,1,0:T(8,128)}, f32[12,128,128]{2,1,0:T(8,128)}) custom-call(f32[8,12,8,128]{3,2,1,0:T(8,128)S(1)} %get-tuple-element.15.spread_ref, s32[12,8,128]{2,1,0:T(8,128)S(1)} %get-tuple-element.16.pick_ref, f32[12,128,128]{2,1,0:T(8,128)S(1)} %get-tuple-element.18.combined_ref, f32[12,128,128]{2,1,0:T(8,128)S(1)} %get-tuple-element.25.dual_ref, ...), custom_call_target="tpu_custom_call" | custom-call | flops 3145728 | bytes 4243456 | tf_op jit(solution)/shard_map/finish/pallas_call | solution.py:323
  (18 shorter events, 0.1 us)
Async XLA Ops:
  0.6 1.1 %copy-start = (f32[12,16,1,1,1024]{4,3,2,1,0:T(1,128)S(1)}, f32[12,16,1,1,1024]{4,3,2,1,0:T(1,128)}, u32[]{:S(2)}) copy-start(f32[12,16,1,1,1024]{4,3,2,1,0:T(1,128)} %param.11) | copy-start | bytes 2359300
  2.6 48.4 %copy-start.2 = (f32[2,192,256]{2,1,0:T(8,128)S(1)}, f32[2,192,256]{2,1,0:T(8,128)}, u32[]{:S(2)}) copy-start(f32[2,192,256]{2,1,0:T(8,128)} %constant.6.clone.rows_ref) | copy-start | bytes 1179652
  2.6 48.4 %copy-start.4 = (f32[128,256]{1,0:T(8,128)S(1)}, f32[128,256]{1,0:T(8,128)}, u32[]{:S(2)}) copy-start(f32[128,256]{1,0:T(8,128)} %constant.7.clone.centre_ref) | copy-start | bytes 393220
  2.6 48.4 %copy-start.5 = (f32[2,24,256]{2,1,0:T(8,128)S(1)}, f32[2,24,256]{2,1,0:T(8,128)}, u32[]{:S(2)}) copy-start(f32[2,24,256]{2,1,0:T(8,128)} %constant.8.clone.sides_ref) | copy-start | bytes 147460
  2.6 48.4 %copy-start.6 = (f32[1,1,12,8]{2,3,1,0:T(8,128)S(1)}, f32[1,1,12,8]{2,3,1,0:T(8,128)}, u32[]{:S(2)}) copy-start(f32[1,1,12,8]{2,3,1,0:T(8,128)} %param.16) | copy-start | bytes 1156
  2.7 48.4 %copy-start.7 = (s32[1,1,2]{2,1,0:T(1,128)S(1)}, s32[1,1,2]{2,1,0:T(1,128)}, u32[]{:S(2)}) copy-start(s32[1,1,2]{2,1,0:T(1,128)} %param.18) | copy-start | bytes 28
  2.7 48.4 %copy-start.8 = (s32[1,1,12]{2,1,0:T(1,128)S(1)}, s32[1,1,12]{2,1,0:T(1,128)}, u32[]{:S(2)}) copy-start(s32[1,1,12]{2,1,0:T(1,128)} %param.17) | copy-start | bytes 148
  2.7 49.2 %copy-start.1 = (f32[12,128,128]{2,1,0:T(8,128)S(1)}, f32[12,128,128]{2,1,0:T(8,128)}, u32[]{:S(2)}) copy-start(f32[12,128,128]{2,1,0:T(8,128)} %nuc_ref.1) | copy-start | bytes 2359300
  45.6 8.2 %collective-permute-start = (f32[16,24,128]{2,1,0:T(8,128)S(1)}, f32[16,24,128]{2,1,0:T(8,128)S(1)}, u32[]{:S(2)}, u32[]{:S(2)}) collective-permute-start(f32[16,24,128]{2,1,0:T(8,128)S(1)} %get-tuple-element.21), channel_id=1, source_target_pairs={{8,16},{16,8},{24,32},{32,24},{40,48},{48,40},{9,17},{17,9},{25,33... | collective-permute-start | bytes 589832 | tf_op jit(solution)/shard_map/ppermute | solution.py:381
  46.3 7.8 %collective-permute-start.1 = (f32[16,24,128]{2,1,0:T(8,128)S(1)}, f32[16,24,128]{2,1,0:T(8,128)S(1)}, u32[]{:S(2)}, u32[]{:S(2)}) collective-permute-start(f32[16,24,128]{2,1,0:T(8,128)S(1)} %get-tuple-element.22), channel_id=1, source_target_pairs={{0,8},{8,0},{16,24},{24,16},{32,40},{40,32},{48,56},{56,48},{1,9},... | collective-permute-start | bytes 589832 | tf_op jit(solution)/shard_map/ppermute | solution.py:382
  53.0 1.1 %copy-start.10 = (f32[12,128,128]{2,1,0:T(8,128)S(1)}, f32[12,128,128]{2,1,0:T(8,128)}, u32[]{:S(2)}) copy-start(f32[12,128,128]{2,1,0:T(8,128)} %wave_ref.1) | copy-start | bytes 2359300
  55.9 22.7 %copy-start.3 = (f32[2,128,128]{2,1,0:T(8,128)S(1)}, f32[2,128,128]{2,1,0:T(8,128)}, u32[]{:S(2)}) copy-start(f32[2,128,128]{2,1,0:T(8,128)} %param.14) | copy-start | bytes 393220
  55.9 22.7 %copy-start.9 = (f32[1,1,8]{2,1,0:T(1,128)S(1)}, f32[1,1,8]{2,1,0:T(1,128)}, u32[]{:S(2)}) copy-start(f32[1,1,8]{2,1,0:T(1,128)} %param.15) | copy-start | bytes 100
  55.9 7.2 %collective-permute-start.2 = (f32[4,160,128]{2,1,0:T(8,128)S(1)}, f32[4,160,128]{2,1,0:T(8,128)S(1)}, u32[]{:S(2)}, u32[]{:S(2)}) collective-permute-start(f32[4,160,128]{2,1,0:T(8,128)S(1)} %get-tuple-element.27), channel_id=1, source_target_pairs={{0,64},{64,0},{128,192},{192,128},{256,320},{320,256},{384,448},{4... | collective-permute-start | bytes 983048 | tf_op jit(solution)/shard_map/ppermute | solution.py:410
  92.8 7.7 %collective-permute-start.3 = (f32[4,160,128]{2,1,0:T(8,128)S(1)}, f32[4,160,128]{2,1,0:T(8,128)S(1)}, u32[]{:S(2)}, u32[]{:S(2)}) collective-permute-start(f32[4,160,128]{2,1,0:T(8,128)S(1)} %all_to_all.17.own_ref), channel_id=1, source_target_pairs={{0,64},{64,0},{128,192},{192,128},{256,320},{320,256},{384,448},{4... | collective-permute-start | bytes 983048 | tf_op jit(solution)/shard_map/ppermute | solution.py:410
